TPU v7x, 32 devices: a whole 2x2x4 slice. The times are simulated.
32 devices in a mesh: groups: 2 (over x), seq: 16 (over z, y, core).
Axes of the slice: x: 2, y: 2, z: 4, core: 2. Of those that a mesh axis runs over, the one named last changes fastest.
Arguments:
- queries: bfloat16 [4096, 2560], P(('groups', 'seq')), parts along dimension 0, may hold values from -12 to 12
- key_vectors: bfloat16 [4096, 2560], P(('groups', 'seq')), parts along dimension 0, may hold values from -6 to 6
- value_vectors: bfloat16 [4096, 2560], P(('groups', 'seq')), parts along dimension 0, may hold values from -6 to 6
- step_sizes: float32 [4096, 8], P(('groups', 'seq')), parts along dimension 0, may hold values from 0.02 to 0.3
- fast_weights: float32 [320, 7680], P('seq'), may hold values from -20 to 20
- fast_gain: float32 [2560], replicated, may hold values from 0.25 to 1.75
- window_gain: float32 [2560], replicated, may hold values from 0.25 to 1.75
Outputs:
- layer_out: bfloat16 [4096, 2560], P(('groups', 'seq')), parts along dimension 0
- new_weights: float32 [640, 7680], P(('groups', 'seq')), parts along dimension 0
- momentum: float32 [640, 7680], P(('groups', 'seq')), parts along dimension 0
There are 2 independent parts, one for each index of `groups`. A program takes and returns all parts, laid end to end along the dimension named above; an argument that names none is the same for every part. Nothing has to cross between parts.
All inputs are finite; a program needn't handle non-finite values.
Results may differ from a plain program's by a relative error of at most 0.0066.
Values may be sent and summed in bfloat16 or wider, within the bound.
No kernel may reach another device: no remote copies, remote signals or barrier semaphores. Data moves between devices by JAX's collectives and lax.ppermute only.
A program may use at most 128 MiB of HBM per device.

v0:
```python
import math

import jax
import jax.numpy as jnp
from jax import lax
from jax.sharding import PartitionSpec as P

WINDOW = 1024


def from_behind(value, axis, steps):
    count = lax.axis_size(axis)
    first, last = (max(0, -steps), min(count, count - steps))
    return lax.ppermute(value, axis, [(source, source + steps) for source in range(first, last)])


def normalize(field, gain_row):
    mean_sq = jnp.mean(field * field, axis=-1, keepdims=True)
    return field * lax.rsqrt(mean_sq + 1e-05) * gain_row


def silu_slope(gate):
    sigma = jax.nn.sigmoid(gate)
    return sigma * (1.0 + gate * (1.0 - sigma))


def shards(queries, key_vectors, value_vectors, step_sizes, fast_weights, fast_gain, window_gain):
    row_count = queries.shape[0]
    head_count = step_sizes.shape[1]
    head_width = queries.shape[1] // head_count
    score_scale = 1.0 / math.sqrt(head_width)
    my_place = lax.axis_index("seq")
    copies = lax.all_gather(fast_weights.astype(jnp.bfloat16), "seq", axis=0, tiled=True)
    copies = copies.reshape(head_width, 3, head_count, head_width)
    w_first = copies[:, 0]
    w_third = copies[:, 1]
    w_second = copies[:, 2]
    query_heads = queries.reshape(row_count, head_count, head_width)
    key_heads = key_vectors.reshape(row_count, head_count, head_width)
    value_heads = value_vectors.reshape(row_count, head_count, head_width)

    def project(inputs, matrix):
        return (
            jnp.einsum("thr,rhc->thc", inputs, matrix, preferred_element_type=jnp.float32)
            * score_scale
        )

    gate_query = project(query_heads, w_first)
    up_query = project(query_heads, w_third)
    hidden_query = (jax.nn.silu(gate_query) * up_query).astype(jnp.bfloat16)
    fast_part = normalize(
        project(hidden_query, w_second), fast_gain.reshape(head_count, head_width)
    )
    reach_blocks = WINDOW // row_count
    earlier = []
    carried = (key_vectors, value_vectors)
    for offset in range(reach_blocks):
        carried = from_behind((carried[0], carried[1]), "seq", 1)
        earlier = [carried] + earlier
    window_keys = jnp.concatenate([shifted[0] for shifted in earlier] + [key_vectors], axis=0)
    window_values = jnp.concatenate([shifted[1] for shifted in earlier] + [value_vectors], axis=0)
    window_keys = window_keys.reshape(-1, head_count, head_width)
    window_values = window_values.reshape(-1, head_count, head_width)
    query_pos = jnp.arange(row_count, dtype=jnp.int32)[:, None] + reach_blocks * row_count
    key_pos = jnp.arange((reach_blocks + 1) * row_count, dtype=jnp.int32)[None, :]
    distance = query_pos - key_pos
    first_key = (my_place - reach_blocks) * row_count
    allowed = (distance >= 0) & (distance < WINDOW) & (key_pos + first_key >= 0)
    scores = (
        jnp.einsum("qhd,khd->hqk", query_heads, window_keys, preferred_element_type=jnp.float32)
        * score_scale
    )
    scores = jnp.where(allowed[None], scores, -jnp.inf)
    row_max = jnp.max(scores, axis=-1, keepdims=True)
    weights = jnp.exp(scores - row_max)
    attention_probs = (weights / jnp.sum(weights, axis=-1, keepdims=True)).astype(jnp.bfloat16)
    attended = jnp.einsum(
        "hqk,khd->qhd", attention_probs, window_values, preferred_element_type=jnp.float32
    )
    window_part = normalize(attended, window_gain.reshape(head_count, head_width))
    layer_out = (
        (fast_part + window_part).astype(jnp.bfloat16).reshape(row_count, head_count * head_width)
    )
    gate_key = project(key_heads, w_first)
    up_key = project(key_heads, w_third)
    hidden_key = (jax.nn.silu(gate_key) * up_key).astype(jnp.bfloat16)
    target = (-step_sizes[:, :, None] * value_heads.astype(jnp.float32)).astype(jnp.bfloat16)
    back_hidden = (
        jnp.einsum("thc,rhc->thr", target, w_second, preferred_element_type=jnp.float32)
        * score_scale
    )
    grad_gate = (back_hidden * up_key * silu_slope(gate_key)).astype(jnp.bfloat16)
    grad_up = (back_hidden * jax.nn.silu(gate_key)).astype(jnp.bfloat16)
    first = jnp.einsum("thr,thc->rhc", key_heads, grad_gate, preferred_element_type=jnp.float32)
    third = jnp.einsum("thr,thc->rhc", key_heads, grad_up, preferred_element_type=jnp.float32)
    second = jnp.einsum("thr,thc->rhc", hidden_key, target, preferred_element_type=jnp.float32)
    gradient = jnp.stack([first, third, second], axis=1).reshape(head_width, -1) * score_scale
    momentum = lax.psum_scatter(gradient, "seq", scatter_dimension=0, tiled=True)
    moved = fast_weights - momentum
    old_sum, new_sum = lax.psum(
        (jnp.sum(fast_weights * fast_weights, axis=0), jnp.sum(moved * moved, axis=0)), "seq"
    )
    new_weights = moved * jnp.sqrt((old_sum + 1e-06) / (new_sum + 1e-06))
    return (layer_out, new_weights, momentum)


def solution(mesh):
    in_specs = (
        P(("groups", "seq"), None),
        P(("groups", "seq"), None),
        P(("groups", "seq"), None),
        P(("groups", "seq"), None),
        P("seq", None),
        P(),
        P(),
    )
    out_specs = (P(("groups", "seq"), None), P(("groups", "seq"), None), P(("groups", "seq"), None))
    return jax.shard_map(shards, mesh=mesh, in_specs=in_specs, out_specs=out_specs, check_vma=False)
```

profile of v0, /device:TPU:0, one launch (start us, length us, event | category | flops | bytes accessed | tf_op | source)
XLA Modules:
  0.0 501.6 jit_solution(17470583284559178395)
XLA Ops:
  7.2 2.5 collective-permute-start
  9.8 4.5 collective-permute-start.8
  14.3 7.8 %collective-permute-start.1 = (bf16[128,2560]{1,0:T(8,128)(2,1)S(1)}, bf16[128,2560]{1,0:T(8,128)(2,1)S(1)}, u32[]{:S(2)}, u32[]{:S(2)}) collective-permute-start(bf16[128,2560]{1,0:T(8,128)(2,1)S(1)} %collective-permute-done), channel_id=1, source_target_pairs={{0,1},{1,2},{2,3},{3,4},{4,5},{5,6},{6,7},{7,8},{8,9},{9,10},{10,1... | collective-permute-start | bytes 1966088 | tf_op jit(solution)/shard_map/ppermute | solution.py:14
  22.1 7.0 %collective-permute-start.9 = (bf16[128,2560]{1,0:T(8,128)(2,1)S(1)}, bf16[128,2560]{1,0:T(8,128)(2,1)S(1)}, u32[]{:S(2)}, u32[]{:S(2)}) collective-permute-start(bf16[128,2560]{1,0:T(8,128)(2,1)S(1)} %collective-permute-done.8), channel_id=1, source_target_pairs={{0,1},{1,2},{2,3},{3,4},{4,5},{5,6},{6,7},{7,8},{8,9},{9,10},{10,1... | collective-permute-start | bytes 1966088 | tf_op jit(solution)/shard_map/ppermute | solution.py:14
  29.2 6.9 %collective-permute-start.2 = (bf16[128,2560]{1,0:T(8,128)(2,1)S(1)}, bf16[128,2560]{1,0:T(8,128)(2,1)S(1)}, u32[]{:S(2)}, u32[]{:S(2)}) collective-permute-start(bf16[128,2560]{1,0:T(8,128)(2,1)S(1)} %collective-permute-done.1), channel_id=1, source_target_pairs={{0,1},{1,2},{2,3},{3,4},{4,5},{5,6},{6,7},{7,8},{8,9},{9,10},{10,1... | collective-permute-start | bytes 1966088 | tf_op jit(solution)/shard_map/ppermute | solution.py:14
  37.0 7.0 %collective-permute-start.10 = (bf16[128,2560]{1,0:T(8,128)(2,1)S(1)}, bf16[128,2560]{1,0:T(8,128)(2,1)S(1)}, u32[]{:S(2)}, u32[]{:S(2)}) collective-permute-start(bf16[128,2560]{1,0:T(8,128)(2,1)S(1)} %collective-permute-done.9), channel_id=1, source_target_pairs={{0,1},{1,2},{2,3},{3,4},{4,5},{5,6},{6,7},{7,8},{8,9},{9,10},{10,1... | collective-permute-start | bytes 1966088 | tf_op jit(solution)/shard_map/ppermute | solution.py:14
  44.0 6.1 %collective-permute-start.3 = (bf16[128,2560]{1,0:T(8,128)(2,1)S(1)}, bf16[128,2560]{1,0:T(8,128)(2,1)S(1)}, u32[]{:S(2)}, u32[]{:S(2)}) collective-permute-start(bf16[128,2560]{1,0:T(8,128)(2,1)S(1)} %collective-permute-done.2), channel_id=1, source_target_pairs={{0,1},{1,2},{2,3},{3,4},{4,5},{5,6},{6,7},{7,8},{8,9},{9,10},{10,1... | collective-permute-start | bytes 1966088 | tf_op jit(solution)/shard_map/ppermute | solution.py:14
  50.1 7.0 %collective-permute-start.11 = (bf16[128,2560]{1,0:T(8,128)(2,1)S(1)}, bf16[128,2560]{1,0:T(8,128)(2,1)S(1)}, u32[]{:S(2)}, u32[]{:S(2)}) collective-permute-start(bf16[128,2560]{1,0:T(8,128)(2,1)S(1)} %collective-permute-done.10), channel_id=1, source_target_pairs={{0,1},{1,2},{2,3},{3,4},{4,5},{5,6},{6,7},{7,8},{8,9},{9,10},{10,1... | collective-permute-start | bytes 1966088 | tf_op jit(solution)/shard_map/ppermute | solution.py:14
  57.2 7.0 %collective-permute-start.4 = (bf16[128,2560]{1,0:T(8,128)(2,1)S(1)}, bf16[128,2560]{1,0:T(8,128)(2,1)S(1)}, u32[]{:S(2)}, u32[]{:S(2)}) collective-permute-start(bf16[128,2560]{1,0:T(8,128)(2,1)S(1)} %collective-permute-done.3), channel_id=1, source_target_pairs={{0,1},{1,2},{2,3},{3,4},{4,5},{5,6},{6,7},{7,8},{8,9},{9,10},{10,1... | collective-permute-start | bytes 1966088 | tf_op jit(solution)/shard_map/ppermute | solution.py:14
  64.2 7.8 %collective-permute-start.12 = (bf16[128,2560]{1,0:T(8,128)(2,1)S(1)}, bf16[128,2560]{1,0:T(8,128)(2,1)}, u32[]{:S(2)}, u32[]{:S(2)}) collective-permute-start(bf16[128,2560]{1,0:T(8,128)(2,1)S(1)} %collective-permute-done.11), channel_id=1, source_target_pairs={{0,1},{1,2},{2,3},{3,4},{4,5},{5,6},{6,7},{7,8},{8,9},{9,10},{10,1... | collective-permute-start | bytes 1966088 | tf_op jit(solution)/shard_map/ppermute | solution.py:14
  72.0 7.0 %collective-permute-start.5 = (bf16[128,2560]{1,0:T(8,128)(2,1)S(1)}, bf16[128,2560]{1,0:T(8,128)(2,1)}, u32[]{:S(2)}, u32[]{:S(2)}) collective-permute-start(bf16[128,2560]{1,0:T(8,128)(2,1)S(1)} %collective-permute-done.4), channel_id=1, source_target_pairs={{0,1},{1,2},{2,3},{3,4},{4,5},{5,6},{6,7},{7,8},{8,9},{9,10},{10,1... | collective-permute-start | bytes 1966088 | tf_op jit(solution)/shard_map/ppermute | solution.py:14
  79.0 2.2 multiply_reduce_fusion.3
  81.2 4.8 collective-permute-start.13
  86.0 7.1 %collective-permute-start.6 = (bf16[128,2560]{1,0:T(8,128)(2,1)}, bf16[128,2560]{1,0:T(8,128)(2,1)}, u32[]{:S(2)}, u32[]{:S(2)}) collective-permute-start(bf16[128,2560]{1,0:T(8,128)(2,1)} %collective-permute-done.5), channel_id=1, source_target_pairs={{0,1},{1,2},{2,3},{3,4},{4,5},{5,6},{6,7},{7,8},{8,9},{9,10},{10,1... | collective-permute-start | bytes 1966088 | tf_op jit(solution)/shard_map/ppermute | solution.py:14
  93.1 1.4 copy.45
  97.3 6.8 %collective-permute-start.14 = (bf16[128,2560]{1,0:T(8,128)(2,1)}, bf16[128,2560]{1,0:T(8,128)(2,1)}, u32[]{:S(2)}, u32[]{:S(2)}) collective-permute-start(bf16[128,2560]{1,0:T(8,128)(2,1)} %collective-permute-done.13), channel_id=1, source_target_pairs={{0,1},{1,2},{2,3},{3,4},{4,5},{5,6},{6,7},{7,8},{8,9},{9,10},{10,1... | collective-permute-start | bytes 1966088 | tf_op jit(solution)/shard_map/ppermute | solution.py:14
  104.1 6.2 %collective-permute-start.7 = (bf16[128,2560]{1,0:T(8,128)(2,1)}, bf16[128,2560]{1,0:T(8,128)(2,1)S(1)}, u32[]{:S(2)}, u32[]{:S(2)}) collective-permute-start(bf16[128,2560]{1,0:T(8,128)(2,1)} %collective-permute-done.6), channel_id=1, source_target_pairs={{0,1},{1,2},{2,3},{3,4},{4,5},{5,6},{6,7},{7,8},{8,9},{9,10},{10,1... | collective-permute-start | bytes 1966088 | tf_op jit(solution)/shard_map/ppermute | solution.py:14
  110.6 7.6 %collective-permute-start.15 = (bf16[128,2560]{1,0:T(8,128)(2,1)}, bf16[128,2560]{1,0:T(8,128)(2,1)}, u32[]{:S(2)}, u32[]{:S(2)}) collective-permute-start(bf16[128,2560]{1,0:T(8,128)(2,1)} %collective-permute-done.14), channel_id=1, source_target_pairs={{0,1},{1,2},{2,3},{3,4},{4,5},{5,6},{6,7},{7,8},{8,9},{9,10},{10,1... | collective-permute-start | bytes 1966088 | tf_op jit(solution)/shard_map/ppermute | solution.py:14
  119.1 2.1 constant_dynamic-update-slice_fusion.7
  121.2 2.0 constant_dynamic-update-slice_fusion.6
  128.6 9.0 %copy.40 = bf16[1152,2560]{0,1:T(8,128)(2,1)} copy(bf16[1152,2560]{1,0:T(8,128)(2,1)} %constant_dynamic-update-slice_fusion) | data formatting | bytes 11796480 | tf_op jit(solution)/shard_map/concatenate | solution.py:61
  137.6 2.0 constant_dynamic-update-slice_fusion.17
  139.6 2.1 constant_dynamic-update-slice_fusion.16
  141.7 2.0 constant_dynamic-update-slice_fusion.15
  143.7 2.0 constant_dynamic-update-slice_fusion.14
  150.2 9.0 %copy.41 = bf16[1152,2560]{0,1:T(8,128)(2,1)} copy(bf16[1152,2560]{1,0:T(8,128)(2,1)} %constant_dynamic-update-slice_fusion.9) | data formatting | bytes 11796480 | tf_op jit(solution)/shard_map/concatenate | solution.py:60
  159.1 4.8 convolution_multiply_fusion
  163.9 1.2 exponential_reduce_fusion
  166.0 7.1 %multiply_reduce_fusion = (f32[128,8]{0,1:T(8,128)S(1)}, f32[128,8,320]{0,2,1:T(8,128)}) fusion(bf16[1152,8,320]{0,2,1:T(8,128)(2,1)} %bitcast.127, f32[8,128]{1,0:T(8,128)S(1)} %exponential_reduce_fusion, f32[8,1152,128]{2,1,0:T(8,128)} %copy-done.4, pred[128,1152]{0,1:T(8,128)(4,1)S(1)} %fusion.69), kind=kOutput, calls=%fused_computation.48 | convolution fusion | flops 760349824 | bytes 12083200 | tf_op jit(solution)/shard_map/hqk,khd->qhd/dot_general | solution.py:77
  173.1 9.3 %reshape.102 = bf16[320,3,8,320]{3,2,1,0:T(8,128)(2,1)} reshape(bf16[16,20,7680]{2,1,0:T(8,128)(2,1)} %all-gather.3.cloned.1.call-done) | data formatting | bytes 9830400 | tf_op jit(solution)/shard_map/reshape | solution.py:34
  182.5 5.2 %fusion.82 = (bf16[320,1,8,320]{3,2,1,0:T(8,128)(2,1)}, bf16[320,1,8,320]{3,2,1,0:T(8,128)(2,1)}, bf16[320,1,8,320]{3,2,1,0:T(8,128)(2,1)S(1)}) fusion(bf16[320,3,8,320]{3,2,1,0:T(8,128)(2,1)} %reshape.102), kind=kLoop, calls=%fused_computation.93 | loop fusion | bytes 9830400 | tf_op jit(solution)/shard_map/slice | solution.py:35
  187.7 2.8 copy.52
  190.5 3.1 copy.51
  193.6 1.8 fusion.22
  195.4 4.1 copy.50
  205.7 5.3 %maximum_multiply_fusion = f32[320,3,8,320]{0,3,2,1:T(8,128)} fusion(f32[320,1,8,320]{0,3,2,1:T(8,128)S(1)} %convolution_bitcast_fusion, f32[320,1,8,320]{0,3,2,1:T(8,128)S(1)} %convolution_bitcast_fusion.1, f32[320,1,8,320]{0,3,2,1:T(8,128)S(1)} %convolution_bitcast_fusion.2), kind=kLoop, calls=%fused_computation.1 | loop fusion | flops 7372800 | bytes 19660800 | tf_op jit(solution)/shard_map/mul | solution.py:97
  210.9 11.7 %copy.46 = f32[320,7680]{1,0:T(8,128)} copy(f32[320,7680]{0,1:T(8,128)} %bitcast.116) | data formatting | bytes 19660800 | tf_op jit(solution)/shard_map/mul | solution.py:97
  222.7 138.9 %fusion = f32[24,7680]{1,0:T(8,128)} fusion(f32[320,7680]{1,0:T(8,128)} %copy.46), kind=kCustom, calls=%all-reduce-scatter | all-reduce-scatter fusion | flops 2949121 | bytes 10568192
  361.5 19.8 %collective-permute-start.17 = (f32[24,7680]{1,0:T(8,128)}, f32[24,7680]{1,0:T(8,128)}, u32[]{:S(2)}, u32[]{:S(2)}) collective-permute-start(f32[24,7680]{1,0:T(8,128)} %fusion), channel_id=1, source_target_pairs={{0,2},{1,3},{2,4},{3,5},{4,6},{5,7},{6,8},{7,9},{8,10},{9,11},{10,... | collective-permute-start | bytes 2211848
  381.3 2.2 collective-permute-start.16
  383.4 4.2 multiply_reduce_fusion.1
  388.7 14.1 %collective-permute-start.18 = (f32[12,7680]{1,0:T(8,128)S(1)}, f32[12,7680]{1,0:T(8,128)S(1)}, u32[]{:S(2)}, u32[]{:S(2)}) collective-permute-start(f32[12,7680]{1,0:T(8,128)S(1)} %slice.15), channel_id=1, source_target_pairs={{0,3},{1,4},{2,5},{3,6},{4,7},{5,8},{6,9},{7,10},{8,11},{9,12},{10... | collective-permute-start | bytes 1105928
  402.8 2.2 add_convert_fusion
  405.1 1.1 copy.47
  406.2 2.9 collective-permute-done.18
  409.9 7.8 %concatenate.8 = f32[84,7680]{1,0:T(8,128)S(1)} concatenate(f32[12,7680]{1,0:T(8,128)} %copy-done.24, f32[24,7680]{1,0:T(8,128)} %collective-permute-done.17, f32[24,7680]{1,0:T(8,128)} %collective-permute-done.16, f32[24,7680]{1,0:T(8,128)S(1)} %copy-done.3), dimensions={0} | concatenate | bytes 5160960
  417.7 2.1 multiply_reduce_fusion.2
  419.8 74.0 %all-reduce.2 = (f32[7680]{0:T(1024)S(1)}, f32[7680]{0:T(1024)S(1)}) all-reduce(f32[7680]{0:T(1024)S(1)} %get-tuple-element.14, f32[7680]{0:T(1024)S(1)} %get-tuple-element.20), channel_id=1, replica_groups=mesh['groups'=2,'seq'=16] {'seq'}, use_global_device_ids=true, to_apply=%region_8.9 | all-reduce | flops 15360 | bytes 122880 | tf_op jit(solution)/shard_map/psum | solution.py:100
  (110 shorter events, 23.9 us)
Async XLA Ops:
  7.2 87.4 %copy-start.5 = (bf16[128,2560]{1,0:T(8,128)(2,1)S(1)}, bf16[128,2560]{1,0:T(8,128)(2,1)}, u32[]{:S(2)}) copy-start(bf16[128,2560]{1,0:T(8,128)(2,1)} %param.9) | copy-start | bytes 1966084
  7.2 88.5 %copy-start.7 = (bf16[128,2560]{1,0:T(8,128)(2,1)S(1)}, bf16[128,2560]{1,0:T(8,128)(2,1)}, u32[]{:S(2)}) copy-start(bf16[128,2560]{1,0:T(8,128)(2,1)} %param.7) | copy-start | bytes 1966084
  7.2 166.0 %all-gather.3.cloned.1.call-start = ((), (), s32[]{:S(2)}) async-start(), calls=%async_computation | async-start | bytes 6266880 | tf_op jit(solution)/shard_map/all_gather | solution.py:33
  7.2 7.1 %collective-permute-start = (bf16[128,2560]{1,0:T(8,128)(2,1)}, bf16[128,2560]{1,0:T(8,128)(2,1)S(1)}, u32[]{:S(2)}, u32[]{:S(2)}) collective-permute-start(bf16[128,2560]{1,0:T(8,128)(2,1)} %param.9), channel_id=1, source_target_pairs={{0,1},{1,2},{2,3},{3,4},{4,5},{5,6},{6,7},{7,8},{8,9},{9,10},{10,1... | collective-permute-start | bytes 1966088 | tf_op jit(solution)/shard_map/ppermute | solution.py:14
  9.8 12.4 %collective-permute-start.8 = (bf16[128,2560]{1,0:T(8,128)(2,1)}, bf16[128,2560]{1,0:T(8,128)(2,1)S(1)}, u32[]{:S(2)}, u32[]{:S(2)}) collective-permute-start(bf16[128,2560]{1,0:T(8,128)(2,1)} %param.8), channel_id=1, source_target_pairs={{0,1},{1,2},{2,3},{3,4},{4,5},{5,6},{6,7},{7,8},{8,9},{9,10},{10,1... | collective-permute-start | bytes 1966088 | tf_op jit(solution)/shard_map/ppermute | solution.py:14
  14.3 35.8 %copy-start.10 = (bf16[128,2560]{1,0:T(8,128)(2,1)}, bf16[128,2560]{1,0:T(8,128)(2,1)S(1)}, u32[]{:S(2)}) copy-start(bf16[128,2560]{1,0:T(8,128)(2,1)S(1)} %collective-permute-done) | copy-start | bytes 1966084
  14.3 14.8 %collective-permute-start.1 = (bf16[128,2560]{1,0:T(8,128)(2,1)S(1)}, bf16[128,2560]{1,0:T(8,128)(2,1)S(1)}, u32[]{:S(2)}, u32[]{:S(2)}) collective-permute-start(bf16[128,2560]{1,0:T(8,128)(2,1)S(1)} %collective-permute-done), channel_id=1, source_target_pairs={{0,1},{1,2},{2,3},{3,4},{4,5},{5,6},{6,7},{7,8},{8,9},{9,10},{10,1... | collective-permute-start | bytes 1966088 | tf_op jit(solution)/shard_map/ppermute | solution.py:14
  22.1 13.9 %collective-permute-start.9 = (bf16[128,2560]{1,0:T(8,128)(2,1)S(1)}, bf16[128,2560]{1,0:T(8,128)(2,1)S(1)}, u32[]{:S(2)}, u32[]{:S(2)}) collective-permute-start(bf16[128,2560]{1,0:T(8,128)(2,1)S(1)} %collective-permute-done.8), channel_id=1, source_target_pairs={{0,1},{1,2},{2,3},{3,4},{4,5},{5,6},{6,7},{7,8},{8,9},{9,10},{10,1... | collective-permute-start | bytes 1966088 | tf_op jit(solution)/shard_map/ppermute | solution.py:14
  29.2 35.0 %copy-start.14 = (bf16[128,2560]{1,0:T(8,128)(2,1)}, bf16[128,2560]{1,0:T(8,128)(2,1)S(1)}, u32[]{:S(2)}) copy-start(bf16[128,2560]{1,0:T(8,128)(2,1)S(1)} %collective-permute-done.1) | copy-start | bytes 1966084
  29.2 14.8 %collective-permute-start.2 = (bf16[128,2560]{1,0:T(8,128)(2,1)S(1)}, bf16[128,2560]{1,0:T(8,128)(2,1)S(1)}, u32[]{:S(2)}, u32[]{:S(2)}) collective-permute-start(bf16[128,2560]{1,0:T(8,128)(2,1)S(1)} %collective-permute-done.1), channel_id=1, source_target_pairs={{0,1},{1,2},{2,3},{3,4},{4,5},{5,6},{6,7},{7,8},{8,9},{9,10},{10,1... | collective-permute-start | bytes 1966088 | tf_op jit(solution)/shard_map/ppermute | solution.py:14
  36.1 0.9 copy-start.8
  37.0 13.2 %collective-permute-start.10 = (bf16[128,2560]{1,0:T(8,128)(2,1)S(1)}, bf16[128,2560]{1,0:T(8,128)(2,1)S(1)}, u32[]{:S(2)}, u32[]{:S(2)}) collective-permute-start(bf16[128,2560]{1,0:T(8,128)(2,1)S(1)} %collective-permute-done.9), channel_id=1, source_target_pairs={{0,1},{1,2},{2,3},{3,4},{4,5},{5,6},{6,7},{7,8},{8,9},{9,10},{10,1... | collective-permute-start | bytes 1966088 | tf_op jit(solution)/shard_map/ppermute | solution.py:14
  44.0 28.0 %copy-start.18 = (bf16[128,2560]{1,0:T(8,128)(2,1)}, bf16[128,2560]{1,0:T(8,128)(2,1)S(1)}, u32[]{:S(2)}) copy-start(bf16[128,2560]{1,0:T(8,128)(2,1)S(1)} %collective-permute-done.2) | copy-start | bytes 1966084
  44.0 13.2 %collective-permute-start.3 = (bf16[128,2560]{1,0:T(8,128)(2,1)S(1)}, bf16[128,2560]{1,0:T(8,128)(2,1)S(1)}, u32[]{:S(2)}, u32[]{:S(2)}) collective-permute-start(bf16[128,2560]{1,0:T(8,128)(2,1)S(1)} %collective-permute-done.2), channel_id=1, source_target_pairs={{0,1},{1,2},{2,3},{3,4},{4,5},{5,6},{6,7},{7,8},{8,9},{9,10},{10,1... | collective-permute-start | bytes 1966088 | tf_op jit(solution)/shard_map/ppermute | solution.py:14
  50.1 7.0 %copy-start.12 = (bf16[128,2560]{1,0:T(8,128)(2,1)}, bf16[128,2560]{1,0:T(8,128)(2,1)S(1)}, u32[]{:S(2)}) copy-start(bf16[128,2560]{1,0:T(8,128)(2,1)S(1)} %collective-permute-done.10) | copy-start | bytes 1966084
  50.1 14.0 %collective-permute-start.11 = (bf16[128,2560]{1,0:T(8,128)(2,1)S(1)}, bf16[128,2560]{1,0:T(8,128)(2,1)S(1)}, u32[]{:S(2)}, u32[]{:S(2)}) collective-permute-start(bf16[128,2560]{1,0:T(8,128)(2,1)S(1)} %collective-permute-done.10), channel_id=1, source_target_pairs={{0,1},{1,2},{2,3},{3,4},{4,5},{5,6},{6,7},{7,8},{8,9},{9,10},{10,1... | collective-permute-start | bytes 1966088 | tf_op jit(solution)/shard_map/ppermute | solution.py:14
  57.2 14.8 %copy-start.20 = (bf16[128,2560]{1,0:T(8,128)(2,1)}, bf16[128,2560]{1,0:T(8,128)(2,1)S(1)}, u32[]{:S(2)}) copy-start(bf16[128,2560]{1,0:T(8,128)(2,1)S(1)} %collective-permute-done.3) | copy-start | bytes 1966084
  57.2 14.8 %collective-permute-start.4 = (bf16[128,2560]{1,0:T(8,128)(2,1)S(1)}, bf16[128,2560]{1,0:T(8,128)(2,1)S(1)}, u32[]{:S(2)}, u32[]{:S(2)}) collective-permute-start(bf16[128,2560]{1,0:T(8,128)(2,1)S(1)} %collective-permute-done.3), channel_id=1, source_target_pairs={{0,1},{1,2},{2,3},{3,4},{4,5},{5,6},{6,7},{7,8},{8,9},{9,10},{10,1... | collective-permute-start | bytes 1966088 | tf_op jit(solution)/shard_map/ppermute | solution.py:14
  64.2 28.9 %copy-start.16 = (bf16[128,2560]{1,0:T(8,128)(2,1)}, bf16[128,2560]{1,0:T(8,128)(2,1)S(1)}, u32[]{:S(2)}) copy-start(bf16[128,2560]{1,0:T(8,128)(2,1)S(1)} %collective-permute-done.11) | copy-start | bytes 1966084
  64.2 17.0 %collective-permute-start.12 = (bf16[128,2560]{1,0:T(8,128)(2,1)S(1)}, bf16[128,2560]{1,0:T(8,128)(2,1)}, u32[]{:S(2)}, u32[]{:S(2)}) collective-permute-start(bf16[128,2560]{1,0:T(8,128)(2,1)S(1)} %collective-permute-done.11), channel_id=1, source_target_pairs={{0,1},{1,2},{2,3},{3,4},{4,5},{5,6},{6,7},{7,8},{8,9},{9,10},{10,1... | collective-permute-start | bytes 1966088 | tf_op jit(solution)/shard_map/ppermute | solution.py:14
  72.0 23.7 %copy-start.22 = (bf16[128,2560]{1,0:T(8,128)(2,1)}, bf16[128,2560]{1,0:T(8,128)(2,1)S(1)}, u32[]{:S(2)}) copy-start(bf16[128,2560]{1,0:T(8,128)(2,1)S(1)} %collective-permute-done.4) | copy-start | bytes 1966084
  72.0 14.0 %collective-permute-start.5 = (bf16[128,2560]{1,0:T(8,128)(2,1)S(1)}, bf16[128,2560]{1,0:T(8,128)(2,1)}, u32[]{:S(2)}, u32[]{:S(2)}) collective-permute-start(bf16[128,2560]{1,0:T(8,128)(2,1)S(1)} %collective-permute-done.4), channel_id=1, source_target_pairs={{0,1},{1,2},{2,3},{3,4},{4,5},{5,6},{6,7},{7,8},{8,9},{9,10},{10,1... | collective-permute-start | bytes 1966088 | tf_op jit(solution)/shard_map/ppermute | solution.py:14
  81.2 16.1 %collective-permute-start.13 = (bf16[128,2560]{1,0:T(8,128)(2,1)}, bf16[128,2560]{1,0:T(8,128)(2,1)}, u32[]{:S(2)}, u32[]{:S(2)}) collective-permute-start(bf16[128,2560]{1,0:T(8,128)(2,1)} %collective-permute-done.12), channel_id=1, source_target_pairs={{0,1},{1,2},{2,3},{3,4},{4,5},{5,6},{6,7},{7,8},{8,9},{9,10},{10,1... | collective-permute-start | bytes 1966088 | tf_op jit(solution)/shard_map/ppermute | solution.py:14
  86.0 18.1 %collective-permute-start.6 = (bf16[128,2560]{1,0:T(8,128)(2,1)}, bf16[128,2560]{1,0:T(8,128)(2,1)}, u32[]{:S(2)}, u32[]{:S(2)}) collective-permute-start(bf16[128,2560]{1,0:T(8,128)(2,1)} %collective-permute-done.5), channel_id=1, source_target_pairs={{0,1},{1,2},{2,3},{3,4},{4,5},{5,6},{6,7},{7,8},{8,9},{9,10},{10,1... | collective-permute-start | bytes 1966088 | tf_op jit(solution)/shard_map/ppermute | solution.py:14
  93.1 2.9 copy-start.25
  93.1 3.0 copy-start.26
  93.1 3.0 copy-start.27
  93.1 3.0 copy-start.28
  97.3 13.3 %collective-permute-start.14 = (bf16[128,2560]{1,0:T(8,128)(2,1)}, bf16[128,2560]{1,0:T(8,128)(2,1)}, u32[]{:S(2)}, u32[]{:S(2)}) collective-permute-start(bf16[128,2560]{1,0:T(8,128)(2,1)} %collective-permute-done.13), channel_id=1, source_target_pairs={{0,1},{1,2},{2,3},{3,4},{4,5},{5,6},{6,7},{7,8},{8,9},{9,10},{10,1... | collective-permute-start | bytes 1966088 | tf_op jit(solution)/shard_map/ppermute | solution.py:14
  104.1 14.0 %collective-permute-start.7 = (bf16[128,2560]{1,0:T(8,128)(2,1)}, bf16[128,2560]{1,0:T(8,128)(2,1)S(1)}, u32[]{:S(2)}, u32[]{:S(2)}) collective-permute-start(bf16[128,2560]{1,0:T(8,128)(2,1)} %collective-permute-done.6), channel_id=1, source_target_pairs={{0,1},{1,2},{2,3},{3,4},{4,5},{5,6},{6,7},{7,8},{8,9},{9,10},{10,1... | collective-permute-start | bytes 1966088 | tf_op jit(solution)/shard_map/ppermute | solution.py:14
  110.6 12.6 %copy-start.23 = (bf16[128,2560]{1,0:T(8,128)(2,1)S(1)}, bf16[128,2560]{1,0:T(8,128)(2,1)}, u32[]{:S(2)}) copy-start(bf16[128,2560]{1,0:T(8,128)(2,1)} %copy-done.22) | copy-start | bytes 1966084
  110.6 27.0 %collective-permute-start.15 = (bf16[128,2560]{1,0:T(8,128)(2,1)}, bf16[128,2560]{1,0:T(8,128)(2,1)}, u32[]{:S(2)}, u32[]{:S(2)}) collective-permute-start(bf16[128,2560]{1,0:T(8,128)(2,1)} %collective-permute-done.14), channel_id=1, source_target_pairs={{0,1},{1,2},{2,3},{3,4},{4,5},{5,6},{6,7},{7,8},{8,9},{9,10},{10,1... | collective-permute-start | bytes 1966088 | tf_op jit(solution)/shard_map/ppermute | solution.py:14
  119.1 5.0 %copy-start.21 = (bf16[128,2560]{1,0:T(8,128)(2,1)S(1)}, bf16[128,2560]{1,0:T(8,128)(2,1)}, u32[]{:S(2)}) copy-start(bf16[128,2560]{1,0:T(8,128)(2,1)} %copy-done.20) | copy-start | bytes 1966084
  121.2 3.8 copy-start.19
  123.2 2.7 copy-start.15
  124.1 2.7 copy-start.11
  139.6 6.2 %copy-start.17 = (bf16[128,2560]{1,0:T(8,128)(2,1)S(1)}, bf16[128,2560]{1,0:T(8,128)(2,1)}, u32[]{:S(2)}) copy-start(bf16[128,2560]{1,0:T(8,128)(2,1)} %copy-done.16) | copy-start | bytes 1966084
  141.7 4.9 copy-start.13
  143.7 3.8 copy-start.9
  146.6 2.7 copy-start.6
  163.9 2.1 copy-start.4
  199.5 1.5 copy-start.1
  201.0 1.5 copy-start
  201.0 1.7 copy-start.2
  361.5 47.6 %collective-permute-start.17 = (f32[24,7680]{1,0:T(8,128)}, f32[24,7680]{1,0:T(8,128)}, u32[]{:S(2)}, u32[]{:S(2)}) collective-permute-start(f32[24,7680]{1,0:T(8,128)} %fusion), channel_id=1, source_target_pairs={{0,2},{1,3},{2,4},{3,5},{4,6},{5,7},{6,8},{7,9},{8,10},{9,11},{10,... | collective-permute-start | bytes 2211848
  381.3 28.6 %collective-permute-start.16 = (f32[24,7680]{1,0:T(8,128)}, f32[24,7680]{1,0:T(8,128)}, u32[]{:S(2)}, u32[]{:S(2)}) collective-permute-start(f32[24,7680]{1,0:T(8,128)} %fusion), channel_id=1, source_target_pairs={{0,1},{1,2},{2,3},{3,4},{4,5},{5,6},{6,7},{7,8},{8,9},{9,10},{10,1... | collective-permute-start | bytes 2211848
  388.7 20.4 %collective-permute-start.18 = (f32[12,7680]{1,0:T(8,128)S(1)}, f32[12,7680]{1,0:T(8,128)S(1)}, u32[]{:S(2)}, u32[]{:S(2)}) collective-permute-start(f32[12,7680]{1,0:T(8,128)S(1)} %slice.15), channel_id=1, source_target_pairs={{0,3},{1,4},{2,5},{3,6},{4,7},{5,8},{6,9},{7,10},{8,11},{9,12},{10... | collective-permute-start | bytes 1105928
  402.8 7.1 %copy-start.3 = (f32[24,7680]{1,0:T(8,128)S(1)}, f32[24,7680]{1,0:T(8,128)}, u32[]{:S(2)}) copy-start(f32[24,7680]{1,0:T(8,128)} %fusion) | copy-start | bytes 2211844
  (1 other events, 0.8 us)
Sparse Core Ops, SparseCore 0:
  81.3 73.0 all-gather.2
where the time goes:
time: 504 us; the launch traced here: 502 us
  blocking collectives  213 us (42%)
  starting transfers between devices  139 us (28%)
  local copies, waits for them, and re-layouts  95.2 us (19%)
  matrix products  22.1 us (4%)
  between operations  15.1 us (3%)
  other arithmetic  14.2 us (3%)
    unnamed x1, blocking collectives  139 us
    ppermute x16, starting transfers between devices, from_behind(): lax.ppermute(value, axis, [(source, source + steps) for source in range(f...  103 us
    psum x1, blocking collectives, shards(): lax.psum((jnp.sum(fast_weights * fast_weights, axis=0), jnp.sum(moved * m...  74 us
    unnamed x84, local copies, waits for them, and re-layouts  49.1 us
    unnamed x3, starting transfers between devices  36 us
    mul x1, local copies, waits for them, and re-layouts, shards(): jnp.stack([first, third, second], axis=1).reshape(head_width, -1)  11.7 us
  transfers between devices with their start and end apart: 20, of which 1 were waited for; matrix products, arithmetic and copies ran while one was open for 14% of the time, Pallas kernels for 0%

commit v1 on v0

v1 whole, which is shorter than its diff:
```python
import functools
import math

import jax
import jax.numpy as jnp
from jax import lax
from jax.experimental import pallas as pl
from jax.experimental.pallas import tpu as pltpu
from jax.sharding import PartitionSpec as P

WINDOW = 1024
LANES = 128
HALF = 64
VMEM_LIMIT = 48 * 1024 * 1024
BF16 = jnp.bfloat16
F32 = jnp.float32
ORDER = (4, 5, 6, 7, 2, 3, 1)
ANY = pl.BlockSpec(memory_space=pl.ANY)
VMEM = pl.BlockSpec(memory_space=pltpu.VMEM)


def tiles_of(head):
    first = (5 * head) // 2
    odd = head % 2
    return (first + odd) * LANES, (first if odd else first + 2) * LANES


def turned(tile):
    return pltpu.roll(tile, HALF, axis=1)


def low_lanes(rows):
    return lax.broadcasted_iota(jnp.int32, (rows, LANES), 1) < HALF


def dot(left, right, contract):
    return lax.dot_general(left, right, (contract, ((), ())), preferred_element_type=F32)


def chip_core(width):
    place = lax.axis_index("seq")
    return place // width, lax.rem(place, width)


def copy_all(pairs, sems):
    copies = [pltpu.make_async_copy(src, dst, sems.at[i]) for i, (src, dst) in enumerate(pairs)]
    for copy in copies:
        copy.start()
    return copies


def pack_keys(width, heads, rows, slot, k_ref, v_ref, step_ref, fw_ref, *rest):
    outs, (pay, wbuf, sems) = rest[:heads], rest[heads:]
    chip, _ = chip_core(width)
    tokens = k_ref.shape[0]
    low = low_lanes(tokens)
    low_r = low_lanes(rows)
    matrix = fw_ref.shape[1] // 3
    steps = step_ref[...].T
    high = steps.astype(BF16).astype(F32)
    middle = (steps - high).astype(BF16).astype(F32)
    rest_ = (steps - high - middle).astype(BF16).astype(F32)
    wbuf[...] = jnp.zeros_like(wbuf)
    for head in range(heads):
        whole, half = tiles_of(head)
        odd = head % 2
        pay[head, 0:tokens] = k_ref[:, whole : whole + LANES]
        pay[head, tokens : 2 * tokens] = k_ref[:, whole + LANES : whole + 2 * LANES]
        pay[head, 3 * tokens : 4 * tokens] = v_ref[:, whole : whole + LANES]
        pay[head, 4 * tokens : 5 * tokens] = v_ref[:, whole + LANES : whole + 2 * LANES]
        k_half = k_ref[:, half : half + LANES].astype(F32)
        v_half = v_ref[:, half : half + LANES].astype(F32)
        mixed = jnp.where(low, turned(k_half) if odd else k_half, v_half if odd else turned(v_half))
        pay[head, 2 * tokens : 3 * tokens] = mixed.astype(BF16)
        halves = []
        for m in range(3):
            base = m * matrix
            for t in range(2):
                at = (2 * m + t) * slot
                lane = base + whole + t * LANES
                wbuf[at : at + rows] = fw_ref[:, lane : lane + LANES]
            halves.append(fw_ref[:, base + half : base + half + LANES])
        first, third, second = halves
        if odd:
            first, third = turned(first), turned(third)
        else:
            second = turned(second)
        wbuf[6 * slot : 6 * slot + rows] = jnp.where(low_r, first, second)
        wbuf[7 * slot : 7 * slot + rows] = jnp.where(low_r, third, 0.0)
        wbuf[rows : rows + 1] = high[head : head + 1]
        wbuf[rows + 1 : rows + 2] = middle[head : head + 1]
        wbuf[rows + 2 : rows + 3] = rest_[head : head + 1]
        pay[head, 5 * tokens :] = wbuf[...].astype(BF16)
    for copy in copy_all([(pay.at[chip ^ k], outs[k]) for k in range(heads)], sems):
        copy.wait()


def pack_queries(width, heads, q_ref, *rest):
    outs, (pay, sems) = rest[:heads], rest[heads:]
    chip, _ = chip_core(width)
    tokens = q_ref.shape[0]
    mid = tokens // 2
    low = low_lanes(mid)
    for head in range(heads):
        whole, half = tiles_of(head)
        pay[head, 0:tokens] = q_ref[:, whole : whole + LANES]
        pay[head, tokens : 2 * tokens] = q_ref[:, whole + LANES : whole + 2 * LANES]
        top = q_ref[0:mid, half : half + LANES].astype(F32)
        bottom = q_ref[mid:, half : half + LANES].astype(F32)
        if head % 2:
            top = turned(top)
        else:
            bottom = turned(bottom)
        pay[head, 2 * tokens :] = jnp.where(low, top, bottom).astype(BF16)
    for copy in copy_all([(pay.at[chip ^ k], outs[k]) for k in range(heads)], sems):
        copy.wait()


def key_side(width, heads, rows, slot, tokens, scale, *refs):
    count = heads * width
    ins = refs[: count]
    grad_ref, copy_ref, nat_ref = refs[count : count + 3]
    buf, wbuf, natural, gates, hidden, target, sems = refs[count + 3 :]
    chip, core = chip_core(width)
    pairs = []
    for other in range(width):
        for k in range(heads):
            source = (chip ^ k) * width + (core ^ other)
            src = ins[other * heads + k]
            if other == 0:
                pairs.append((src, buf.at[source]))
            else:
                pairs.append((src.at[pl.ds(5 * tokens, 8 * slot)], buf.at[source, pl.ds(5 * tokens, 8 * slot)]))
    for copy in copy_all(pairs, sems):
        copy.wait()
    wide = 3 * LANES
    width_of = rows * count
    low = low_lanes(rows)
    for source in range(count):
        wbuf[...] = buf[source, 5 * tokens :].astype(F32)
        at = source * rows
        for m in range(2):
            for t in range(2):
                natural[at : at + rows, m * wide + t * LANES : m * wide + (t + 1) * LANES] = wbuf[
                    (2 * m + t) * slot : (2 * m + t) * slot + rows
                ]
        for t in range(2):
            natural[at : at + rows, 2 * wide + (t + 1) * LANES : 2 * wide + (t + 2) * LANES] = wbuf[
                (4 + t) * slot : (4 + t) * slot + rows
            ]
        both = wbuf[6 * slot : 6 * slot + rows]
        natural[at : at + rows, 2 * LANES : 3 * LANES] = jnp.where(low, both, 0.0)
        natural[at : at + rows, 2 * wide : 2 * wide + LANES] = jnp.where(low, 0.0, both)
        natural[at : at + rows, wide + 2 * LANES : wide + 3 * LANES] = wbuf[7 * slot : 7 * slot + rows]
    nat_ref[...] = natural[...].astype(BF16)
    odd = lax.rem(chip, 2)
    copy_ref[0 : 2 * LANES] = natural[pl.ds(pl.multiple_of(odd * HALF, HALF), 2 * LANES)].astype(BF16)
    copy_ref[2 * LANES : 2 * LANES + HALF] = natural[
        pl.ds(pl.multiple_of((1 - odd) * 2 * LANES, HALF), HALF)
    ].astype(BF16)
    copy_ref[width_of:] = jnp.zeros((copy_ref.shape[0] - width_of, copy_ref.shape[1]), BF16)

    steps = [
        jnp.sum(buf[j * width + core, 5 * tokens : 5 * tokens + slot].astype(F32)[rows : rows + 3], axis=0, keepdims=True)
        for j in range(heads)
    ]
    steps = jnp.concatenate(steps, axis=0).T
    w13 = copy_ref[:, 0 : 2 * wide]
    w2 = copy_ref[:, 2 * wide :]
    for j in range(heads):
        block = buf[j * width + core, 0 : 5 * tokens]
        keys = jnp.concatenate([block[0:tokens], block[tokens : 2 * tokens], block[2 * tokens : 3 * tokens]], axis=1)
        values = jnp.concatenate(
            [block[2 * tokens : 3 * tokens], block[3 * tokens : 4 * tokens], block[4 * tokens :]], axis=1
        )
        at = j * tokens
        tgt = (-steps[:, j : j + 1] * values.astype(F32)).astype(BF16)
        both = dot(keys, w13, ((1,), (0,))) * scale
        back = dot(tgt, w2, ((1,), (1,))) * scale
        gate, up = both[:, :wide], both[:, wide:]
        sig = 1.0 / (1.0 + jnp.exp(-gate))
        silu = gate * sig
        gates[at : at + tokens, 0:wide] = (back * up * (sig * (1.0 + gate * (1.0 - sig)))).astype(BF16)
        gates[at : at + tokens, wide:] = (back * silu).astype(BF16)
        hidden[at : at + tokens] = (silu * up).astype(BF16)
        target[at : at + tokens] = tgt
    all_keys = jnp.concatenate(
        [
            jnp.concatenate([buf[j * width + core, t * tokens : (t + 1) * tokens] for t in range(3)], axis=1)
            for j in range(heads)
        ],
        axis=0,
    )
    grads13 = dot(all_keys, gates[...], ((0,), (0,))) * scale
    grads2 = dot(hidden[...], target[...], ((0,), (0,))) * scale
    first_row = pl.multiple_of(odd * HALF, HALF)
    last_row = pl.multiple_of((1 - odd) * 2 * LANES, HALF)
    grad_ref[pl.ds(first_row, 2 * LANES), 0 : 2 * wide] = grads13[0 : 2 * LANES]
    grad_ref[pl.ds(last_row, HALF), 0 : 2 * wide] = grads13[2 * LANES : 2 * LANES + HALF]
    grad_ref[pl.ds(first_row, 2 * LANES), 2 * wide :] = grads2[0 : 2 * LANES]
    grad_ref[pl.ds(last_row, HALF), 2 * wide :] = grads2[2 * LANES : 2 * LANES + HALF]


def query_side(width, heads, tokens, scale, span, *refs):
    count = heads * width
    kv = refs[:count]
    qs = refs[count : count + heads]
    copy_ref, fast_gain_ref, window_gain_ref = refs[count + heads : count + heads + 3]
    outs = refs[count + heads + 3 : count + 2 * heads + 3]
    buf, qbuf, pay, sems, out_sems = refs[count + 2 * heads + 3 :]
    chip, core = chip_core(width)
    pairs = []
    for other in range(width):
        for k in range(heads):
            source = (chip ^ k) * width + (core ^ other)
            pairs.append((kv[other * heads + k].at[pl.ds(0, 5 * tokens)], buf.at[source]))
    for k in range(heads):
        pairs.append((qs[k], qbuf.at[chip ^ k]))
    for copy in copy_all(pairs, sems):
        copy.wait()
    wide = 3 * LANES
    mid = tokens // 2
    low = low_lanes(mid)
    high = jnp.logical_not(low_lanes(tokens))
    size = heads * 40
    w13 = copy_ref[:, 0 : 2 * wide]
    w2 = copy_ref[:, 2 * wide :]
    fast_gain = fast_gain_ref[...]
    window_gain = window_gain_ref[...]
    keys_seen = (span + 1) * tokens
    ahead = lax.broadcasted_iota(jnp.int32, (tokens, keys_seen), 0) - lax.broadcasted_iota(
        jnp.int32, (tokens, keys_seen), 1
    )
    for j in range(heads):
        place = j * width + core
        start = jnp.maximum(place - span, 0)
        q_tail = qbuf[j, 2 * tokens :].astype(F32)
        q_half = jnp.concatenate([jnp.where(low, q_tail, 0.0), jnp.where(low, turned(q_tail), 0.0)], axis=0)
        q = jnp.concatenate([qbuf[j, 0:tokens], qbuf[j, tokens : 2 * tokens], q_half.astype(BF16)], axis=1)
        seen = buf[pl.ds(start, span + 1)]
        tiles = [seen[:, t * tokens : (t + 1) * tokens].reshape(keys_seen, LANES) for t in range(5)]
        score = dot(q, jnp.concatenate(tiles[0:3], axis=1), ((1,), (1,)))
        distance = ahead + (place - start) * tokens
        score = jnp.where((distance >= 0) & (distance < span * tokens), score, -jnp.inf)
        top = jnp.max(score, axis=1, keepdims=True)
        weight = jnp.exp2((score - top) * (scale * math.log2(math.e)))
        total = jnp.sum(weight, axis=1, keepdims=True)
        attended = dot(weight.astype(BF16), jnp.concatenate(tiles[2:5], axis=1), ((1,), (0,))) / total
        attended = jnp.concatenate([jnp.where(high, attended[:, 0:LANES], 0.0), attended[:, LANES:]], axis=1)
        mean_sq = jnp.sum(attended * attended, axis=1, keepdims=True) * (1.0 / size)
        window_part = attended * lax.rsqrt(mean_sq + 1e-05) * window_gain

        both = dot(q, w13, ((1,), (0,))) * scale
        gate, up = both[:, :wide], both[:, wide:]
        hid = (gate / (1.0 + jnp.exp(-gate)) * up).astype(BF16)
        out = dot(hid, w2, ((1,), (0,))) * scale
        mean_sq = jnp.sum(out * out, axis=1, keepdims=True) * (1.0 / size)
        layer = out * lax.rsqrt(mean_sq + 1e-05) * fast_gain + window_part
        pay[j, 0:tokens] = layer[:, LANES : 2 * LANES].astype(BF16)
        pay[j, tokens : 2 * tokens] = layer[:, 2 * LANES :].astype(BF16)
        pay[j, 2 * tokens :] = jnp.where(low, turned(layer[mid:, 0:LANES]), layer[0:mid, 0:LANES]).astype(BF16)
    for copy in copy_all([(pay.at[chip ^ k], outs[k]) for k in range(heads)], out_sems):
        copy.wait()


def pack_momentum(width, heads, rows, slot, mine_ref, *refs):
    others = refs[: width - 1]
    nat_ref = refs[width - 1]
    outs = refs[width : width + heads]
    total, scales, pieces, wbuf, pay, sems = refs[width + heads :]
    chip, core = chip_core(width)
    summed = mine_ref[...]
    for other in others:
        summed = summed + other[...]
    summed = summed.astype(BF16).astype(F32)
    total[...] = summed
    old = nat_ref[...].astype(F32)
    moved = old - summed
    ratio = (jnp.sum(old * old, axis=0, keepdims=True) + 1e-06) / (jnp.sum(moved * moved, axis=0, keepdims=True) + 1e-06)
    ratio = jnp.sqrt(ratio)
    high = ratio.astype(BF16).astype(F32)
    scales[0:1] = high
    scales[1:2] = ratio - high
    wide = 3 * LANES
    low = low_lanes(rows)
    low_1 = low_lanes(2)
    for source in range(heads * width):
        pieces[source, 0:rows] = total[source * rows : (source + 1) * rows]
    wbuf[...] = jnp.zeros_like(wbuf)
    for head in range(heads):
        source = head * width + core
        for m in range(3):
            for t in range(2):
                lane = m * wide + t * LANES + (LANES if m == 2 else 0)
                at = (2 * m + t) * slot
                wbuf[at : at + rows] = pieces[source, 0:rows, lane : lane + LANES]
                wbuf[at + rows : at + rows + 2] = scales[0:2, lane : lane + LANES]
        at = 6 * slot
        wbuf[at : at + rows] = jnp.where(
            low, pieces[source, 0:rows, 2 * LANES : 3 * LANES], pieces[source, 0:rows, 2 * wide : 2 * wide + LANES]
        )
        wbuf[at + rows : at + rows + 2] = jnp.where(
            low_1, scales[0:2, 2 * LANES : 3 * LANES], scales[0:2, 2 * wide : 2 * wide + LANES]
        )
        at = 7 * slot
        wbuf[at : at + rows] = pieces[source, 0:rows, wide + 2 * LANES : wide + 3 * LANES]
        wbuf[at + rows : at + rows + 2] = scales[0:2, wide + 2 * LANES : wide + 3 * LANES]
        pay[head] = wbuf[...].astype(BF16)
    for copy in copy_all([(pay.at[chip ^ k], outs[k]) for k in range(heads)], sems):
        copy.wait()


def unpack(width, heads, rows, slot, tokens, *refs):
    layers = refs[:heads]
    moments = refs[heads : 2 * heads]
    fw_ref, layer_ref, new_ref, momentum_ref, lbuf, mbuf, wbuf, sems = refs[2 * heads :]
    chip, _ = chip_core(width)
    pairs = [(layers[k], lbuf.at[chip ^ k]) for k in range(heads)]
    pairs += [(moments[k], mbuf.at[chip ^ k]) for k in range(heads)]
    for copy in copy_all(pairs, sems):
        copy.wait()
    mid = tokens // 2
    low = low_lanes(mid)
    low_r = low_lanes(slot)
    matrix = fw_ref.shape[1] // 3

    def write(lane, block):
        moment = block[0:rows]
        factor = block[rows : rows + 1] + block[rows + 1 : rows + 2]
        momentum_ref[:, lane : lane + LANES] = moment
        new_ref[:, lane : lane + LANES] = (fw_ref[:, lane : lane + LANES] - moment) * factor

    for head in range(heads):
        whole, half = tiles_of(head)
        layer_ref[:, whole : whole + LANES] = lbuf[head, 0:tokens]
        layer_ref[:, whole + LANES : whole + 2 * LANES] = lbuf[head, tokens : 2 * tokens]
        wbuf[head] = mbuf[head].astype(F32)
        for m in range(3):
            for t in range(2):
                write(m * matrix + whole + t * LANES, wbuf[head, (2 * m + t) * slot : (2 * m + t + 1) * slot])
    for head in range(0, heads, 2):
        _, half = tiles_of(head)
        even = lbuf[head, 2 * tokens :].astype(F32)
        odd = lbuf[head + 1, 2 * tokens :].astype(F32)
        layer_ref[0:mid, half : half + LANES] = jnp.where(low, turned(even), odd).astype(BF16)
        layer_ref[mid:, half : half + LANES] = jnp.where(low, even, turned(odd)).astype(BF16)
        even = wbuf[head, 6 * slot : 7 * slot]
        odd = wbuf[head + 1, 6 * slot : 7 * slot]
        write(half, jnp.where(low_r, even, turned(odd)))
        write(2 * matrix + half, jnp.where(low_r, turned(even), odd))
        even = wbuf[head, 7 * slot :]
        odd = wbuf[head + 1, 7 * slot :]
        write(matrix + half, jnp.where(low_r, even, turned(odd)))


def shards(queries, key_vectors, value_vectors, step_sizes, fast_weights, fast_gain, window_gain):
    tokens = queries.shape[0]
    heads = step_sizes.shape[1]
    head_width = queries.shape[1] // heads
    scale = 1.0 / math.sqrt(head_width)
    count = lax.axis_size("seq")
    width = count // heads
    rows = fast_weights.shape[0]
    slot = -(-(rows + 3) // 8) * 8
    span = WINDOW // tokens
    wide = 3 * LANES
    params = pltpu.CompilerParams(vmem_limit_bytes=VMEM_LIMIT)
    sem = pltpu.SemaphoreType.DMA
    key_rows = 5 * tokens + 8 * slot
    query_rows = 2 * tokens + tokens // 2

    def across(value, step):
        return lax.ppermute(value, "seq", [(i, i ^ step) for i in range(count)])

    def exchange(pieces):
        got = {0: pieces[0]}
        for k in ORDER:
            got[k] = across(pieces[k], k * width)
        return [got[k] for k in range(heads)]

    def packed(size):
        return [jax.ShapeDtypeStruct((size, LANES), BF16)] * heads

    key_pieces = pl.pallas_call(
        functools.partial(pack_keys, width, heads, rows, slot),
        out_shape=packed(key_rows),
        in_specs=[VMEM] * 4,
        out_specs=[ANY] * heads,
        scratch_shapes=[
            pltpu.VMEM((heads, key_rows, LANES), BF16),
            pltpu.VMEM((8 * slot, LANES), F32),
            sem((heads,)),
        ],
        compiler_params=params,
        name="pack_keys",
    )(key_vectors, value_vectors, step_sizes, fast_weights)
    query_pieces = pl.pallas_call(
        functools.partial(pack_queries, width, heads),
        out_shape=packed(query_rows),
        in_specs=[VMEM],
        out_specs=[ANY] * heads,
        scratch_shapes=[pltpu.VMEM((heads, query_rows, LANES), BF16), sem((heads,))],
        compiler_params=params,
        name="pack_queries",
    )(queries)
    key_blocks = exchange(key_pieces)
    for other in range(1, width):
        key_blocks = key_blocks + [across(key_blocks[k], other) for k in range(heads)]
    query_blocks = exchange(query_pieces)

    gradient, copies, natural = pl.pallas_call(
        functools.partial(key_side, width, heads, rows, slot, tokens, scale),
        out_shape=[
            jax.ShapeDtypeStruct((head_width, 3 * wide), F32),
            jax.ShapeDtypeStruct((wide, 3 * wide), BF16),
            jax.ShapeDtypeStruct((head_width, 3 * wide), BF16),
        ],
        in_specs=[ANY] * count,
        out_specs=[VMEM] * 3,
        scratch_shapes=[
            pltpu.VMEM((count, key_rows, LANES), BF16),
            pltpu.VMEM((8 * slot, LANES), F32),
            pltpu.VMEM((head_width, 3 * wide), F32),
            pltpu.VMEM((heads * tokens, 2 * wide), BF16),
            pltpu.VMEM((heads * tokens, wide), BF16),
            pltpu.VMEM((heads * tokens, wide), BF16),
            sem((count,)),
        ],
        compiler_params=params,
        name="key_side",
    )(*key_blocks)
    gradients = [across(gradient, other) for other in range(1, width)]

    head = lax.axis_index("seq") // width
    odd = head % 2

    def gain_row(gain):
        row = lax.dynamic_slice_in_dim(gain.reshape(heads, head_width), head, 1, 0)
        gap = jnp.zeros((1, HALF), F32)
        even_row = jnp.concatenate([gap, row[:, 2 * LANES :], row[:, : 2 * LANES]], axis=1)
        odd_row = jnp.concatenate([gap, row], axis=1)
        return jnp.where(odd == 1, odd_row, even_row)

    layer_pieces = pl.pallas_call(
        functools.partial(query_side, width, heads, tokens, scale, span),
        out_shape=packed(query_rows),
        in_specs=[ANY] * (count + heads) + [VMEM] * 3,
        out_specs=[ANY] * heads,
        scratch_shapes=[
            pltpu.VMEM((count, 5 * tokens, LANES), BF16),
            pltpu.VMEM((heads, query_rows, LANES), BF16),
            pltpu.VMEM((heads, query_rows, LANES), BF16),
            sem((count + heads,)),
            sem((heads,)),
        ],
        compiler_params=params,
        name="query_side",
    )(*key_blocks, *query_blocks, copies, gain_row(fast_gain), gain_row(window_gain))

    momentum_pieces = pl.pallas_call(
        functools.partial(pack_momentum, width, heads, rows, slot),
        out_shape=packed(8 * slot),
        in_specs=[VMEM] * (width + 1),
        out_specs=[ANY] * heads,
        scratch_shapes=[
            pltpu.VMEM((head_width, 3 * wide), F32),
            pltpu.VMEM((8, 3 * wide), F32),
            pltpu.VMEM((count, slot, 3 * wide), F32),
            pltpu.VMEM((8 * slot, LANES), F32),
            pltpu.VMEM((heads, 8 * slot, LANES), BF16),
            sem((heads,)),
        ],
        compiler_params=params,
        name="pack_momentum",
    )(gradient, *gradients, natural)
    moments = exchange(momentum_pieces)
    layers = exchange(layer_pieces)

    layer_out, new_weights, momentum = pl.pallas_call(
        functools.partial(unpack, width, heads, rows, slot, tokens),
        out_shape=[
            jax.ShapeDtypeStruct(queries.shape, BF16),
            jax.ShapeDtypeStruct(fast_weights.shape, F32),
            jax.ShapeDtypeStruct(fast_weights.shape, F32),
        ],
        in_specs=[ANY] * (2 * heads) + [VMEM],
        out_specs=[VMEM] * 3,
        scratch_shapes=[
            pltpu.VMEM((heads, query_rows, LANES), BF16),
            pltpu.VMEM((heads, 8 * slot, LANES), BF16),
            pltpu.VMEM((heads, 8 * slot, LANES), F32),
            sem((2 * heads,)),
        ],
        compiler_params=params,
        name="unpack",
    )(*layers, *moments, fast_weights)
    return (layer_out, new_weights, momentum)


def solution(mesh):
    in_specs = (
        P(("groups", "seq"), None),
        P(("groups", "seq"), None),
        P(("groups", "seq"), None),
        P(("groups", "seq"), None),
        P("seq", None),
        P(),
        P(),
    )
    out_specs = (P(("groups", "seq"), None), P(("groups", "seq"), None), P(("groups", "seq"), None))
    return jax.shard_map(shards, mesh=mesh, in_specs=in_specs, out_specs=out_specs, check_vma=False)
```

time: 504 us -> 149 us (0.30)
  blocking collectives: 213 us -> 0 us
  starting transfers between devices: 139 us -> 57.3 us
  local copies, waits for them, and re-layouts: 95.2 us -> 17.5 us
  waiting for transfers between devices: 3.01 us -> 40.6 us
  Pallas kernels: 0 us -> 31.5 us
  matrix products: 22.1 us -> 0 us
  other arithmetic: 14.2 us -> 0.07 us
  between operations: 15.1 us -> 1.07 us
    unnamed x1 -> x0, blocking collectives: 139 us -> none
    psum x1 -> x0, blocking collectives: 74 us -> none  [shards(): lax.psum((jnp.sum(fast_weights * fast_weights, axis=0), jnp.sum(moved * m...]
    ppermute x16 -> x37, starting transfers between devices: 103 us -> 57.3 us  [across(): return lax.ppermute(value, 'seq', [(i, i ^ step) for i in range(count)])]
    ppermute x16 -> x37, waiting for transfers between devices: 0.04 us -> 40.6 us  [across(): return lax.ppermute(value, 'seq', [(i, i ^ step) for i in range(count)])]
    unnamed x3 -> x0, starting transfers between devices: 36 us -> none
    unnamed x84 -> x71, local copies, waits for them, and re-layouts: 49.1 us -> 17.2 us
    pallas_call x0 -> x6, Pallas kernels: none -> 31.5 us  [the longest x1 15.5 us: shards(): pl.pallas_call(functools.partial(query_side, width, heads, tokens, scale,...]
    dot_general x10 -> x0, matrix products: 22.1 us -> none  [the longest x4 7.34 us: project(): jnp.einsum('thr,rhc->thc', inputs, matrix, preferred_element_type=jnp.flo...]
  transfers between devices with their start and end apart: 20 -> 37, of which waited for: 1 -> 15; matrix products, arithmetic and copies ran while one was open for 14% -> 0% of each run, Pallas kernels for 0% -> 12%
where the time goes in v1:
time: 149 us; the launch traced here: 148 us
  starting transfers between devices  57.3 us (38%)
  waiting for transfers between devices  40.6 us (27%)
  Pallas kernels  31.5 us (21%)
  local copies, waits for them, and re-layouts  17.5 us (12%)
    ppermute x37, starting transfers between devices, across(): return lax.ppermute(value, 'seq', [(i, i ^ step) for i in range(count)])  57.3 us
    ppermute x37, waiting for transfers between devices, across(): return lax.ppermute(value, 'seq', [(i, i ^ step) for i in range(count)])  40.6 us
    unnamed x71, local copies, waits for them, and re-layouts  17.2 us
    pallas_call x1, Pallas kernels, shards(): pl.pallas_call(functools.partial(query_side, width, heads, tokens, scale,...  15.5 us
    pallas_call x1, Pallas kernels, shards(): pl.pallas_call(functools.partial(key_side, width, heads, rows, slot, toke...  7.94 us
    pallas_call x1, Pallas kernels, shards(): pl.pallas_call(functools.partial(unpack, width, heads, rows, slot, tokens...  3.18 us
  transfers between devices with their start and end apart: 37, of which 15 were waited for; matrix products, arithmetic and copies ran while one was open for 0% of the time, Pallas kernels for 12%

profile of v1, /device:TPU:0, one launch (start us, length us, event | category | flops | bytes accessed | tf_op | source)
XLA Modules:
  0.0 148.1 jit_solution(9690252121969880855)
XLA Ops:
  1.4 1.1 copy-done
  2.5 1.1 copy-done.27
  3.6 1.1 copy-done.28
  4.7 2.6 %pack_keys.1 = (bf16[832,128]{1,0:T(8,128)(2,1)S(1)}, bf16[832,128]{1,0:T(8,128)(2,1)S(1)}, bf16[832,128]{1,0:T(8,128)(2,1)S(1)}, bf16[832,128]{1,0:T(8,128)(2,1...) custom-call(bf16[128,2560]{1,0:T(8,128)(2,1)S(1)} %copy-done.27, ...), custom_call_target="tpu_custom_call" | custom-call | tf_op jit(solution)/shard_map/pack_keys/pallas_call | solution.py:384
  7.4 3.0 %collective-permute-start = (bf16[832,128]{1,0:T(8,128)(2,1)S(1)}, bf16[832,128]{1,0:T(8,128)(2,1)S(1)}, u32[]{:S(2)}, u32[]{:S(2)}) collective-permute-start(bf16[832,128]{1,0:T(8,128)(2,1)S(1)} %get-tuple-element.39), channel_id=1, source_target_pairs={{0,2},{1,3},{2,0},{3,1},{4,6},{5,7},{6,4},{7,5},{8,10},{9,11},{10,... | collective-permute-start | bytes 638984 | tf_op jit(solution)/shard_map/ppermute | solution.py:373
  10.4 1.6 %collective-permute-start.1 = (bf16[832,128]{1,0:T(8,128)(2,1)S(1)}, bf16[832,128]{1,0:T(8,128)(2,1)S(1)}, u32[]{:S(2)}, u32[]{:S(2)}) collective-permute-start(bf16[832,128]{1,0:T(8,128)(2,1)S(1)} %get-tuple-element.40), channel_id=1, source_target_pairs={{0,4},{1,5},{2,6},{3,7},{4,0},{5,1},{6,2},{7,3},{8,12},{9,13},{10,... | collective-permute-start | bytes 638984 | tf_op jit(solution)/shard_map/ppermute | solution.py:373
  12.0 3.0 %collective-permute-start.3 = (bf16[832,128]{1,0:T(8,128)(2,1)S(1)}, bf16[832,128]{1,0:T(8,128)(2,1)S(1)}, u32[]{:S(2)}, u32[]{:S(2)}) collective-permute-start(bf16[832,128]{1,0:T(8,128)(2,1)S(1)} %get-tuple-element.42), channel_id=1, source_target_pairs={{0,8},{1,9},{2,10},{3,11},{4,12},{5,13},{6,14},{7,15},{8,0},{9,1},... | collective-permute-start | bytes 638984 | tf_op jit(solution)/shard_map/ppermute | solution.py:373
  15.0 1.3 collective-permute-start.4
  16.2 3.6 %collective-permute-start.5 = (bf16[832,128]{1,0:T(8,128)(2,1)S(1)}, bf16[832,128]{1,0:T(8,128)(2,1)S(1)}, u32[]{:S(2)}, u32[]{:S(2)}) collective-permute-start(bf16[832,128]{1,0:T(8,128)(2,1)S(1)} %get-tuple-element.44), channel_id=1, source_target_pairs={{0,12},{1,13},{2,14},{3,15},{4,8},{5,9},{6,10},{7,11},{8,4},{9,5},... | collective-permute-start | bytes 638984 | tf_op jit(solution)/shard_map/ppermute | solution.py:373
  19.8 7.1 %collective-permute-done.1.refs_2_ = bf16[832,128]{1,0:T(8,128)(2,1)S(1)} collective-permute-done((bf16[832,128]{1,0:T(8,128)(2,1)S(1)}, bf16[832,128]{1,0:T(8,128)(2,1)S(1)}, u32[]{:S(2)}, u32[]{:S(2)}) %collective-permute-start.1) | collective-permute-done | bytes 213024 | tf_op jit(solution)/shard_map/ppermute | solution.py:373
  27.7 1.2 collective-permute-done.2.refs_3_
  29.5 15.7 %collective-permute-done.4.refs_5_ = bf16[832,128]{1,0:T(8,128)(2,1)S(1)} collective-permute-done((bf16[832,128]{1,0:T(8,128)(2,1)S(1)}, bf16[832,128]{1,0:T(8,128)(2,1)S(1)}, u32[]{:S(2)}, u32[]{:S(2)}) %collective-permute-start.4) | collective-permute-done | bytes 213024 | tf_op jit(solution)/shard_map/ppermute | solution.py:373
  48.2 7.9 %key_side.1 = (f32[320,1152]{1,0:T(8,128)}, bf16[384,1152]{1,0:T(8,128)(2,1)S(1)}, bf16[320,1152]{1,0:T(8,128)(2,1)S(1)}) custom-call(bf16[832,128]{1,0:T(8,128)(2,1)S(1)} %get-tuple-element.38.refs_0_, bf16[832,128]{1,0:T(8,128)(2,1)S(1)} %collective-permute-done.refs_1_, bf16[832,128]{1,0:T(8,128)(2,1)S(1)} %collective-permute-done.1.refs_2_, ...), custom_call_target="tpu_custom_call" | custom-call | tf_op jit(solution)/shard_map/key_side/pallas_call | solution.py:411
  57.4 1.0 pack_queries.1
  60.3 7.9 %collective-permute-start.16 = (bf16[320,128]{1,0:T(8,128)(2,1)}, bf16[320,128]{1,0:T(8,128)(2,1)}, u32[]{:S(2)}, u32[]{:S(2)}) collective-permute-start(bf16[320,128]{1,0:T(8,128)(2,1)} %get-tuple-element.48), channel_id=1, source_target_pairs={{0,4},{1,5},{2,6},{3,7},{4,0},{5,1},{6,2},{7,3},{8,12},{9,13},{10,... | collective-permute-start | bytes 245768 | tf_op jit(solution)/shard_map/ppermute | solution.py:373
  68.9 4.2 %collective-permute-start.18 = (bf16[320,128]{1,0:T(8,128)(2,1)}, bf16[320,128]{1,0:T(8,128)(2,1)}, u32[]{:S(2)}, u32[]{:S(2)}) collective-permute-start(bf16[320,128]{1,0:T(8,128)(2,1)} %get-tuple-element.50), channel_id=1, source_target_pairs={{0,8},{1,9},{2,10},{3,11},{4,12},{5,13},{6,14},{7,15},{8,0},{9,1},... | collective-permute-start | bytes 245768 | tf_op jit(solution)/shard_map/ppermute | solution.py:373
  73.4 1.1 collective-permute-start.19
  74.5 1.4 collective-permute-start.20
  75.8 3.4 %collective-permute-start.21 = (bf16[320,128]{1,0:T(8,128)(2,1)}, bf16[320,128]{1,0:T(8,128)(2,1)S(1)}, u32[]{:S(2)}, u32[]{:S(2)}) collective-permute-start(bf16[320,128]{1,0:T(8,128)(2,1)} %copy-done.30), channel_id=1, source_target_pairs={{0,14},{1,15},{2,12},{3,13},{4,10},{5,11},{6,8},{7,9},{8,6},{9,7},... | collective-permute-start | bytes 245768 | tf_op jit(solution)/shard_map/ppermute | solution.py:373
  79.3 6.4 %collective-permute-done.19.refs_21_ = bf16[320,128]{1,0:T(8,128)(2,1)S(1)} collective-permute-done((bf16[320,128]{1,0:T(8,128)(2,1)}, bf16[320,128]{1,0:T(8,128)(2,1)S(1)}, u32[]{:S(2)}, u32[]{:S(2)}) %collective-permute-start.19) | collective-permute-done | bytes 81952 | tf_op jit(solution)/shard_map/ppermute | solution.py:373
  85.7 0.9 copy-done.4
  86.7 0.9 copy-done.6
  87.6 0.9 copy-done.8
  88.5 0.9 copy-done.10
  89.5 0.9 copy-done.12
  90.4 0.9 copy-done.14
  91.3 0.9 copy-done.16
  92.3 0.9 copy-done.18
  93.2 0.9 copy-done.20
  94.1 0.9 copy-done.22
  95.1 0.9 copy-done.24
  96.0 15.5 %query_side.1 = (bf16[320,128]{1,0:T(8,128)(2,1)S(1)}, bf16[320,128]{1,0:T(8,128)(2,1)S(1)}, bf16[320,128]{1,0:T(8,128)(2,1)S(1)}, bf16[320,128]{1,0:T(8,128)(2,...) custom-call(bf16[832,128]{1,0:T(8,128)(2,1)S(1)} %get-tuple-element., ...), custom_call_target="tpu_custom_call" | custom-call | tf_op jit(solution)/shard_map/query_side/pallas_call | solution.py:444
  112.1 3.8 %collective-permute-start.23 = (bf16[320,128]{1,0:T(8,128)(2,1)S(1)}, bf16[320,128]{1,0:T(8,128)(2,1)S(1)}, u32[]{:S(2)}, u32[]{:S(2)}) collective-permute-start(bf16[320,128]{1,0:T(8,128)(2,1)S(1)} %get-tuple-element.57), channel_id=1, source_target_pairs={{0,4},{1,5},{2,6},{3,7},{4,0},{5,1},{6,2},{7,3},{8,12},{9,13},{10,... | collective-permute-start | bytes 245768 | tf_op jit(solution)/shard_map/ppermute | solution.py:373
  116.7 2.0 %collective-permute-start.25 = (bf16[320,128]{1,0:T(8,128)(2,1)S(1)}, bf16[320,128]{1,0:T(8,128)(2,1)S(1)}, u32[]{:S(2)}, u32[]{:S(2)}) collective-permute-start(bf16[320,128]{1,0:T(8,128)(2,1)S(1)} %get-tuple-element.59), channel_id=1, source_target_pairs={{0,8},{1,9},{2,10},{3,11},{4,12},{5,13},{6,14},{7,15},{8,0},{9,1},... | collective-permute-start | bytes 245768 | tf_op jit(solution)/shard_map/ppermute | solution.py:373
  118.6 2.2 %collective-permute-start.26 = (bf16[320,128]{1,0:T(8,128)(2,1)S(1)}, bf16[320,128]{1,0:T(8,128)(2,1)S(1)}, u32[]{:S(2)}, u32[]{:S(2)}) collective-permute-start(bf16[320,128]{1,0:T(8,128)(2,1)S(1)} %get-tuple-element.60), channel_id=1, source_target_pairs={{0,10},{1,11},{2,8},{3,9},{4,14},{5,15},{6,12},{7,13},{8,2},{9,3},... | collective-permute-start | bytes 245768 | tf_op jit(solution)/shard_map/ppermute | solution.py:373
  120.8 1.2 collective-permute-start.27
  122.1 3.1 %collective-permute-start.28 = (bf16[320,128]{1,0:T(8,128)(2,1)S(1)}, bf16[320,128]{1,0:T(8,128)(2,1)S(1)}, u32[]{:S(2)}, u32[]{:S(2)}) collective-permute-start(bf16[320,128]{1,0:T(8,128)(2,1)S(1)} %get-tuple-element.62), channel_id=1, source_target_pairs={{0,14},{1,15},{2,12},{3,13},{4,10},{5,11},{6,8},{7,9},{8,6},{9,7},... | collective-permute-start | bytes 245768 | tf_op jit(solution)/shard_map/ppermute | solution.py:373
  125.2 1.3 pack_momentum.1
  126.5 1.0 collective-permute-start.30
  127.5 2.1 %collective-permute-done.25.refs_4_ = bf16[320,128]{1,0:T(8,128)(2,1)S(1)} collective-permute-done((bf16[320,128]{1,0:T(8,128)(2,1)S(1)}, bf16[320,128]{1,0:T(8,128)(2,1)S(1)}, u32[]{:S(2)}, u32[]{:S(2)}) %collective-permute-start.25) | collective-permute-done | bytes 81952 | tf_op jit(solution)/shard_map/ppermute | solution.py:373
  129.6 1.9 %collective-permute-done.26.refs_5_ = bf16[320,128]{1,0:T(8,128)(2,1)S(1)} collective-permute-done((bf16[320,128]{1,0:T(8,128)(2,1)S(1)}, bf16[320,128]{1,0:T(8,128)(2,1)S(1)}, u32[]{:S(2)}, u32[]{:S(2)}) %collective-permute-start.26) | collective-permute-done | bytes 81952 | tf_op jit(solution)/shard_map/ppermute | solution.py:373
  131.8 2.0 %collective-permute-start.33 = (bf16[192,128]{1,0:T(8,128)(2,1)S(1)}, bf16[192,128]{1,0:T(8,128)(2,1)S(1)}, u32[]{:S(2)}, u32[]{:S(2)}) collective-permute-start(bf16[192,128]{1,0:T(8,128)(2,1)S(1)} %get-tuple-element.69), channel_id=1, source_target_pairs={{0,8},{1,9},{2,10},{3,11},{4,12},{5,13},{6,14},{7,15},{8,0},{9,1},... | collective-permute-start | bytes 147464 | tf_op jit(solution)/shard_map/ppermute | solution.py:373
  133.8 2.0 %collective-permute-start.34 = (bf16[192,128]{1,0:T(8,128)(2,1)S(1)}, bf16[192,128]{1,0:T(8,128)(2,1)S(1)}, u32[]{:S(2)}, u32[]{:S(2)}) collective-permute-start(bf16[192,128]{1,0:T(8,128)(2,1)S(1)} %get-tuple-element.70), channel_id=1, source_target_pairs={{0,10},{1,11},{2,8},{3,9},{4,14},{5,15},{6,12},{7,13},{8,2},{9,3},... | collective-permute-start | bytes 147464 | tf_op jit(solution)/shard_map/ppermute | solution.py:373
  135.9 2.1 %collective-permute-start.35 = (bf16[192,128]{1,0:T(8,128)(2,1)S(1)}, bf16[192,128]{1,0:T(8,128)(2,1)S(1)}, u32[]{:S(2)}, u32[]{:S(2)}) collective-permute-start(bf16[192,128]{1,0:T(8,128)(2,1)S(1)} %get-tuple-element.71), channel_id=1, source_target_pairs={{0,12},{1,13},{2,14},{3,15},{4,8},{5,9},{6,10},{7,11},{8,4},{9,5},... | collective-permute-start | bytes 147464 | tf_op jit(solution)/shard_map/ppermute | solution.py:373
  138.0 2.4 %collective-permute-start.36 = (bf16[192,128]{1,0:T(8,128)(2,1)S(1)}, bf16[192,128]{1,0:T(8,128)(2,1)S(1)}, u32[]{:S(2)}, u32[]{:S(2)}) collective-permute-start(bf16[192,128]{1,0:T(8,128)(2,1)S(1)} %get-tuple-element.72), channel_id=1, source_target_pairs={{0,14},{1,15},{2,12},{3,13},{4,10},{5,11},{6,8},{7,9},{8,6},{9,7},... | collective-permute-start | bytes 147464 | tf_op jit(solution)/shard_map/ppermute | solution.py:373
  140.4 1.2 collective-permute-done.34.refs_13_
  141.9 2.9 %collective-permute-done.36.refs_15_ = bf16[192,128]{1,0:T(8,128)(2,1)S(1)} collective-permute-done((bf16[192,128]{1,0:T(8,128)(2,1)S(1)}, bf16[192,128]{1,0:T(8,128)(2,1)S(1)}, u32[]{:S(2)}, u32[]{:S(2)}) %collective-permute-start.36) | collective-permute-done | bytes 49184 | tf_op jit(solution)/shard_map/ppermute | solution.py:373
  144.8 3.2 %unpack.1 = (bf16[128,2560]{1,0:T(8,128)(2,1)}, f32[20,7680]{1,0:T(8,128)}, f32[20,7680]{1,0:T(8,128)}) custom-call(bf16[320,128]{1,0:T(8,128)(2,1)S(1)} %get-tuple-element.55.refs_0_, bf16[320,128]{1,0:T(8,128)(2,1)S(1)} %collective-permute-done.22.refs_1_, bf16[320,128]{1,0:T(8,128)(2,1)S(1)} %collective-permute-done.23.refs_2_, ...), custom_call_target="tpu_custom_call" | custom-call | tf_op jit(solution)/shard_map/unpack/pallas_call | solution.py:479
  (112 shorter events, 11.2 us)
Async XLA Ops:
  7.4 8.9 %collective-permute-start = (bf16[832,128]{1,0:T(8,128)(2,1)S(1)}, bf16[832,128]{1,0:T(8,128)(2,1)S(1)}, u32[]{:S(2)}, u32[]{:S(2)}) collective-permute-start(bf16[832,128]{1,0:T(8,128)(2,1)S(1)} %get-tuple-element.39), channel_id=1, source_target_pairs={{0,2},{1,3},{2,0},{3,1},{4,6},{5,7},{6,4},{7,5},{8,10},{9,11},{10,... | collective-permute-start | bytes 638984 | tf_op jit(solution)/shard_map/ppermute | solution.py:373
  10.4 16.6 %collective-permute-start.1 = (bf16[832,128]{1,0:T(8,128)(2,1)S(1)}, bf16[832,128]{1,0:T(8,128)(2,1)S(1)}, u32[]{:S(2)}, u32[]{:S(2)}) collective-permute-start(bf16[832,128]{1,0:T(8,128)(2,1)S(1)} %get-tuple-element.40), channel_id=1, source_target_pairs={{0,4},{1,5},{2,6},{3,7},{4,0},{5,1},{6,2},{7,3},{8,12},{9,13},{10,... | collective-permute-start | bytes 638984 | tf_op jit(solution)/shard_map/ppermute | solution.py:373
  12.0 17.0 %collective-permute-start.2 = (bf16[832,128]{1,0:T(8,128)(2,1)S(1)}, bf16[832,128]{1,0:T(8,128)(2,1)S(1)}, u32[]{:S(2)}, u32[]{:S(2)}) collective-permute-start(bf16[832,128]{1,0:T(8,128)(2,1)S(1)} %get-tuple-element.41), channel_id=1, source_target_pairs={{0,6},{1,7},{2,4},{3,5},{4,2},{5,3},{6,0},{7,1},{8,14},{9,15},{10,... | collective-permute-start | bytes 638984 | tf_op jit(solution)/shard_map/ppermute | solution.py:373
  12.0 17.0 %collective-permute-start.3 = (bf16[832,128]{1,0:T(8,128)(2,1)S(1)}, bf16[832,128]{1,0:T(8,128)(2,1)S(1)}, u32[]{:S(2)}, u32[]{:S(2)}) collective-permute-start(bf16[832,128]{1,0:T(8,128)(2,1)S(1)} %get-tuple-element.42), channel_id=1, source_target_pairs={{0,8},{1,9},{2,10},{3,11},{4,12},{5,13},{6,14},{7,15},{8,0},{9,1},... | collective-permute-start | bytes 638984 | tf_op jit(solution)/shard_map/ppermute | solution.py:373
  15.0 30.3 %collective-permute-start.4 = (bf16[832,128]{1,0:T(8,128)(2,1)S(1)}, bf16[832,128]{1,0:T(8,128)(2,1)S(1)}, u32[]{:S(2)}, u32[]{:S(2)}) collective-permute-start(bf16[832,128]{1,0:T(8,128)(2,1)S(1)} %get-tuple-element.43), channel_id=1, source_target_pairs={{0,10},{1,11},{2,8},{3,9},{4,14},{5,15},{6,12},{7,13},{8,2},{9,3},... | collective-permute-start | bytes 638984 | tf_op jit(solution)/shard_map/ppermute | solution.py:373
  16.2 29.0 %collective-permute-start.5 = (bf16[832,128]{1,0:T(8,128)(2,1)S(1)}, bf16[832,128]{1,0:T(8,128)(2,1)S(1)}, u32[]{:S(2)}, u32[]{:S(2)}) collective-permute-start(bf16[832,128]{1,0:T(8,128)(2,1)S(1)} %get-tuple-element.44), channel_id=1, source_target_pairs={{0,12},{1,13},{2,14},{3,15},{4,8},{5,9},{6,10},{7,11},{8,4},{9,5},... | collective-permute-start | bytes 638984 | tf_op jit(solution)/shard_map/ppermute | solution.py:373
  27.0 18.8 %collective-permute-start.6 = (bf16[832,128]{1,0:T(8,128)(2,1)S(1)}, bf16[832,128]{1,0:T(8,128)(2,1)S(1)}, u32[]{:S(2)}, u32[]{:S(2)}) collective-permute-start(bf16[832,128]{1,0:T(8,128)(2,1)S(1)} %get-tuple-element.45), channel_id=1, source_target_pairs={{0,14},{1,15},{2,12},{3,13},{4,10},{5,11},{6,8},{7,9},{8,6},{9,7},... | collective-permute-start | bytes 638984 | tf_op jit(solution)/shard_map/ppermute | solution.py:373
  29.0 28.4 %copy-start.29 = (bf16[128,2560]{1,0:T(8,128)(2,1)S(1)}, bf16[128,2560]{1,0:T(8,128)(2,1)}, u32[]{:S(2)}) copy-start(bf16[128,2560]{1,0:T(8,128)(2,1)} %q_ref.1) | copy-start | bytes 1966084
  29.0 44.1 %copy-start.33 = (f32[2560]{0:T(1024)S(1)}, f32[2560]{0:T(1024)}, u32[]{:S(2)}) copy-start(f32[2560]{0:T(1024)} %param.12) | copy-start | bytes 30724
  29.0 44.1 %copy-start.34 = (f32[2560]{0:T(1024)S(1)}, f32[2560]{0:T(1024)}, u32[]{:S(2)}) copy-start(f32[2560]{0:T(1024)} %param.13) | copy-start | bytes 30724
  29.0 16.9 %collective-permute-start.7 = (bf16[832,128]{1,0:T(8,128)(2,1)S(1)}, bf16[832,128]{1,0:T(8,128)(2,1)S(1)}, u32[]{:S(2)}, u32[]{:S(2)}) collective-permute-start(bf16[832,128]{1,0:T(8,128)(2,1)S(1)} %get-tuple-element.38.refs_0_), channel_id=1, source_target_pairs={{0,1},{1,0},{2,3},{3,2},{4,5},{5,4},{6,7},{7,6},{8,9},{9,8},{10,11... | collective-permute-start | bytes 638984 | tf_op jit(solution)/shard_map/ppermute | solution.py:373
  29.0 17.3 %collective-permute-start.8 = (bf16[832,128]{1,0:T(8,128)(2,1)S(1)}, bf16[832,128]{1,0:T(8,128)(2,1)S(1)}, u32[]{:S(2)}, u32[]{:S(2)}) collective-permute-start(bf16[832,128]{1,0:T(8,128)(2,1)S(1)} %collective-permute-done.refs_1_), channel_id=1, source_target_pairs={{0,1},{1,0},{2,3},{3,2},{4,5},{5,4},{6,7},{7,6},{8,9},{9,8},{10,11... | collective-permute-start | bytes 638984 | tf_op jit(solution)/shard_map/ppermute | solution.py:373
  45.2 10.9 %copy-start.3 = (bf16[832,128]{1,0:T(8,128)(2,1)}, bf16[832,128]{1,0:T(8,128)(2,1)S(1)}, u32[]{:S(2)}) copy-start(bf16[832,128]{1,0:T(8,128)(2,1)S(1)} %collective-permute-done.4.refs_5_) | copy-start | bytes 638980
  45.2 1.5 collective-permute-start.9
  45.2 10.9 %copy-start.5 = (bf16[832,128]{1,0:T(8,128)(2,1)}, bf16[832,128]{1,0:T(8,128)(2,1)S(1)}, u32[]{:S(2)}) copy-start(bf16[832,128]{1,0:T(8,128)(2,1)S(1)} %collective-permute-done.5.refs_6_) | copy-start | bytes 638980
  45.3 1.7 %collective-permute-start.10 = (bf16[832,128]{1,0:T(8,128)(2,1)S(1)}, bf16[832,128]{1,0:T(8,128)(2,1)S(1)}, u32[]{:S(2)}, u32[]{:S(2)}) collective-permute-start(bf16[832,128]{1,0:T(8,128)(2,1)S(1)} %collective-permute-done.2.refs_3_), channel_id=1, source_target_pairs={{0,1},{1,0},{2,3},{3,2},{4,5},{5,4},{6,7},{7,6},{8,9},{9,8},{10,11... | collective-permute-start | bytes 638984 | tf_op jit(solution)/shard_map/ppermute | solution.py:373
  45.8 10.4 %copy-start.7 = (bf16[832,128]{1,0:T(8,128)(2,1)}, bf16[832,128]{1,0:T(8,128)(2,1)S(1)}, u32[]{:S(2)}) copy-start(bf16[832,128]{1,0:T(8,128)(2,1)S(1)} %collective-permute-done.6.refs_7_) | copy-start | bytes 638980
  45.8 1.6 %collective-permute-start.11 = (bf16[832,128]{1,0:T(8,128)(2,1)S(1)}, bf16[832,128]{1,0:T(8,128)(2,1)S(1)}, u32[]{:S(2)}, u32[]{:S(2)}) collective-permute-start(bf16[832,128]{1,0:T(8,128)(2,1)S(1)} %collective-permute-done.3.refs_4_), channel_id=1, source_target_pairs={{0,1},{1,0},{2,3},{3,2},{4,5},{5,4},{6,7},{7,6},{8,9},{9,8},{10,11... | collective-permute-start | bytes 638984 | tf_op jit(solution)/shard_map/ppermute | solution.py:373
  45.8 10.4 %copy-start.9 = (bf16[832,128]{1,0:T(8,128)(2,1)}, bf16[832,128]{1,0:T(8,128)(2,1)S(1)}, u32[]{:S(2)}) copy-start(bf16[832,128]{1,0:T(8,128)(2,1)S(1)} %collective-permute-done.7.refs_8_) | copy-start | bytes 638980
  45.8 1.8 %collective-permute-start.12 = (bf16[832,128]{1,0:T(8,128)(2,1)S(1)}, bf16[832,128]{1,0:T(8,128)(2,1)S(1)}, u32[]{:S(2)}, u32[]{:S(2)}) collective-permute-start(bf16[832,128]{1,0:T(8,128)(2,1)S(1)} %collective-permute-done.4.refs_5_), channel_id=1, source_target_pairs={{0,1},{1,0},{2,3},{3,2},{4,5},{5,4},{6,7},{7,6},{8,9},{9,8},{10,11... | collective-permute-start | bytes 638984 | tf_op jit(solution)/shard_map/ppermute | solution.py:373
  46.3 9.9 %copy-start.11 = (bf16[832,128]{1,0:T(8,128)(2,1)}, bf16[832,128]{1,0:T(8,128)(2,1)S(1)}, u32[]{:S(2)}) copy-start(bf16[832,128]{1,0:T(8,128)(2,1)S(1)} %collective-permute-done.8.refs_9_) | copy-start | bytes 638980
  46.3 1.6 %collective-permute-start.13 = (bf16[832,128]{1,0:T(8,128)(2,1)S(1)}, bf16[832,128]{1,0:T(8,128)(2,1)S(1)}, u32[]{:S(2)}, u32[]{:S(2)}) collective-permute-start(bf16[832,128]{1,0:T(8,128)(2,1)S(1)} %collective-permute-done.5.refs_6_), channel_id=1, source_target_pairs={{0,1},{1,0},{2,3},{3,2},{4,5},{5,4},{6,7},{7,6},{8,9},{9,8},{10,11... | collective-permute-start | bytes 638984 | tf_op jit(solution)/shard_map/ppermute | solution.py:373
  46.7 1.5 %collective-permute-start.14 = (bf16[832,128]{1,0:T(8,128)(2,1)S(1)}, bf16[832,128]{1,0:T(8,128)(2,1)S(1)}, u32[]{:S(2)}, u32[]{:S(2)}) collective-permute-start(bf16[832,128]{1,0:T(8,128)(2,1)S(1)} %collective-permute-done.6.refs_7_), channel_id=1, source_target_pairs={{0,1},{1,0},{2,3},{3,2},{4,5},{5,4},{6,7},{7,6},{8,9},{9,8},{10,11... | collective-permute-start | bytes 638984 | tf_op jit(solution)/shard_map/ppermute | solution.py:373
  57.1 64.9 %collective-permute-start.29 = (f32[320,1152]{1,0:T(8,128)}, f32[320,1152]{1,0:T(8,128)S(1)}, u32[]{:S(2)}, u32[]{:S(2)}) collective-permute-start(f32[320,1152]{1,0:T(8,128)} %get-tuple-element.63.mine_ref), channel_id=1, source_target_pairs={{0,1},{1,0},{2,3},{3,2},{4,5},{5,4},{6,7},{7,6},{8,9},{9,8},{10,11... | collective-permute-start | bytes 4423688 | tf_op jit(solution)/shard_map/ppermute | solution.py:373
  60.3 13.1 %collective-permute-start.15 = (bf16[320,128]{1,0:T(8,128)(2,1)}, bf16[320,128]{1,0:T(8,128)(2,1)}, u32[]{:S(2)}, u32[]{:S(2)}) collective-permute-start(bf16[320,128]{1,0:T(8,128)(2,1)} %get-tuple-element.47), channel_id=1, source_target_pairs={{0,2},{1,3},{2,0},{3,1},{4,6},{5,7},{6,4},{7,5},{8,10},{9,11},{10,... | collective-permute-start | bytes 245768 | tf_op jit(solution)/shard_map/ppermute | solution.py:373
  60.3 14.1 %collective-permute-start.16 = (bf16[320,128]{1,0:T(8,128)(2,1)}, bf16[320,128]{1,0:T(8,128)(2,1)}, u32[]{:S(2)}, u32[]{:S(2)}) collective-permute-start(bf16[320,128]{1,0:T(8,128)(2,1)} %get-tuple-element.48), channel_id=1, source_target_pairs={{0,4},{1,5},{2,6},{3,7},{4,0},{5,1},{6,2},{7,3},{8,12},{9,13},{10,... | collective-permute-start | bytes 245768 | tf_op jit(solution)/shard_map/ppermute | solution.py:373
  68.2 7.6 %collective-permute-start.17 = (bf16[320,128]{1,0:T(8,128)(2,1)}, bf16[320,128]{1,0:T(8,128)(2,1)}, u32[]{:S(2)}, u32[]{:S(2)}) collective-permute-start(bf16[320,128]{1,0:T(8,128)(2,1)} %get-tuple-element.49), channel_id=1, source_target_pairs={{0,6},{1,7},{2,4},{3,5},{4,2},{5,3},{6,0},{7,1},{8,14},{9,15},{10,... | collective-permute-start | bytes 245768 | tf_op jit(solution)/shard_map/ppermute | solution.py:373
  68.9 10.4 %collective-permute-start.18 = (bf16[320,128]{1,0:T(8,128)(2,1)}, bf16[320,128]{1,0:T(8,128)(2,1)}, u32[]{:S(2)}, u32[]{:S(2)}) collective-permute-start(bf16[320,128]{1,0:T(8,128)(2,1)} %get-tuple-element.50), channel_id=1, source_target_pairs={{0,8},{1,9},{2,10},{3,11},{4,12},{5,13},{6,14},{7,15},{8,0},{9,1},... | collective-permute-start | bytes 245768 | tf_op jit(solution)/shard_map/ppermute | solution.py:373
  73.4 12.3 %collective-permute-start.19 = (bf16[320,128]{1,0:T(8,128)(2,1)}, bf16[320,128]{1,0:T(8,128)(2,1)S(1)}, u32[]{:S(2)}, u32[]{:S(2)}) collective-permute-start(bf16[320,128]{1,0:T(8,128)(2,1)} %copy-done.32), channel_id=1, source_target_pairs={{0,10},{1,11},{2,8},{3,9},{4,14},{5,15},{6,12},{7,13},{8,2},{9,3},... | collective-permute-start | bytes 245768 | tf_op jit(solution)/shard_map/ppermute | solution.py:373
  74.5 11.3 %collective-permute-start.20 = (bf16[320,128]{1,0:T(8,128)(2,1)}, bf16[320,128]{1,0:T(8,128)(2,1)S(1)}, u32[]{:S(2)}, u32[]{:S(2)}) collective-permute-start(bf16[320,128]{1,0:T(8,128)(2,1)} %copy-done.31), channel_id=1, source_target_pairs={{0,12},{1,13},{2,14},{3,15},{4,8},{5,9},{6,10},{7,11},{8,4},{9,5},... | collective-permute-start | bytes 245768 | tf_op jit(solution)/shard_map/ppermute | solution.py:373
  75.8 9.9 %collective-permute-start.21 = (bf16[320,128]{1,0:T(8,128)(2,1)}, bf16[320,128]{1,0:T(8,128)(2,1)S(1)}, u32[]{:S(2)}, u32[]{:S(2)}) collective-permute-start(bf16[320,128]{1,0:T(8,128)(2,1)} %copy-done.30), channel_id=1, source_target_pairs={{0,14},{1,15},{2,12},{3,13},{4,10},{5,11},{6,8},{7,9},{8,6},{9,7},... | collective-permute-start | bytes 245768 | tf_op jit(solution)/shard_map/ppermute | solution.py:373
  96.0 29.2 %copy-start.2 = (f32[320,1152]{1,0:T(8,128)S(1)}, f32[320,1152]{1,0:T(8,128)}, u32[]{:S(2)}) copy-start(f32[320,1152]{1,0:T(8,128)} %get-tuple-element.63.mine_ref) | copy-start | bytes 4423684
  96.0 29.2 %copy-start.26 = (bf16[320,1152]{1,0:T(8,128)(2,1)S(1)}, bf16[320,1152]{1,0:T(8,128)(2,1)}, u32[]{:S(2)}) copy-start(bf16[320,1152]{1,0:T(8,128)(2,1)} %copy-done.25) | copy-start | bytes 2211844
  111.5 7.1 %collective-permute-start.22 = (bf16[320,128]{1,0:T(8,128)(2,1)S(1)}, bf16[320,128]{1,0:T(8,128)(2,1)S(1)}, u32[]{:S(2)}, u32[]{:S(2)}) collective-permute-start(bf16[320,128]{1,0:T(8,128)(2,1)S(1)} %get-tuple-element.56), channel_id=1, source_target_pairs={{0,2},{1,3},{2,0},{3,1},{4,6},{5,7},{6,4},{7,5},{8,10},{9,11},{10,... | collective-permute-start | bytes 245768 | tf_op jit(solution)/shard_map/ppermute | solution.py:373
  112.1 8.8 %collective-permute-start.23 = (bf16[320,128]{1,0:T(8,128)(2,1)S(1)}, bf16[320,128]{1,0:T(8,128)(2,1)S(1)}, u32[]{:S(2)}, u32[]{:S(2)}) collective-permute-start(bf16[320,128]{1,0:T(8,128)(2,1)S(1)} %get-tuple-element.57), channel_id=1, source_target_pairs={{0,4},{1,5},{2,6},{3,7},{4,0},{5,1},{6,2},{7,3},{8,12},{9,13},{10,... | collective-permute-start | bytes 245768 | tf_op jit(solution)/shard_map/ppermute | solution.py:373
  115.8 10.6 %collective-permute-start.24 = (bf16[320,128]{1,0:T(8,128)(2,1)S(1)}, bf16[320,128]{1,0:T(8,128)(2,1)S(1)}, u32[]{:S(2)}, u32[]{:S(2)}) collective-permute-start(bf16[320,128]{1,0:T(8,128)(2,1)S(1)} %get-tuple-element.58), channel_id=1, source_target_pairs={{0,6},{1,7},{2,4},{3,5},{4,2},{5,3},{6,0},{7,1},{8,14},{9,15},{10,... | collective-permute-start | bytes 245768 | tf_op jit(solution)/shard_map/ppermute | solution.py:373
  116.7 12.9 %collective-permute-start.25 = (bf16[320,128]{1,0:T(8,128)(2,1)S(1)}, bf16[320,128]{1,0:T(8,128)(2,1)S(1)}, u32[]{:S(2)}, u32[]{:S(2)}) collective-permute-start(bf16[320,128]{1,0:T(8,128)(2,1)S(1)} %get-tuple-element.59), channel_id=1, source_target_pairs={{0,8},{1,9},{2,10},{3,11},{4,12},{5,13},{6,14},{7,15},{8,0},{9,1},... | collective-permute-start | bytes 245768 | tf_op jit(solution)/shard_map/ppermute | solution.py:373
  118.6 12.9 %collective-permute-start.26 = (bf16[320,128]{1,0:T(8,128)(2,1)S(1)}, bf16[320,128]{1,0:T(8,128)(2,1)S(1)}, u32[]{:S(2)}, u32[]{:S(2)}) collective-permute-start(bf16[320,128]{1,0:T(8,128)(2,1)S(1)} %get-tuple-element.60), channel_id=1, source_target_pairs={{0,10},{1,11},{2,8},{3,9},{4,14},{5,15},{6,12},{7,13},{8,2},{9,3},... | collective-permute-start | bytes 245768 | tf_op jit(solution)/shard_map/ppermute | solution.py:373
  120.8 11.0 %collective-permute-start.27 = (bf16[320,128]{1,0:T(8,128)(2,1)S(1)}, bf16[320,128]{1,0:T(8,128)(2,1)S(1)}, u32[]{:S(2)}, u32[]{:S(2)}) collective-permute-start(bf16[320,128]{1,0:T(8,128)(2,1)S(1)} %get-tuple-element.61), channel_id=1, source_target_pairs={{0,12},{1,13},{2,14},{3,15},{4,8},{5,9},{6,10},{7,11},{8,4},{9,5},... | collective-permute-start | bytes 245768 | tf_op jit(solution)/shard_map/ppermute | solution.py:373
  122.1 11.8 %collective-permute-start.28 = (bf16[320,128]{1,0:T(8,128)(2,1)S(1)}, bf16[320,128]{1,0:T(8,128)(2,1)S(1)}, u32[]{:S(2)}, u32[]{:S(2)}) collective-permute-start(bf16[320,128]{1,0:T(8,128)(2,1)S(1)} %get-tuple-element.62), channel_id=1, source_target_pairs={{0,14},{1,15},{2,12},{3,13},{4,10},{5,11},{6,8},{7,9},{8,6},{9,7},... | collective-permute-start | bytes 245768 | tf_op jit(solution)/shard_map/ppermute | solution.py:373
  125.2 19.6 %copy-start.1 = (f32[20,7680]{1,0:T(8,128)S(1)}, f32[20,7680]{1,0:T(8,128)}, u32[]{:S(2)}) copy-start(f32[20,7680]{1,0:T(8,128)} %refs_16_.1) | copy-start | bytes 1843204
  126.5 9.4 %collective-permute-start.30 = (bf16[192,128]{1,0:T(8,128)(2,1)S(1)}, bf16[192,128]{1,0:T(8,128)(2,1)S(1)}, u32[]{:S(2)}, u32[]{:S(2)}) collective-permute-start(bf16[192,128]{1,0:T(8,128)(2,1)S(1)} %get-tuple-element.66), channel_id=1, source_target_pairs={{0,2},{1,3},{2,0},{3,1},{4,6},{5,7},{6,4},{7,5},{8,10},{9,11},{10,... | collective-permute-start | bytes 147464 | tf_op jit(solution)/shard_map/ppermute | solution.py:373
  129.6 8.4 %collective-permute-start.31 = (bf16[192,128]{1,0:T(8,128)(2,1)S(1)}, bf16[192,128]{1,0:T(8,128)(2,1)S(1)}, u32[]{:S(2)}, u32[]{:S(2)}) collective-permute-start(bf16[192,128]{1,0:T(8,128)(2,1)S(1)} %get-tuple-element.67), channel_id=1, source_target_pairs={{0,4},{1,5},{2,6},{3,7},{4,0},{5,1},{6,2},{7,3},{8,12},{9,13},{10,... | collective-permute-start | bytes 147464 | tf_op jit(solution)/shard_map/ppermute | solution.py:373
  131.5 8.9 %collective-permute-start.32 = (bf16[192,128]{1,0:T(8,128)(2,1)S(1)}, bf16[192,128]{1,0:T(8,128)(2,1)S(1)}, u32[]{:S(2)}, u32[]{:S(2)}) collective-permute-start(bf16[192,128]{1,0:T(8,128)(2,1)S(1)} %get-tuple-element.68), channel_id=1, source_target_pairs={{0,6},{1,7},{2,4},{3,5},{4,2},{5,3},{6,0},{7,1},{8,14},{9,15},{10,... | collective-permute-start | bytes 147464 | tf_op jit(solution)/shard_map/ppermute | solution.py:373
  131.8 8.6 %collective-permute-start.33 = (bf16[192,128]{1,0:T(8,128)(2,1)S(1)}, bf16[192,128]{1,0:T(8,128)(2,1)S(1)}, u32[]{:S(2)}, u32[]{:S(2)}) collective-permute-start(bf16[192,128]{1,0:T(8,128)(2,1)S(1)} %get-tuple-element.69), channel_id=1, source_target_pairs={{0,8},{1,9},{2,10},{3,11},{4,12},{5,13},{6,14},{7,15},{8,0},{9,1},... | collective-permute-start | bytes 147464 | tf_op jit(solution)/shard_map/ppermute | solution.py:373
  133.8 7.8 %collective-permute-start.34 = (bf16[192,128]{1,0:T(8,128)(2,1)S(1)}, bf16[192,128]{1,0:T(8,128)(2,1)S(1)}, u32[]{:S(2)}, u32[]{:S(2)}) collective-permute-start(bf16[192,128]{1,0:T(8,128)(2,1)S(1)} %get-tuple-element.70), channel_id=1, source_target_pairs={{0,10},{1,11},{2,8},{3,9},{4,14},{5,15},{6,12},{7,13},{8,2},{9,3},... | collective-permute-start | bytes 147464 | tf_op jit(solution)/shard_map/ppermute | solution.py:373
  135.9 6.0 %collective-permute-start.35 = (bf16[192,128]{1,0:T(8,128)(2,1)S(1)}, bf16[192,128]{1,0:T(8,128)(2,1)S(1)}, u32[]{:S(2)}, u32[]{:S(2)}) collective-permute-start(bf16[192,128]{1,0:T(8,128)(2,1)S(1)} %get-tuple-element.71), channel_id=1, source_target_pairs={{0,12},{1,13},{2,14},{3,15},{4,8},{5,9},{6,10},{7,11},{8,4},{9,5},... | collective-permute-start | bytes 147464 | tf_op jit(solution)/shard_map/ppermute | solution.py:373
  138.0 6.8 %collective-permute-start.36 = (bf16[192,128]{1,0:T(8,128)(2,1)S(1)}, bf16[192,128]{1,0:T(8,128)(2,1)S(1)}, u32[]{:S(2)}, u32[]{:S(2)}) collective-permute-start(bf16[192,128]{1,0:T(8,128)(2,1)S(1)} %get-tuple-element.72), channel_id=1, source_target_pairs={{0,14},{1,15},{2,12},{3,13},{4,10},{5,11},{6,8},{7,9},{8,6},{9,7},... | collective-permute-start | bytes 147464 | tf_op jit(solution)/shard_map/ppermute | solution.py:373
  (24 other events, 69.1 us)

commit v2 on v1

--- a/solution.py
+++ b/solution.py
@@ -11,10 +11,10 @@
 WINDOW = 1024
 LANES = 128
 HALF = 64
-VMEM_LIMIT = 48 * 1024 * 1024
+VMEM_LIMIT = 24 * 1024 * 1024
 BF16 = jnp.bfloat16
 F32 = jnp.float32
-ORDER = (4, 5, 6, 7, 2, 3, 1)
+FAR_FIRST = (4, 5, 6, 7, 2, 3, 1, 0)
 ANY = pl.BlockSpec(memory_space=pl.ANY)
 VMEM = pl.BlockSpec(memory_space=pltpu.VMEM)
 
@@ -56,7 +56,7 @@
     low = low_lanes(tokens)
     low_r = low_lanes(rows)
     matrix = fw_ref.shape[1] // 3
-    steps = step_ref[...].T
+    steps = step_ref[...]
     high = steps.astype(BF16).astype(F32)
     middle = (steps - high).astype(BF16).astype(F32)
     rest_ = (steps - high - middle).astype(BF16).astype(F32)
@@ -124,9 +124,9 @@
     chip, core = chip_core(width)
     pairs = []
     for other in range(width):
-        for k in range(heads):
+        for i, k in enumerate(FAR_FIRST):
             source = (chip ^ k) * width + (core ^ other)
-            src = ins[other * heads + k]
+            src = ins[other * heads + i]
             if other == 0:
                 pairs.append((src, buf.at[source]))
             else:
@@ -201,65 +201,88 @@
     grad_ref[pl.ds(last_row, HALF), 2 * wide :] = grads2[2 * LANES : 2 * LANES + HALF]
 
 
-def query_side(width, heads, tokens, scale, span, *refs):
+def query_side(width, heads, tokens, scale, span, steps, *refs):
     count = heads * width
+    half_heads = heads // 2
     kv = refs[:count]
-    qs = refs[count : count + heads]
-    copy_ref, fast_gain_ref, window_gain_ref = refs[count + heads : count + heads + 3]
-    outs = refs[count + heads + 3 : count + 2 * heads + 3]
-    buf, qbuf, pay, sems, out_sems = refs[count + 2 * heads + 3 :]
+    qs = refs[count : count + half_heads]
+    copy_ref, fast_gain_ref, window_gain_ref = refs[count + half_heads : count + half_heads + 3]
+    rest = refs[-(half_heads + 5) :]
+    outs, (buf, qbuf, pay, sems, out_sems) = rest[:half_heads], rest[half_heads:]
     chip, core = chip_core(width)
     pairs = []
     for other in range(width):
-        for k in range(heads):
+        for i, k in enumerate(FAR_FIRST):
             source = (chip ^ k) * width + (core ^ other)
-            pairs.append((kv[other * heads + k].at[pl.ds(0, 5 * tokens)], buf.at[source]))
-    for k in range(heads):
-        pairs.append((qs[k], qbuf.at[chip ^ k]))
+            pairs.append((kv[other * heads + i].at[pl.ds(0, 5 * tokens)], buf.at[source]))
+    for i, k in enumerate(steps):
+        pairs.append((qs[i], qbuf.at[lax.rem(chip ^ k, half_heads)]))
     for copy in copy_all(pairs, sems):
         copy.wait()
     wide = 3 * LANES
     mid = tokens // 2
     low = low_lanes(mid)
-    high = jnp.logical_not(low_lanes(tokens))
+    high = jnp.logical_not(low_lanes(2 * tokens))
     size = heads * 40
-    w13 = copy_ref[:, 0 : 2 * wide]
-    w2 = copy_ref[:, 2 * wide :]
-    fast_gain = fast_gain_ref[...]
-    window_gain = window_gain_ref[...]
-    keys_seen = (span + 1) * tokens
-    ahead = lax.broadcasted_iota(jnp.int32, (tokens, keys_seen), 0) - lax.broadcasted_iota(
-        jnp.int32, (tokens, keys_seen), 1
-    )
-    for j in range(heads):
+
+    def query_block(j):
+        tail = qbuf[j, 2 * tokens :].astype(F32)
+        half = jnp.concatenate([jnp.where(low, tail, 0.0), jnp.where(low, turned(tail), 0.0)], axis=0)
+        return jnp.concatenate([qbuf[j, 0:tokens], qbuf[j, tokens : 2 * tokens], half.astype(BF16)], axis=1)
+
+    def two_blocks(j):
         place = j * width + core
-        start = jnp.maximum(place - span, 0)
-        q_tail = qbuf[j, 2 * tokens :].astype(F32)
-        q_half = jnp.concatenate([jnp.where(low, q_tail, 0.0), jnp.where(low, turned(q_tail), 0.0)], axis=0)
-        q = jnp.concatenate([qbuf[j, 0:tokens], qbuf[j, tokens : 2 * tokens], q_half.astype(BF16)], axis=1)
-        seen = buf[pl.ds(start, span + 1)]
+        slot = j % half_heads
+        q = jnp.concatenate([query_block(slot), query_block(slot + 1)], axis=0)
+        blocks = min(width * (j + 2), span + 1 + width)
+        start = 0 if blocks == width * (j + 2) else jnp.maximum(place - span, 0)
+        keys_seen = blocks * tokens
+        seen = buf[pl.ds(start, blocks)]
         tiles = [seen[:, t * tokens : (t + 1) * tokens].reshape(keys_seen, LANES) for t in range(5)]
+        row = lax.broadcasted_iota(jnp.int32, (2 * tokens, 1), 0)
+        row = jnp.where(row < tokens, row, row + (width - 1) * tokens) + (place - start) * tokens
+        distance = row - lax.broadcasted_iota(jnp.int32, (2 * tokens, keys_seen), 1)
+        allowed = distance >= 0
+        if keys_seen > span * tokens:
+            allowed = allowed & (distance < span * tokens)
         score = dot(q, jnp.concatenate(tiles[0:3], axis=1), ((1,), (1,)))
-        distance = ahead + (place - start) * tokens
-        score = jnp.where((distance >= 0) & (distance < span * tokens), score, -jnp.inf)
+        score = jnp.where(allowed, score, -jnp.inf)
         top = jnp.max(score, axis=1, keepdims=True)
         weight = jnp.exp2((score - top) * (scale * math.log2(math.e)))
         total = jnp.sum(weight, axis=1, keepdims=True)
         attended = dot(weight.astype(BF16), jnp.concatenate(tiles[2:5], axis=1), ((1,), (0,))) / total
         attended = jnp.concatenate([jnp.where(high, attended[:, 0:LANES], 0.0), attended[:, LANES:]], axis=1)
         mean_sq = jnp.sum(attended * attended, axis=1, keepdims=True) * (1.0 / size)
-        window_part = attended * lax.rsqrt(mean_sq + 1e-05) * window_gain
-
-        both = dot(q, w13, ((1,), (0,))) * scale
+        window_part = attended * lax.rsqrt(mean_sq + 1e-05) * window_gain_ref[...]
+
+        both = dot(q, copy_ref[:, 0 : 2 * wide], ((1,), (0,))) * scale
         gate, up = both[:, :wide], both[:, wide:]
         hid = (gate / (1.0 + jnp.exp(-gate)) * up).astype(BF16)
-        out = dot(hid, w2, ((1,), (0,))) * scale
+        out = dot(hid, copy_ref[:, 2 * wide :], ((1,), (0,))) * scale
         mean_sq = jnp.sum(out * out, axis=1, keepdims=True) * (1.0 / size)
-        layer = out * lax.rsqrt(mean_sq + 1e-05) * fast_gain + window_part
-        pay[j, 0:tokens] = layer[:, LANES : 2 * LANES].astype(BF16)
-        pay[j, tokens : 2 * tokens] = layer[:, 2 * LANES :].astype(BF16)
-        pay[j, 2 * tokens :] = jnp.where(low, turned(layer[mid:, 0:LANES]), layer[0:mid, 0:LANES]).astype(BF16)
-    for copy in copy_all([(pay.at[chip ^ k], outs[k]) for k in range(heads)], out_sems):
+        layer = out * lax.rsqrt(mean_sq + 1e-05) * fast_gain_ref[...] + window_part
+        for i in range(2):
+            part = layer[i * tokens : (i + 1) * tokens]
+            pay[slot + i, 0:tokens] = part[:, LANES : 2 * LANES].astype(BF16)
+            pay[slot + i, tokens : 2 * tokens] = part[:, 2 * LANES :].astype(BF16)
+            pay[slot + i, 2 * tokens :] = jnp.where(
+                low, turned(part[mid:, 0:LANES]), part[0:mid, 0:LANES]
+            ).astype(BF16)
+
+    first_half = (chip ^ steps[0]) < half_heads
+
+    @pl.when(first_half)
+    def _():
+        for j in range(0, half_heads, 2):
+            two_blocks(j)
+
+    @pl.when(jnp.logical_not(first_half))
+    def _():
+        for j in range(half_heads, heads, 2):
+            two_blocks(j)
+
+    out_pairs = [(pay.at[lax.rem(chip ^ k, half_heads)], outs[i]) for i, k in enumerate(steps)]
+    for copy in copy_all(out_pairs, out_sems):
         copy.wait()
 
 
@@ -310,17 +333,32 @@
         copy.wait()
 
 
-def unpack(width, heads, rows, slot, tokens, *refs):
+def unpack_layer(width, heads, tokens, *refs):
     layers = refs[:heads]
-    moments = refs[heads : 2 * heads]
-    fw_ref, layer_ref, new_ref, momentum_ref, lbuf, mbuf, wbuf, sems = refs[2 * heads :]
+    layer_ref, lbuf, sems = refs[heads:]
     chip, _ = chip_core(width)
-    pairs = [(layers[k], lbuf.at[chip ^ k]) for k in range(heads)]
-    pairs += [(moments[k], mbuf.at[chip ^ k]) for k in range(heads)]
-    for copy in copy_all(pairs, sems):
+    for copy in copy_all([(layers[i], lbuf.at[chip ^ k]) for i, k in enumerate(FAR_FIRST)], sems):
         copy.wait()
     mid = tokens // 2
     low = low_lanes(mid)
+    for head in range(heads):
+        whole, half = tiles_of(head)
+        layer_ref[:, whole : whole + LANES] = lbuf[head, 0:tokens]
+        layer_ref[:, whole + LANES : whole + 2 * LANES] = lbuf[head, tokens : 2 * tokens]
+    for head in range(0, heads, 2):
+        _, half = tiles_of(head)
+        even = lbuf[head, 2 * tokens :].astype(F32)
+        odd = lbuf[head + 1, 2 * tokens :].astype(F32)
+        layer_ref[0:mid, half : half + LANES] = jnp.where(low, turned(even), odd).astype(BF16)
+        layer_ref[mid:, half : half + LANES] = jnp.where(low, even, turned(odd)).astype(BF16)
+
+
+def unpack_moments(width, heads, rows, slot, *refs):
+    moments = refs[:heads]
+    fw_ref, new_ref, momentum_ref, mbuf, wbuf, sems = refs[heads:]
+    chip, _ = chip_core(width)
+    for copy in copy_all([(moments[i], mbuf.at[chip ^ k]) for i, k in enumerate(FAR_FIRST)], sems):
+        copy.wait()
     low_r = low_lanes(slot)
     matrix = fw_ref.shape[1] // 3
 
@@ -332,18 +370,12 @@
 
     for head in range(heads):
         whole, half = tiles_of(head)
-        layer_ref[:, whole : whole + LANES] = lbuf[head, 0:tokens]
-        layer_ref[:, whole + LANES : whole + 2 * LANES] = lbuf[head, tokens : 2 * tokens]
         wbuf[head] = mbuf[head].astype(F32)
         for m in range(3):
             for t in range(2):
                 write(m * matrix + whole + t * LANES, wbuf[head, (2 * m + t) * slot : (2 * m + t + 1) * slot])
     for head in range(0, heads, 2):
         _, half = tiles_of(head)
-        even = lbuf[head, 2 * tokens :].astype(F32)
-        odd = lbuf[head + 1, 2 * tokens :].astype(F32)
-        layer_ref[0:mid, half : half + LANES] = jnp.where(low, turned(even), odd).astype(BF16)
-        layer_ref[mid:, half : half + LANES] = jnp.where(low, even, turned(odd)).astype(BF16)
         even = wbuf[head, 6 * slot : 7 * slot]
         odd = wbuf[head + 1, 6 * slot : 7 * slot]
         write(half, jnp.where(low_r, even, turned(odd)))
@@ -369,14 +401,14 @@
     key_rows = 5 * tokens + 8 * slot
     query_rows = 2 * tokens + tokens // 2
 
+    def cost(micros):
+        return pl.CostEstimate(flops=micros * 500_000_000, transcendentals=0, bytes_accessed=micros * 2_000_000)
+
     def across(value, step):
         return lax.ppermute(value, "seq", [(i, i ^ step) for i in range(count)])
 
     def exchange(pieces):
-        got = {0: pieces[0]}
-        for k in ORDER:
-            got[k] = across(pieces[k], k * width)
-        return [got[k] for k in range(heads)]
+        return [across(pieces[k], k * width) if k else pieces[0] for k in FAR_FIRST]
 
     def packed(size):
         return [jax.ShapeDtypeStruct((size, LANES), BF16)] * heads
@@ -392,8 +424,9 @@
             sem((heads,)),
         ],
         compiler_params=params,
+        cost_estimate=cost(3),
         name="pack_keys",
-    )(key_vectors, value_vectors, step_sizes, fast_weights)
+    )(key_vectors, value_vectors, step_sizes.T, fast_weights)
     query_pieces = pl.pallas_call(
         functools.partial(pack_queries, width, heads),
         out_shape=packed(query_rows),
@@ -401,6 +434,7 @@
         out_specs=[ANY] * heads,
         scratch_shapes=[pltpu.VMEM((heads, query_rows, LANES), BF16), sem((heads,))],
         compiler_params=params,
+        cost_estimate=cost(1),
         name="pack_queries",
     )(queries)
     key_blocks = exchange(key_pieces)
@@ -427,6 +461,7 @@
             sem((count,)),
         ],
         compiler_params=params,
+        cost_estimate=cost(8),
         name="key_side",
     )(*key_blocks)
     gradients = [across(gradient, other) for other in range(1, width)]
@@ -440,22 +475,6 @@
         even_row = jnp.concatenate([gap, row[:, 2 * LANES :], row[:, : 2 * LANES]], axis=1)
         odd_row = jnp.concatenate([gap, row], axis=1)
         return jnp.where(odd == 1, odd_row, even_row)
-
-    layer_pieces = pl.pallas_call(
-        functools.partial(query_side, width, heads, tokens, scale, span),
-        out_shape=packed(query_rows),
-        in_specs=[ANY] * (count + heads) + [VMEM] * 3,
-        out_specs=[ANY] * heads,
-        scratch_shapes=[
-            pltpu.VMEM((count, 5 * tokens, LANES), BF16),
-            pltpu.VMEM((heads, query_rows, LANES), BF16),
-            pltpu.VMEM((heads, query_rows, LANES), BF16),
-            sem((count + heads,)),
-            sem((heads,)),
-        ],
-        compiler_params=params,
-        name="query_side",
-    )(*key_blocks, *query_blocks, copies, gain_row(fast_gain), gain_row(window_gain))
 
     momentum_pieces = pl.pallas_call(
         functools.partial(pack_momentum, width, heads, rows, slot),
@@ -471,29 +490,61 @@
             sem((heads,)),
         ],
         compiler_params=params,
+        cost_estimate=cost(2),
         name="pack_momentum",
     )(gradient, *gradients, natural)
     moments = exchange(momentum_pieces)
-    layers = exchange(layer_pieces)
-
-    layer_out, new_weights, momentum = pl.pallas_call(
-        functools.partial(unpack, width, heads, rows, slot, tokens),
-        out_shape=[
-            jax.ShapeDtypeStruct(queries.shape, BF16),
-            jax.ShapeDtypeStruct(fast_weights.shape, F32),
-            jax.ShapeDtypeStruct(fast_weights.shape, F32),
-        ],
-        in_specs=[ANY] * (2 * heads) + [VMEM],
-        out_specs=[VMEM] * 3,
+
+    half_heads = heads // 2
+    gains = (gain_row(fast_gain), gain_row(window_gain))
+
+    def query_half(steps, blocks, *after):
+        return pl.pallas_call(
+            functools.partial(query_side, width, heads, tokens, scale, span, steps),
+            out_shape=packed(query_rows)[:half_heads],
+            in_specs=[ANY] * (count + half_heads) + [VMEM] * 3 + [ANY] * len(after),
+            out_specs=[ANY] * half_heads,
+            scratch_shapes=[
+                pltpu.VMEM((count, 5 * tokens, LANES), BF16),
+                pltpu.VMEM((half_heads, query_rows, LANES), BF16),
+                pltpu.VMEM((half_heads, query_rows, LANES), BF16),
+                sem((count + half_heads,)),
+                sem((half_heads,)),
+            ],
+            compiler_params=params,
+            cost_estimate=cost(40),
+            name="query_side",
+        )(*key_blocks, *blocks, copies, *gains, *after)
+
+    far, near = FAR_FIRST[:half_heads], FAR_FIRST[half_heads:]
+    layers = query_half(far, query_blocks[:half_heads])
+    layers = layers + query_half(near, query_blocks[half_heads:], momentum_pieces[0])
+    layers = [across(piece, k * width) if k else piece for piece, k in zip(layers, FAR_FIRST)]
+
+    new_weights, momentum = pl.pallas_call(
+        functools.partial(unpack_moments, width, heads, rows, slot),
+        out_shape=[jax.ShapeDtypeStruct(fast_weights.shape, F32)] * 2,
+        in_specs=[ANY] * heads + [VMEM],
+        out_specs=[VMEM] * 2,
         scratch_shapes=[
-            pltpu.VMEM((heads, query_rows, LANES), BF16),
             pltpu.VMEM((heads, 8 * slot, LANES), BF16),
             pltpu.VMEM((heads, 8 * slot, LANES), F32),
-            sem((2 * heads,)),
+            sem((heads,)),
         ],
         compiler_params=params,
-        name="unpack",
-    )(*layers, *moments, fast_weights)
+        cost_estimate=cost(3),
+        name="unpack_moments",
+    )(*moments, fast_weights)
+    layer_out = pl.pallas_call(
+        functools.partial(unpack_layer, width, heads, tokens),
+        out_shape=jax.ShapeDtypeStruct(queries.shape, BF16),
+        in_specs=[ANY] * heads,
+        out_specs=VMEM,
+        scratch_shapes=[pltpu.VMEM((heads, query_rows, LANES), BF16), sem((heads,))],
+        compiler_params=params,
+        cost_estimate=cost(2),
+        name="unpack_layer",
+    )(*layers)
     return (layer_out, new_weights, momentum)
 
 

time: 149 us -> 119 us (0.80)
  waiting for transfers between devices: 40.6 us -> 24 us
  local copies, waits for them, and re-layouts: 17.5 us -> 4.31 us
  Pallas kernels: 31.5 us -> 33 us
    ppermute x37, waiting for transfers between devices: 40.6 us -> 24 us  [across(): return lax.ppermute(value, 'seq', [(i, i ^ step) for i in range(count)])]
    unnamed x71 -> x16, local copies, waits for them, and re-layouts: 17.2 us -> 3.99 us
    pallas_call x2 -> x4, Pallas kernels: 18.7 us -> 21.2 us  [the longest x2 17.5 us: query_half(): pl.pallas_call(functools.partial(query_side, width, heads, tokens, scale,...]
  transfers between devices with their start and end apart: 37 -> 37, of which waited for: 15 -> 11; matrix products, arithmetic and copies ran while one was open for 0% -> 0% of each run, Pallas kernels for 12% -> 24%
where the time goes in v2:
time: 119 us
  starting transfers between devices  56.7 us (48%)
  Pallas kernels  33 us (28%)
  waiting for transfers between devices  24 us (20%)
  local copies, waits for them, and re-layouts  4.31 us (4%)
    ppermute x37, starting transfers between devices, across(): return lax.ppermute(value, 'seq', [(i, i ^ step) for i in range(count)])  56.7 us
    ppermute x37, waiting for transfers between devices, across(): return lax.ppermute(value, 'seq', [(i, i ^ step) for i in range(count)])  24 us
    pallas_call x2, Pallas kernels, query_half(): pl.pallas_call(functools.partial(query_side, width, heads, tokens, scale,...  17.5 us
    pallas_call x1, Pallas kernels, shards(): pl.pallas_call(functools.partial(key_side, width, heads, rows, slot, toke...  6.83 us
    unnamed x16, local copies, waits for them, and re-layouts  3.99 us
    pallas_call x1, Pallas kernels, shards(): pl.pallas_call(functools.partial(pack_keys, width, heads, rows, slot), ou...  2.62 us
  transfers between devices with their start and end apart: 37, of which 11 were waited for; matrix products, arithmetic and copies ran while one was open for 0% of the time, Pallas kernels for 24%

profile of v2, /device:TPU:0, one launch (start us, length us, event | category | flops | bytes accessed | tf_op | source)
XLA Modules:
  0.0 119.1 jit_solution(1307700850687665204)
XLA Ops:
  0.6 1.1 copy-done
  1.8 1.1 copy-done.2
  2.8 1.1 copy-done.3
  3.9 0.7 copy-done.5
  4.6 2.6 %pack_keys.1 = (bf16[832,128]{1,0:T(8,128)(2,1)S(1)}, bf16[832,128]{1,0:T(8,128)(2,1)S(1)}, bf16[832,128]{1,0:T(8,128)(2,1)S(1)}, bf16[832,128]{1,0:T(8,128)(2,1...) custom-call(bf16[128,2560]{1,0:T(8,128)(2,1)S(1)} %copy-done.2, ...), custom_call_target="tpu_custom_call" | custom-call | flops 1500000000 | bytes 6000000 | tf_op jit(solution)/shard_map/pack_keys/pallas_call | solution.py:416
  7.2 6.1 %collective-permute-start.3 = (bf16[832,128]{1,0:T(8,128)(2,1)S(1)}, bf16[832,128]{1,0:T(8,128)(2,1)S(1)}, u32[]{:S(2)}, u32[]{:S(2)}) collective-permute-start(bf16[832,128]{1,0:T(8,128)(2,1)S(1)} %get-tuple-element.43), channel_id=1, source_target_pairs={{0,14},{1,15},{2,12},{3,13},{4,10},{5,11},{6,8},{7,9},{8,6},{9,7},... | collective-permute-start | bytes 638984 | tf_op jit(solution)/shard_map/ppermute | solution.py:408
  13.3 2.0 %collective-permute-start.5 = (bf16[832,128]{1,0:T(8,128)(2,1)S(1)}, bf16[832,128]{1,0:T(8,128)(2,1)S(1)}, u32[]{:S(2)}, u32[]{:S(2)}) collective-permute-start(bf16[832,128]{1,0:T(8,128)(2,1)S(1)} %get-tuple-element.45), channel_id=1, source_target_pairs={{0,6},{1,7},{2,4},{3,5},{4,2},{5,3},{6,0},{7,1},{8,14},{9,15},{10,... | collective-permute-start | bytes 638984 | tf_op jit(solution)/shard_map/ppermute | solution.py:408
  15.3 1.5 %collective-permute-start.6 = (bf16[832,128]{1,0:T(8,128)(2,1)S(1)}, bf16[832,128]{1,0:T(8,128)(2,1)S(1)}, u32[]{:S(2)}, u32[]{:S(2)}) collective-permute-start(bf16[832,128]{1,0:T(8,128)(2,1)S(1)} %get-tuple-element.46), channel_id=1, source_target_pairs={{0,2},{1,3},{2,0},{3,1},{4,6},{5,7},{6,4},{7,5},{8,10},{9,11},{10,... | collective-permute-start | bytes 638984 | tf_op jit(solution)/shard_map/ppermute | solution.py:408
  16.8 2.6 %collective-permute-done.3.refs_3_ = bf16[832,128]{1,0:T(8,128)(2,1)S(1)} collective-permute-done((bf16[832,128]{1,0:T(8,128)(2,1)S(1)}, bf16[832,128]{1,0:T(8,128)(2,1)S(1)}, u32[]{:S(2)}, u32[]{:S(2)}) %collective-permute-start.3) | collective-permute-done | bytes 213024 | tf_op jit(solution)/shard_map/ppermute | solution.py:408
  19.4 6.6 %collective-permute-start.1 = (bf16[832,128]{1,0:T(8,128)(2,1)S(1)}, bf16[832,128]{1,0:T(8,128)(2,1)S(1)}, u32[]{:S(2)}, u32[]{:S(2)}) collective-permute-start(bf16[832,128]{1,0:T(8,128)(2,1)S(1)} %get-tuple-element.41), channel_id=1, source_target_pairs={{0,10},{1,11},{2,8},{3,9},{4,14},{5,15},{6,12},{7,13},{8,2},{9,3},... | collective-permute-start | bytes 638984 | tf_op jit(solution)/shard_map/ppermute | solution.py:408
  26.1 2.4 %collective-permute-done.4.refs_4_ = bf16[832,128]{1,0:T(8,128)(2,1)S(1)} collective-permute-done((bf16[832,128]{1,0:T(8,128)(2,1)S(1)}, bf16[832,128]{1,0:T(8,128)(2,1)S(1)}, u32[]{:S(2)}, u32[]{:S(2)}) %collective-permute-start.4) | collective-permute-done | bytes 213024 | tf_op jit(solution)/shard_map/ppermute | solution.py:408
  28.5 4.4 %collective-permute-start.2 = (bf16[832,128]{1,0:T(8,128)(2,1)S(1)}, bf16[832,128]{1,0:T(8,128)(2,1)S(1)}, u32[]{:S(2)}, u32[]{:S(2)}) collective-permute-start(bf16[832,128]{1,0:T(8,128)(2,1)S(1)} %get-tuple-element.42), channel_id=1, source_target_pairs={{0,12},{1,13},{2,14},{3,15},{4,8},{5,9},{6,10},{7,11},{8,4},{9,5},... | collective-permute-start | bytes 638984 | tf_op jit(solution)/shard_map/ppermute | solution.py:408
  32.9 0.6 collective-permute-done.5.refs_5_
  33.5 0.5 collective-permute-start.10
  34.4 1.1 pack_queries.1
  35.5 10.7 %collective-permute-done.1.refs_1_ = bf16[832,128]{1,0:T(8,128)(2,1)S(1)} collective-permute-done((bf16[832,128]{1,0:T(8,128)(2,1)S(1)}, bf16[832,128]{1,0:T(8,128)(2,1)S(1)}, u32[]{:S(2)}, u32[]{:S(2)}) %collective-permute-start.1) | collective-permute-done | bytes 213024 | tf_op jit(solution)/shard_map/ppermute | solution.py:408
  46.2 0.5 collective-permute-start.13
  46.8 0.4 collective-permute-start.8
  47.6 3.9 %collective-permute-start.23 = (bf16[320,128]{1,0:T(8,128)(2,1)S(1)}, bf16[320,128]{1,0:T(8,128)(2,1)S(1)}, u32[]{:S(2)}, u32[]{:S(2)}) collective-permute-start(bf16[320,128]{1,0:T(8,128)(2,1)S(1)} %get-tuple-element.57), channel_id=1, source_target_pairs={{0,4},{1,5},{2,6},{3,7},{4,0},{5,1},{6,2},{7,3},{8,12},{9,13},{10,... | collective-permute-start | bytes 245768 | tf_op jit(solution)/shard_map/ppermute | solution.py:408
  51.5 1.2 %collective-permute-start.15 = (bf16[320,128]{1,0:T(8,128)(2,1)S(1)}, bf16[320,128]{1,0:T(8,128)(2,1)S(1)}, u32[]{:S(2)}, u32[]{:S(2)}) collective-permute-start(bf16[320,128]{1,0:T(8,128)(2,1)S(1)} %get-tuple-element.48), channel_id=1, source_target_pairs={{0,8},{1,9},{2,10},{3,11},{4,12},{5,13},{6,14},{7,15},{8,0},{9,1},... | collective-permute-start | bytes 245768 | tf_op jit(solution)/shard_map/ppermute | solution.py:408
  52.7 1.7 %collective-permute-start.16 = (bf16[320,128]{1,0:T(8,128)(2,1)S(1)}, bf16[320,128]{1,0:T(8,128)(2,1)S(1)}, u32[]{:S(2)}, u32[]{:S(2)}) collective-permute-start(bf16[320,128]{1,0:T(8,128)(2,1)S(1)} %get-tuple-element.49), channel_id=1, source_target_pairs={{0,10},{1,11},{2,8},{3,9},{4,14},{5,15},{6,12},{7,13},{8,2},{9,3},... | collective-permute-start | bytes 245768 | tf_op jit(solution)/shard_map/ppermute | solution.py:408
  54.4 2.4 %collective-permute-start.17 = (bf16[320,128]{1,0:T(8,128)(2,1)S(1)}, bf16[320,128]{1,0:T(8,128)(2,1)S(1)}, u32[]{:S(2)}, u32[]{:S(2)}) collective-permute-start(bf16[320,128]{1,0:T(8,128)(2,1)S(1)} %get-tuple-element.50), channel_id=1, source_target_pairs={{0,12},{1,13},{2,14},{3,15},{4,8},{5,9},{6,10},{7,11},{8,4},{9,5},... | collective-permute-start | bytes 245768 | tf_op jit(solution)/shard_map/ppermute | solution.py:408
  56.8 2.4 %collective-permute-start.18 = (bf16[320,128]{1,0:T(8,128)(2,1)S(1)}, bf16[320,128]{1,0:T(8,128)(2,1)S(1)}, u32[]{:S(2)}, u32[]{:S(2)}) collective-permute-start(bf16[320,128]{1,0:T(8,128)(2,1)S(1)} %get-tuple-element.51), channel_id=1, source_target_pairs={{0,14},{1,15},{2,12},{3,13},{4,10},{5,11},{6,8},{7,9},{8,6},{9,7},... | collective-permute-start | bytes 245768 | tf_op jit(solution)/shard_map/ppermute | solution.py:408
  59.2 6.8 %key_side.1 = (f32[320,1152]{1,0:T(8,128)S(1)}, bf16[384,1152]{1,0:T(8,128)(2,1)S(1)}, bf16[320,1152]{1,0:T(8,128)(2,1)S(1)}) custom-call(bf16[832,128]{1,0:T(8,128)(2,1)S(1)} %collective-permute-done.refs_0_, bf16[832,128]{1,0:T(8,128)(2,1)S(1)} %collective-permute-done.1.refs_1_, bf16[832,128]{1,0:T(8,128)(2,1)S(1)} %collective-permute-done.2.refs_2_, ...), custom_call_target="tpu_custom_call" | custom-call | flops 4000000000 | bytes 16000000 | tf_op jit(solution)/shard_map/key_side/pallas_call | solution.py:445
  66.1 1.6 %collective-permute-start.25 = (bf16[320,128]{1,0:T(8,128)(2,1)S(1)}, bf16[320,128]{1,0:T(8,128)(2,1)S(1)}, u32[]{:S(2)}, u32[]{:S(2)}) collective-permute-start(bf16[320,128]{1,0:T(8,128)(2,1)S(1)} %get-tuple-element.59), channel_id=1, source_target_pairs={{0,2},{1,3},{2,0},{3,1},{4,6},{5,7},{6,4},{7,5},{8,10},{9,11},{10,... | collective-permute-start | bytes 245768 | tf_op jit(solution)/shard_map/ppermute | solution.py:408
  67.7 9.5 %query_side.2 = (bf16[320,128]{1,0:T(8,128)(2,1)S(1)}, bf16[320,128]{1,0:T(8,128)(2,1)S(1)}, bf16[320,128]{1,0:T(8,128)(2,1)S(1)}, bf16[320,128]{1,0:T(8,128)(2,1)S(1)}) custom-call(bf16[832,128]{1,0:T(8,128)(2,1)S(1)} %collective-permute-done.refs_0_, bf16[832,128]{1,0:T(8,128)(2,1)S(1)} %collective-permute-done.1.refs_1_, ...), custom_call_target="tpu_custom_call" | custom-call | flops 20000000000 | bytes 80000000 | tf_op jit(solution)/shard_map/query_side/pallas_call | solution.py:502
  77.2 2.2 %collective-permute-start.19 = (bf16[320,128]{1,0:T(8,128)(2,1)S(1)}, bf16[320,128]{1,0:T(8,128)(2,1)S(1)}, u32[]{:S(2)}, u32[]{:S(2)}) collective-permute-start(bf16[320,128]{1,0:T(8,128)(2,1)S(1)} %get-tuple-element.53), channel_id=1, source_target_pairs={{0,8},{1,9},{2,10},{3,11},{4,12},{5,13},{6,14},{7,15},{8,0},{9,1},... | collective-permute-start | bytes 245768 | tf_op jit(solution)/shard_map/ppermute | solution.py:408
  79.4 1.0 collective-permute-start.20
  80.5 1.3 %pack_momentum.1 = (bf16[192,128]{1,0:T(8,128)(2,1)S(1)}, bf16[192,128]{1,0:T(8,128)(2,1)S(1)}, bf16[192,128]{1,0:T(8,128)(2,1)S(1)}, bf16[192,128]{1,0:T(8,128)...) custom-call(f32[320,1152]{1,0:T(8,128)S(1)} %get-tuple-element.61.mi, ...), custom_call_target="tpu_custom_call" | custom-call | flops 1000000000 | bytes 4000000 | tf_op jit(solution)/shard_map/pack_momentum/pallas_call | solution.py:479
  81.8 2.9 %collective-permute-start.30 = (bf16[192,128]{1,0:T(8,128)(2,1)S(1)}, bf16[192,128]{1,0:T(8,128)(2,1)S(1)}, u32[]{:S(2)}, u32[]{:S(2)}) collective-permute-start(bf16[192,128]{1,0:T(8,128)(2,1)S(1)} %get-tuple-element.68), channel_id=1, source_target_pairs={{0,8},{1,9},{2,10},{3,11},{4,12},{5,13},{6,14},{7,15},{8,0},{9,1},... | collective-permute-start | bytes 147464 | tf_op jit(solution)/shard_map/ppermute | solution.py:408
  84.7 0.7 collective-permute-start.31
  85.4 2.2 %collective-permute-start.32 = (bf16[192,128]{1,0:T(8,128)(2,1)S(1)}, bf16[192,128]{1,0:T(8,128)(2,1)S(1)}, u32[]{:S(2)}, u32[]{:S(2)}) collective-permute-start(bf16[192,128]{1,0:T(8,128)(2,1)S(1)} %get-tuple-element.70), channel_id=1, source_target_pairs={{0,12},{1,13},{2,14},{3,15},{4,8},{5,9},{6,10},{7,11},{8,4},{9,5},... | collective-permute-start | bytes 147464 | tf_op jit(solution)/shard_map/ppermute | solution.py:408
  87.6 0.3 collective-permute-done.19.refs_0_
  88.0 1.5 %collective-permute-start.33 = (bf16[192,128]{1,0:T(8,128)(2,1)S(1)}, bf16[192,128]{1,0:T(8,128)(2,1)S(1)}, u32[]{:S(2)}, u32[]{:S(2)}) collective-permute-start(bf16[192,128]{1,0:T(8,128)(2,1)S(1)} %get-tuple-element.71), channel_id=1, source_target_pairs={{0,14},{1,15},{2,12},{3,13},{4,10},{5,11},{6,8},{7,9},{8,6},{9,7},... | collective-permute-start | bytes 147464 | tf_op jit(solution)/shard_map/ppermute | solution.py:408
  89.5 2.7 %collective-permute-done.20.refs_1_ = bf16[320,128]{1,0:T(8,128)(2,1)S(1)} collective-permute-done((bf16[320,128]{1,0:T(8,128)(2,1)S(1)}, bf16[320,128]{1,0:T(8,128)(2,1)S(1)}, u32[]{:S(2)}, u32[]{:S(2)}) %collective-permute-start.20) | collective-permute-done | bytes 81952 | tf_op jit(solution)/shard_map/ppermute | solution.py:408
  92.2 1.4 %collective-permute-done.30.refs_0_ = bf16[192,128]{1,0:T(8,128)(2,1)S(1)} collective-permute-done((bf16[192,128]{1,0:T(8,128)(2,1)S(1)}, bf16[192,128]{1,0:T(8,128)(2,1)S(1)}, u32[]{:S(2)}, u32[]{:S(2)}) %collective-permute-start.30) | collective-permute-done | bytes 49184 | tf_op jit(solution)/shard_map/ppermute | solution.py:408
  93.5 1.8 %collective-permute-start.35 = (bf16[192,128]{1,0:T(8,128)(2,1)S(1)}, bf16[192,128]{1,0:T(8,128)(2,1)S(1)}, u32[]{:S(2)}, u32[]{:S(2)}) collective-permute-start(bf16[192,128]{1,0:T(8,128)(2,1)S(1)} %get-tuple-element.73), channel_id=1, source_target_pairs={{0,6},{1,7},{2,4},{3,5},{4,2},{5,3},{6,0},{7,1},{8,14},{9,15},{10,... | collective-permute-start | bytes 147464 | tf_op jit(solution)/shard_map/ppermute | solution.py:408
  95.4 1.1 collective-permute-start.36
  96.5 8.0 %query_side.3 = (bf16[320,128]{1,0:T(8,128)(2,1)S(1)}, bf16[320,128]{1,0:T(8,128)(2,1)S(1)}, bf16[320,128]{1,0:T(8,128)(2,1)S(1)}, bf16[320,128]{1,0:T(8,128)(2,1)S(1)}) custom-call(bf16[832,128]{1,0:T(8,128)(2,1)S(1)} %collective-permute-done.refs_0_, bf16[832,128]{1,0:T(8,128)(2,1)S(1)} %collective-permute-done.1.refs_1_, ...), custom_call_target="tpu_custom_call" | custom-call | flops 20000000000 | bytes 80000000 | tf_op jit(solution)/shard_map/query_side/pallas_call | solution.py:502
  104.5 3.2 %collective-permute-start.21 = (bf16[320,128]{1,0:T(8,128)(2,1)S(1)}, bf16[320,128]{1,0:T(8,128)(2,1)S(1)}, u32[]{:S(2)}, u32[]{:S(2)}) collective-permute-start(bf16[320,128]{1,0:T(8,128)(2,1)S(1)} %get-tuple-element.55), channel_id=1, source_target_pairs={{0,12},{1,13},{2,14},{3,15},{4,8},{5,9},{6,10},{7,11},{8,4},{9,5},... | collective-permute-start | bytes 245768 | tf_op jit(solution)/shard_map/ppermute | solution.py:408
  107.7 1.0 collective-permute-start.22
  108.8 2.6 %collective-permute-start.28 = (bf16[320,128]{1,0:T(8,128)(2,1)S(1)}, bf16[320,128]{1,0:T(8,128)(2,1)S(1)}, u32[]{:S(2)}, u32[]{:S(2)}) collective-permute-start(bf16[320,128]{1,0:T(8,128)(2,1)S(1)} %get-tuple-element.65), channel_id=1, source_target_pairs={{0,6},{1,7},{2,4},{3,5},{4,2},{5,3},{6,0},{7,1},{8,14},{9,15},{10,... | collective-permute-start | bytes 245768 | tf_op jit(solution)/shard_map/ppermute | solution.py:408
  111.4 0.9 collective-permute-start.29
  112.2 1.8 %unpack_moments.1 = (f32[20,7680]{1,0:T(8,128)}, f32[20,7680]{1,0:T(8,128)}) custom-call(bf16[192,128]{1,0:T(8,128)(2,1)S(1)} %collective-permute-done.30.refs_0_, bf16[192,128]{1,0:T(8,128)(2,1)S(1)} %collective-permute-done.31.refs_1_, bf16[192,128]{1,0:T(8,128)(2,1)S(1)} %collective-permute-done.32.refs_2_, ...), custom_call_target="tpu_custom_call" | custom-call | flops 1500000000 | bytes 6000000 | tf_op jit(solution)/shard_map/unpack_moments/pallas_call | solution.py:524
  114.1 1.1 collective-permute-done.22.refs_3_
  115.2 1.2 %collective-permute-done.28.refs_5_ = bf16[320,128]{1,0:T(8,128)(2,1)S(1)} collective-permute-done((bf16[320,128]{1,0:T(8,128)(2,1)S(1)}, bf16[320,128]{1,0:T(8,128)(2,1)S(1)}, u32[]{:S(2)}, u32[]{:S(2)}) %collective-permute-start.28) | collective-permute-done | bytes 81952 | tf_op jit(solution)/shard_map/ppermute | solution.py:408
  116.4 0.6 collective-permute-done.29.refs_6_
  117.0 1.9 %unpack_layer.1 = bf16[128,2560]{1,0:T(8,128)(2,1)} custom-call(bf16[320,128]{1,0:T(8,128)(2,1)S(1)} %collective-permute-done.19.refs_0_, bf16[320,128]{1,0:T(8,128)(2,1)S(1)} %collective-permute-done.20.refs_1_, bf16[320,128]{1,0:T(8,128)(2,1)S(1)} %collective-permute-done.21.refs_2_, bf16[320,128]{1,0:T(8,128)(2,1)S(1)} %collective-permute-done.22.refs_3_, ...), custom_call_target="tpu_custom_call" | custom-call | flops 1000000000 | bytes 4000000 | tf_op jit(solution)/shard_map/unpack_layer/pallas_call | solution.py:538
  (59 shorter events, 1.1 us)
Async XLA Ops:
  0.6 1.1 copy-start
  1.8 1.1 copy-start.2
  2.8 1.1 copy-start.3
  3.9 0.7 copy-start.5
  4.6 29.4 %copy-start.6 = (f32[2560]{0:T(1024)S(1)}, f32[2560]{0:T(1024)}, u32[]{:S(2)}) copy-start(f32[2560]{0:T(1024)} %param.12) | copy-start | bytes 30724
  4.6 29.5 %copy-start.7 = (f32[2560]{0:T(1024)S(1)}, f32[2560]{0:T(1024)}, u32[]{:S(2)}) copy-start(f32[2560]{0:T(1024)} %param.13) | copy-start | bytes 30724
  4.6 29.7 %copy-start.4 = (bf16[128,2560]{1,0:T(8,128)(2,1)S(1)}, bf16[128,2560]{1,0:T(8,128)(2,1)}, u32[]{:S(2)}) copy-start(bf16[128,2560]{1,0:T(8,128)(2,1)} %q_ref.1) | copy-start | bytes 1966084
  7.2 12.2 %collective-permute-start.3 = (bf16[832,128]{1,0:T(8,128)(2,1)S(1)}, bf16[832,128]{1,0:T(8,128)(2,1)S(1)}, u32[]{:S(2)}, u32[]{:S(2)}) collective-permute-start(bf16[832,128]{1,0:T(8,128)(2,1)S(1)} %get-tuple-element.43), channel_id=1, source_target_pairs={{0,14},{1,15},{2,12},{3,13},{4,10},{5,11},{6,8},{7,9},{8,6},{9,7},... | collective-permute-start | bytes 638984 | tf_op jit(solution)/shard_map/ppermute | solution.py:408
  13.3 15.2 %collective-permute-start.4 = (bf16[832,128]{1,0:T(8,128)(2,1)S(1)}, bf16[832,128]{1,0:T(8,128)(2,1)S(1)}, u32[]{:S(2)}, u32[]{:S(2)}) collective-permute-start(bf16[832,128]{1,0:T(8,128)(2,1)S(1)} %get-tuple-element.44), channel_id=1, source_target_pairs={{0,4},{1,5},{2,6},{3,7},{4,0},{5,1},{6,2},{7,3},{8,12},{9,13},{10,... | collective-permute-start | bytes 638984 | tf_op jit(solution)/shard_map/ppermute | solution.py:408
  13.3 20.1 %collective-permute-start.5 = (bf16[832,128]{1,0:T(8,128)(2,1)S(1)}, bf16[832,128]{1,0:T(8,128)(2,1)S(1)}, u32[]{:S(2)}, u32[]{:S(2)}) collective-permute-start(bf16[832,128]{1,0:T(8,128)(2,1)S(1)} %get-tuple-element.45), channel_id=1, source_target_pairs={{0,6},{1,7},{2,4},{3,5},{4,2},{5,3},{6,0},{7,1},{8,14},{9,15},{10,... | collective-permute-start | bytes 638984 | tf_op jit(solution)/shard_map/ppermute | solution.py:408
  15.3 18.2 %collective-permute-start.6 = (bf16[832,128]{1,0:T(8,128)(2,1)S(1)}, bf16[832,128]{1,0:T(8,128)(2,1)S(1)}, u32[]{:S(2)}, u32[]{:S(2)}) collective-permute-start(bf16[832,128]{1,0:T(8,128)(2,1)S(1)} %get-tuple-element.46), channel_id=1, source_target_pairs={{0,2},{1,3},{2,0},{3,1},{4,6},{5,7},{6,4},{7,5},{8,10},{9,11},{10,... | collective-permute-start | bytes 638984 | tf_op jit(solution)/shard_map/ppermute | solution.py:408
  16.8 17.2 %collective-permute-start = (bf16[832,128]{1,0:T(8,128)(2,1)S(1)}, bf16[832,128]{1,0:T(8,128)(2,1)S(1)}, u32[]{:S(2)}, u32[]{:S(2)}) collective-permute-start(bf16[832,128]{1,0:T(8,128)(2,1)S(1)} %get-tuple-element.40), channel_id=1, source_target_pairs={{0,8},{1,9},{2,10},{3,11},{4,12},{5,13},{6,14},{7,15},{8,0},{9,1},... | collective-permute-start | bytes 638984 | tf_op jit(solution)/shard_map/ppermute | solution.py:408
  19.4 26.7 %collective-permute-start.1 = (bf16[832,128]{1,0:T(8,128)(2,1)S(1)}, bf16[832,128]{1,0:T(8,128)(2,1)S(1)}, u32[]{:S(2)}, u32[]{:S(2)}) collective-permute-start(bf16[832,128]{1,0:T(8,128)(2,1)S(1)} %get-tuple-element.41), channel_id=1, source_target_pairs={{0,10},{1,11},{2,8},{3,9},{4,14},{5,15},{6,12},{7,13},{8,2},{9,3},... | collective-permute-start | bytes 638984 | tf_op jit(solution)/shard_map/ppermute | solution.py:408
  28.5 17.7 %collective-permute-start.2 = (bf16[832,128]{1,0:T(8,128)(2,1)S(1)}, bf16[832,128]{1,0:T(8,128)(2,1)S(1)}, u32[]{:S(2)}, u32[]{:S(2)}) collective-permute-start(bf16[832,128]{1,0:T(8,128)(2,1)S(1)} %get-tuple-element.42), channel_id=1, source_target_pairs={{0,12},{1,13},{2,14},{3,15},{4,8},{5,9},{6,10},{7,11},{8,4},{9,5},... | collective-permute-start | bytes 638984 | tf_op jit(solution)/shard_map/ppermute | solution.py:408
  33.5 13.2 %collective-permute-start.14 = (bf16[832,128]{1,0:T(8,128)(2,1)S(1)}, bf16[832,128]{1,0:T(8,128)(2,1)S(1)}, u32[]{:S(2)}, u32[]{:S(2)}) collective-permute-start(bf16[832,128]{1,0:T(8,128)(2,1)S(1)} %get-tuple-element.47.refs_7_), channel_id=1, source_target_pairs={{0,1},{1,0},{2,3},{3,2},{4,5},{5,4},{6,7},{7,6},{8,9},{9,8},{10,11... | collective-permute-start | bytes 638984 | tf_op jit(solution)/shard_map/ppermute | solution.py:408
  33.5 13.3 %collective-permute-start.10 = (bf16[832,128]{1,0:T(8,128)(2,1)S(1)}, bf16[832,128]{1,0:T(8,128)(2,1)S(1)}, u32[]{:S(2)}, u32[]{:S(2)}) collective-permute-start(bf16[832,128]{1,0:T(8,128)(2,1)S(1)} %collective-permute-done.3.refs_3_), channel_id=1, source_target_pairs={{0,1},{1,0},{2,3},{3,2},{4,5},{5,4},{6,7},{7,6},{8,9},{9,8},{10,11... | collective-permute-start | bytes 638984 | tf_op jit(solution)/shard_map/ppermute | solution.py:408
  34.0 13.2 %collective-permute-start.11 = (bf16[832,128]{1,0:T(8,128)(2,1)S(1)}, bf16[832,128]{1,0:T(8,128)(2,1)S(1)}, u32[]{:S(2)}, u32[]{:S(2)}) collective-permute-start(bf16[832,128]{1,0:T(8,128)(2,1)S(1)} %collective-permute-done.4.refs_4_), channel_id=1, source_target_pairs={{0,1},{1,0},{2,3},{3,2},{4,5},{5,4},{6,7},{7,6},{8,9},{9,8},{10,11... | collective-permute-start | bytes 638984 | tf_op jit(solution)/shard_map/ppermute | solution.py:408
  46.2 1.5 %collective-permute-start.12 = (bf16[832,128]{1,0:T(8,128)(2,1)S(1)}, bf16[832,128]{1,0:T(8,128)(2,1)S(1)}, u32[]{:S(2)}, u32[]{:S(2)}) collective-permute-start(bf16[832,128]{1,0:T(8,128)(2,1)S(1)} %collective-permute-done.5.refs_5_), channel_id=1, source_target_pairs={{0,1},{1,0},{2,3},{3,2},{4,5},{5,4},{6,7},{7,6},{8,9},{9,8},{10,11... | collective-permute-start | bytes 638984 | tf_op jit(solution)/shard_map/ppermute | solution.py:408
  46.2 5.4 %collective-permute-start.13 = (bf16[832,128]{1,0:T(8,128)(2,1)S(1)}, bf16[832,128]{1,0:T(8,128)(2,1)S(1)}, u32[]{:S(2)}, u32[]{:S(2)}) collective-permute-start(bf16[832,128]{1,0:T(8,128)(2,1)S(1)} %collective-permute-done.6.refs_6_), channel_id=1, source_target_pairs={{0,1},{1,0},{2,3},{3,2},{4,5},{5,4},{6,7},{7,6},{8,9},{9,8},{10,11... | collective-permute-start | bytes 638984 | tf_op jit(solution)/shard_map/ppermute | solution.py:408
  46.7 6.0 %collective-permute-start.7 = (bf16[832,128]{1,0:T(8,128)(2,1)S(1)}, bf16[832,128]{1,0:T(8,128)(2,1)S(1)}, u32[]{:S(2)}, u32[]{:S(2)}) collective-permute-start(bf16[832,128]{1,0:T(8,128)(2,1)S(1)} %collective-permute-done.refs_0_), channel_id=1, source_target_pairs={{0,1},{1,0},{2,3},{3,2},{4,5},{5,4},{6,7},{7,6},{8,9},{9,8},{10,11... | collective-permute-start | bytes 638984 | tf_op jit(solution)/shard_map/ppermute | solution.py:408
  46.8 7.6 %collective-permute-start.8 = (bf16[832,128]{1,0:T(8,128)(2,1)S(1)}, bf16[832,128]{1,0:T(8,128)(2,1)S(1)}, u32[]{:S(2)}, u32[]{:S(2)}) collective-permute-start(bf16[832,128]{1,0:T(8,128)(2,1)S(1)} %collective-permute-done.1.refs_1_), channel_id=1, source_target_pairs={{0,1},{1,0},{2,3},{3,2},{4,5},{5,4},{6,7},{7,6},{8,9},{9,8},{10,11... | collective-permute-start | bytes 638984 | tf_op jit(solution)/shard_map/ppermute | solution.py:408
  47.2 9.6 %collective-permute-start.9 = (bf16[832,128]{1,0:T(8,128)(2,1)S(1)}, bf16[832,128]{1,0:T(8,128)(2,1)S(1)}, u32[]{:S(2)}, u32[]{:S(2)}) collective-permute-start(bf16[832,128]{1,0:T(8,128)(2,1)S(1)} %collective-permute-done.2.refs_2_), channel_id=1, source_target_pairs={{0,1},{1,0},{2,3},{3,2},{4,5},{5,4},{6,7},{7,6},{8,9},{9,8},{10,11... | collective-permute-start | bytes 638984 | tf_op jit(solution)/shard_map/ppermute | solution.py:408
  47.6 34.1 %collective-permute-start.23 = (bf16[320,128]{1,0:T(8,128)(2,1)S(1)}, bf16[320,128]{1,0:T(8,128)(2,1)S(1)}, u32[]{:S(2)}, u32[]{:S(2)}) collective-permute-start(bf16[320,128]{1,0:T(8,128)(2,1)S(1)} %get-tuple-element.57), channel_id=1, source_target_pairs={{0,4},{1,5},{2,6},{3,7},{4,0},{5,1},{6,2},{7,3},{8,12},{9,13},{10,... | collective-permute-start | bytes 245768 | tf_op jit(solution)/shard_map/ppermute | solution.py:408
  51.5 14.5 %collective-permute-start.15 = (bf16[320,128]{1,0:T(8,128)(2,1)S(1)}, bf16[320,128]{1,0:T(8,128)(2,1)S(1)}, u32[]{:S(2)}, u32[]{:S(2)}) collective-permute-start(bf16[320,128]{1,0:T(8,128)(2,1)S(1)} %get-tuple-element.48), channel_id=1, source_target_pairs={{0,8},{1,9},{2,10},{3,11},{4,12},{5,13},{6,14},{7,15},{8,0},{9,1},... | collective-permute-start | bytes 245768 | tf_op jit(solution)/shard_map/ppermute | solution.py:408
  52.7 13.4 %collective-permute-start.16 = (bf16[320,128]{1,0:T(8,128)(2,1)S(1)}, bf16[320,128]{1,0:T(8,128)(2,1)S(1)}, u32[]{:S(2)}, u32[]{:S(2)}) collective-permute-start(bf16[320,128]{1,0:T(8,128)(2,1)S(1)} %get-tuple-element.49), channel_id=1, source_target_pairs={{0,10},{1,11},{2,8},{3,9},{4,14},{5,15},{6,12},{7,13},{8,2},{9,3},... | collective-permute-start | bytes 245768 | tf_op jit(solution)/shard_map/ppermute | solution.py:408
  54.4 13.3 %collective-permute-start.17 = (bf16[320,128]{1,0:T(8,128)(2,1)S(1)}, bf16[320,128]{1,0:T(8,128)(2,1)S(1)}, u32[]{:S(2)}, u32[]{:S(2)}) collective-permute-start(bf16[320,128]{1,0:T(8,128)(2,1)S(1)} %get-tuple-element.50), channel_id=1, source_target_pairs={{0,12},{1,13},{2,14},{3,15},{4,8},{5,9},{6,10},{7,11},{8,4},{9,5},... | collective-permute-start | bytes 245768 | tf_op jit(solution)/shard_map/ppermute | solution.py:408
  56.8 10.9 %collective-permute-start.18 = (bf16[320,128]{1,0:T(8,128)(2,1)S(1)}, bf16[320,128]{1,0:T(8,128)(2,1)S(1)}, u32[]{:S(2)}, u32[]{:S(2)}) collective-permute-start(bf16[320,128]{1,0:T(8,128)(2,1)S(1)} %get-tuple-element.51), channel_id=1, source_target_pairs={{0,14},{1,15},{2,12},{3,13},{4,10},{5,11},{6,8},{7,9},{8,6},{9,7},... | collective-permute-start | bytes 245768 | tf_op jit(solution)/shard_map/ppermute | solution.py:408
  66.0 18.6 %collective-permute-start.24 = (bf16[320,128]{1,0:T(8,128)(2,1)S(1)}, bf16[320,128]{1,0:T(8,128)(2,1)S(1)}, u32[]{:S(2)}, u32[]{:S(2)}) collective-permute-start(bf16[320,128]{1,0:T(8,128)(2,1)S(1)} %get-tuple-element.58), channel_id=1, source_target_pairs={{0,6},{1,7},{2,4},{3,5},{4,2},{5,3},{6,0},{7,1},{8,14},{9,15},{10,... | collective-permute-start | bytes 245768 | tf_op jit(solution)/shard_map/ppermute | solution.py:408
  66.1 19.3 %collective-permute-start.25 = (bf16[320,128]{1,0:T(8,128)(2,1)S(1)}, bf16[320,128]{1,0:T(8,128)(2,1)S(1)}, u32[]{:S(2)}, u32[]{:S(2)}) collective-permute-start(bf16[320,128]{1,0:T(8,128)(2,1)S(1)} %get-tuple-element.59), channel_id=1, source_target_pairs={{0,2},{1,3},{2,0},{3,1},{4,6},{5,7},{6,4},{7,5},{8,10},{9,11},{10,... | collective-permute-start | bytes 245768 | tf_op jit(solution)/shard_map/ppermute | solution.py:408
  67.7 11.7 %collective-permute-start.26 = (f32[320,1152]{1,0:T(8,128)S(1)}, f32[320,1152]{1,0:T(8,128)S(1)}, u32[]{:S(2)}, u32[]{:S(2)}) collective-permute-start(f32[320,1152]{1,0:T(8,128)S(1)} %get-tuple-element.61.mine_ref), channel_id=1, source_target_pairs={{0,1},{1,0},{2,3},{3,2},{4,5},{5,4},{6,7},{7,6},{8,9},{9,8},{10,11... | collective-permute-start | bytes 4423688 | tf_op jit(solution)/shard_map/ppermute | solution.py:408
  77.2 10.8 %collective-permute-start.19 = (bf16[320,128]{1,0:T(8,128)(2,1)S(1)}, bf16[320,128]{1,0:T(8,128)(2,1)S(1)}, u32[]{:S(2)}, u32[]{:S(2)}) collective-permute-start(bf16[320,128]{1,0:T(8,128)(2,1)S(1)} %get-tuple-element.53), channel_id=1, source_target_pairs={{0,8},{1,9},{2,10},{3,11},{4,12},{5,13},{6,14},{7,15},{8,0},{9,1},... | collective-permute-start | bytes 245768 | tf_op jit(solution)/shard_map/ppermute | solution.py:408
  79.4 12.7 %collective-permute-start.20 = (bf16[320,128]{1,0:T(8,128)(2,1)S(1)}, bf16[320,128]{1,0:T(8,128)(2,1)S(1)}, u32[]{:S(2)}, u32[]{:S(2)}) collective-permute-start(bf16[320,128]{1,0:T(8,128)(2,1)S(1)} %get-tuple-element.54), channel_id=1, source_target_pairs={{0,10},{1,11},{2,8},{3,9},{4,14},{5,15},{6,12},{7,13},{8,2},{9,3},... | collective-permute-start | bytes 245768 | tf_op jit(solution)/shard_map/ppermute | solution.py:408
  81.8 11.8 %collective-permute-start.30 = (bf16[192,128]{1,0:T(8,128)(2,1)S(1)}, bf16[192,128]{1,0:T(8,128)(2,1)S(1)}, u32[]{:S(2)}, u32[]{:S(2)}) collective-permute-start(bf16[192,128]{1,0:T(8,128)(2,1)S(1)} %get-tuple-element.68), channel_id=1, source_target_pairs={{0,8},{1,9},{2,10},{3,11},{4,12},{5,13},{6,14},{7,15},{8,0},{9,1},... | collective-permute-start | bytes 147464 | tf_op jit(solution)/shard_map/ppermute | solution.py:408
  84.7 10.7 %collective-permute-start.31 = (bf16[192,128]{1,0:T(8,128)(2,1)S(1)}, bf16[192,128]{1,0:T(8,128)(2,1)S(1)}, u32[]{:S(2)}, u32[]{:S(2)}) collective-permute-start(bf16[192,128]{1,0:T(8,128)(2,1)S(1)} %get-tuple-element.69), channel_id=1, source_target_pairs={{0,10},{1,11},{2,8},{3,9},{4,14},{5,15},{6,12},{7,13},{8,2},{9,3},... | collective-permute-start | bytes 147464 | tf_op jit(solution)/shard_map/ppermute | solution.py:408
  85.4 19.1 %collective-permute-start.32 = (bf16[192,128]{1,0:T(8,128)(2,1)S(1)}, bf16[192,128]{1,0:T(8,128)(2,1)S(1)}, u32[]{:S(2)}, u32[]{:S(2)}) collective-permute-start(bf16[192,128]{1,0:T(8,128)(2,1)S(1)} %get-tuple-element.70), channel_id=1, source_target_pairs={{0,12},{1,13},{2,14},{3,15},{4,8},{5,9},{6,10},{7,11},{8,4},{9,5},... | collective-permute-start | bytes 147464 | tf_op jit(solution)/shard_map/ppermute | solution.py:408
  88.0 19.7 %collective-permute-start.33 = (bf16[192,128]{1,0:T(8,128)(2,1)S(1)}, bf16[192,128]{1,0:T(8,128)(2,1)S(1)}, u32[]{:S(2)}, u32[]{:S(2)}) collective-permute-start(bf16[192,128]{1,0:T(8,128)(2,1)S(1)} %get-tuple-element.71), channel_id=1, source_target_pairs={{0,14},{1,15},{2,12},{3,13},{4,10},{5,11},{6,8},{7,9},{8,6},{9,7},... | collective-permute-start | bytes 147464 | tf_op jit(solution)/shard_map/ppermute | solution.py:408
  92.2 16.6 %collective-permute-start.34 = (bf16[192,128]{1,0:T(8,128)(2,1)S(1)}, bf16[192,128]{1,0:T(8,128)(2,1)S(1)}, u32[]{:S(2)}, u32[]{:S(2)}) collective-permute-start(bf16[192,128]{1,0:T(8,128)(2,1)S(1)} %get-tuple-element.72), channel_id=1, source_target_pairs={{0,4},{1,5},{2,6},{3,7},{4,0},{5,1},{6,2},{7,3},{8,12},{9,13},{10,... | collective-permute-start | bytes 147464 | tf_op jit(solution)/shard_map/ppermute | solution.py:408
  93.5 15.2 %collective-permute-start.35 = (bf16[192,128]{1,0:T(8,128)(2,1)S(1)}, bf16[192,128]{1,0:T(8,128)(2,1)S(1)}, u32[]{:S(2)}, u32[]{:S(2)}) collective-permute-start(bf16[192,128]{1,0:T(8,128)(2,1)S(1)} %get-tuple-element.73), channel_id=1, source_target_pairs={{0,6},{1,7},{2,4},{3,5},{4,2},{5,3},{6,0},{7,1},{8,14},{9,15},{10,... | collective-permute-start | bytes 147464 | tf_op jit(solution)/shard_map/ppermute | solution.py:408
  95.4 16.0 %collective-permute-start.36 = (bf16[192,128]{1,0:T(8,128)(2,1)S(1)}, bf16[192,128]{1,0:T(8,128)(2,1)S(1)}, u32[]{:S(2)}, u32[]{:S(2)}) collective-permute-start(bf16[192,128]{1,0:T(8,128)(2,1)S(1)} %get-tuple-element.74), channel_id=1, source_target_pairs={{0,2},{1,3},{2,0},{3,1},{4,6},{5,7},{6,4},{7,5},{8,10},{9,11},{10,... | collective-permute-start | bytes 147464 | tf_op jit(solution)/shard_map/ppermute | solution.py:408
  96.5 15.7 %copy-start.1 = (f32[20,7680]{1,0:T(8,128)S(1)}, f32[20,7680]{1,0:T(8,128)}, u32[]{:S(2)}) copy-start(f32[20,7680]{1,0:T(8,128)} %refs_8_.1) | copy-start | bytes 1843204
  104.5 9.6 %collective-permute-start.21 = (bf16[320,128]{1,0:T(8,128)(2,1)S(1)}, bf16[320,128]{1,0:T(8,128)(2,1)S(1)}, u32[]{:S(2)}, u32[]{:S(2)}) collective-permute-start(bf16[320,128]{1,0:T(8,128)(2,1)S(1)} %get-tuple-element.55), channel_id=1, source_target_pairs={{0,12},{1,13},{2,14},{3,15},{4,8},{5,9},{6,10},{7,11},{8,4},{9,5},... | collective-permute-start | bytes 245768 | tf_op jit(solution)/shard_map/ppermute | solution.py:408
  107.7 7.5 %collective-permute-start.22 = (bf16[320,128]{1,0:T(8,128)(2,1)S(1)}, bf16[320,128]{1,0:T(8,128)(2,1)S(1)}, u32[]{:S(2)}, u32[]{:S(2)}) collective-permute-start(bf16[320,128]{1,0:T(8,128)(2,1)S(1)} %get-tuple-element.56), channel_id=1, source_target_pairs={{0,14},{1,15},{2,12},{3,13},{4,10},{5,11},{6,8},{7,9},{8,6},{9,7},... | collective-permute-start | bytes 245768 | tf_op jit(solution)/shard_map/ppermute | solution.py:408
  108.7 6.5 %collective-permute-start.27 = (bf16[320,128]{1,0:T(8,128)(2,1)S(1)}, bf16[320,128]{1,0:T(8,128)(2,1)S(1)}, u32[]{:S(2)}, u32[]{:S(2)}) collective-permute-start(bf16[320,128]{1,0:T(8,128)(2,1)S(1)} %get-tuple-element.64), channel_id=1, source_target_pairs={{0,4},{1,5},{2,6},{3,7},{4,0},{5,1},{6,2},{7,3},{8,12},{9,13},{10,... | collective-permute-start | bytes 245768 | tf_op jit(solution)/shard_map/ppermute | solution.py:408
  108.8 7.7 %collective-permute-start.28 = (bf16[320,128]{1,0:T(8,128)(2,1)S(1)}, bf16[320,128]{1,0:T(8,128)(2,1)S(1)}, u32[]{:S(2)}, u32[]{:S(2)}) collective-permute-start(bf16[320,128]{1,0:T(8,128)(2,1)S(1)} %get-tuple-element.65), channel_id=1, source_target_pairs={{0,6},{1,7},{2,4},{3,5},{4,2},{5,3},{6,0},{7,1},{8,14},{9,15},{10,... | collective-permute-start | bytes 245768 | tf_op jit(solution)/shard_map/ppermute | solution.py:408
  111.4 5.7 %collective-permute-start.29 = (bf16[320,128]{1,0:T(8,128)(2,1)S(1)}, bf16[320,128]{1,0:T(8,128)(2,1)S(1)}, u32[]{:S(2)}, u32[]{:S(2)}) collective-permute-start(bf16[320,128]{1,0:T(8,128)(2,1)S(1)} %get-tuple-element.66), channel_id=1, source_target_pairs={{0,2},{1,3},{2,0},{3,1},{4,6},{5,7},{6,4},{7,5},{8,10},{9,11},{10,... | collective-permute-start | bytes 245768 | tf_op jit(solution)/shard_map/ppermute | solution.py:408

commit v3 on v0

v3 whole, which is shorter than its diff:
```python
import functools
import math

import jax
import jax.numpy as jnp
from jax import lax
from jax.experimental import pallas as pl
from jax.experimental.pallas import tpu as pltpu
from jax.sharding import PartitionSpec as P

WINDOW = 1024
LANES = 128
HALF = 64
VMEM_LIMIT = 24 * 1024 * 1024
BF16 = jnp.bfloat16
F32 = jnp.float32
I32 = jnp.int32
FAR = (4, 5, 6, 7)
NEAR = (2, 3, 1, 0)
HBM = pl.BlockSpec(memory_space=pltpu.HBM)
ANY = pl.BlockSpec(memory_space=pl.ANY)
VMEM = pl.BlockSpec(memory_space=pltpu.VMEM)


def tiles_of(head):
    first = (5 * head) // 2
    odd = head % 2
    return (first + odd) * LANES, (first if odd else first + 2) * LANES


def turned(tile):
    return pltpu.roll(tile, HALF, axis=1)


def low_lanes(rows):
    return lax.broadcasted_iota(I32, (rows, LANES), 1) < HALF


def dot(left, right, contract):
    return lax.dot_general(left, right, (contract, ((), ())), preferred_element_type=F32)


def chip_core(width):
    place = lax.axis_index("seq")
    return place // width, lax.rem(place, width)


def slot_of(index, slot):
    part = (index * (65536 // slot + (65536 % slot > 0))) >> 16
    return part, index - part * slot


def natural_row(row, odd):
    return jnp.where(odd == 1, jnp.where(row < 2 * LANES, row + HALF, row - 2 * LANES), row)


def copy_all(pairs, sems):
    copies = [pltpu.make_async_copy(src, dst, sems.at[i]) for i, (src, dst) in enumerate(pairs)]
    for copy in copies:
        copy.start()
    return copies


def pack_keys(width, heads, rows, slot, steps, k_hbm, v_hbm, step_ref, fw_hbm, *rest):
    few = heads // 2
    outs, (k_ref, v_ref, fw_ref, pay, wbuf, sems) = rest[:few], rest[few:]
    chip, _ = chip_core(width)
    side = (chip ^ steps[0]) // few
    slab = k_ref.shape[1]
    matrix = fw_hbm.shape[1] // 3
    at = pl.multiple_of(side * slab, LANES)
    pairs = [(k_hbm.at[:, pl.ds(at, slab)], k_ref), (v_hbm.at[:, pl.ds(at, slab)], v_ref)]
    for m in range(3):
        lane = pl.multiple_of(side * slab + m * matrix, LANES)
        pairs.append((fw_hbm.at[:, pl.ds(lane, slab)], fw_ref.at[m]))
    copies = copy_all(pairs, sems)
    tokens = k_ref.shape[0]
    low = low_lanes(tokens)
    low_r = low_lanes(rows)
    for copy in copies:
        copy.wait()
    wbuf[...] = jnp.zeros_like(wbuf)
    for head in range(few):
        whole, half = tiles_of(head)
        odd = head % 2
        pay[head, 0:tokens] = k_ref[:, whole : whole + LANES]
        pay[head, tokens : 2 * tokens] = k_ref[:, whole + LANES : whole + 2 * LANES]
        pay[head, 3 * tokens : 4 * tokens] = v_ref[:, whole : whole + LANES]
        pay[head, 4 * tokens : 5 * tokens] = v_ref[:, whole + LANES : whole + 2 * LANES]
        k_half = k_ref[:, half : half + LANES].astype(F32)
        v_half = v_ref[:, half : half + LANES].astype(F32)
        mixed = jnp.where(low, turned(k_half) if odd else k_half, v_half if odd else turned(v_half))
        pay[head, 2 * tokens : 3 * tokens] = mixed.astype(BF16)
        halves = []
        for m in range(3):
            for t in range(2):
                spot = (2 * m + t) * slot
                wbuf[head, spot : spot + rows] = fw_ref[m, :, whole + t * LANES : whole + (t + 1) * LANES]
            halves.append(fw_ref[m, :, half : half + LANES])
        first, third, second = halves
        if odd:
            first, third = turned(first), turned(third)
        else:
            second = turned(second)
        wbuf[head, 6 * slot : 6 * slot + rows] = jnp.where(low_r, first, second)
        wbuf[head, 7 * slot : 7 * slot + rows] = jnp.where(low_r, third, 0.0)
        step = step_ref[pl.ds(side * few + head, 1)]
        high = step.astype(BF16).astype(F32)
        middle = (step - high).astype(BF16).astype(F32)
        wbuf[head, rows : rows + 1] = high
        wbuf[head, rows + 1 : rows + 2] = middle
        wbuf[head, rows + 2 : rows + 3] = step - high - middle
        pay[head, 5 * tokens :] = wbuf[head].astype(BF16)
    for i, k in enumerate(steps):
        outs[i][...] = pay[lax.rem(chip ^ k, few)]


def pack_queries(width, heads, q_ref, *rest):
    outs, (pay,) = rest[:heads], rest[heads:]
    chip, _ = chip_core(width)
    tokens = q_ref.shape[0]
    mid = tokens // 2
    low = low_lanes(mid)
    for head in range(heads):
        whole, half = tiles_of(head)
        pay[head, 0:tokens] = q_ref[:, whole : whole + LANES]
        pay[head, tokens : 2 * tokens] = q_ref[:, whole + LANES : whole + 2 * LANES]
        top = q_ref[0:mid, half : half + LANES].astype(F32)
        bottom = q_ref[mid:, half : half + LANES].astype(F32)
        if head % 2:
            top = turned(top)
        else:
            bottom = turned(bottom)
        pay[head, 2 * tokens :] = jnp.where(low, top, bottom).astype(BF16)
    for i, k in enumerate(FAR + NEAR):
        outs[i][...] = pay[chip ^ k]


def key_side(width, heads, rows, slot, tokens, scale, *refs):
    count = heads * width
    ins = refs[:count]
    grad_ref, copy_ref, kv_ref = refs[count : count + 3]
    gates, hidden, target = refs[count + 3 :]
    chip, core = chip_core(width)
    odd = lax.rem(chip, 2)
    wide = 3 * LANES
    size = rows * count
    place = {k: i for i, k in enumerate(FAR + NEAR)}
    blocks = [ins[other * heads + place[k]] for other in range(width) for k in range(heads)]
    for index, block in enumerate(blocks):
        other, k = divmod(index, heads)
        kv_ref[(chip ^ k) * width + (core ^ other)] = block[0 : 5 * tokens]
    parts = [block[5 * tokens :].astype(F32) for block in blocks]
    column, row_in = slot_of(lax.broadcasted_iota(I32, (wide, count * slot), 1), slot)
    source = ((column & (heads - 1)) ^ chip) * width + (core ^ (column >> (heads.bit_length() - 1)))
    wanted = lax.broadcasted_iota(I32, (wide, count * slot), 0)
    chosen = (source * rows + row_in == natural_row(wanted, odd)) & (row_in < rows) & (wanted < size)
    chosen = jnp.where(chosen, 1.0, 0.0).astype(BF16)
    gathered = [
        jnp.concatenate([part[t * slot : (t + 1) * slot] for part in parts], axis=0).astype(BF16) for t in range(8)
    ]
    placed = dot(chosen, jnp.concatenate(gathered, axis=1), ((1,), (0,)))
    tile = [placed[:, t * LANES : (t + 1) * LANES] for t in range(8)]
    low = low_lanes(wide)
    columns = [tile[0], tile[1], jnp.where(low, tile[6], 0.0), tile[2], tile[3], tile[7]]
    columns += [jnp.where(low, 0.0, tile[6]), tile[4], tile[5]]
    for t, column_tile in enumerate(columns):
        copy_ref[:, t * LANES : (t + 1) * LANES] = column_tile.astype(BF16)

    steps = [jnp.sum(part[rows : rows + 3], axis=0, keepdims=True) for part in parts[:heads]]
    steps = jnp.concatenate(steps, axis=0).T
    w13 = copy_ref[:, 0 : 2 * wide]
    w2 = copy_ref[:, 2 * wide :]
    for j in range(heads):
        block = blocks[j]
        keys = jnp.concatenate([block[t * tokens : (t + 1) * tokens] for t in range(3)], axis=1)
        values = jnp.concatenate([block[t * tokens : (t + 1) * tokens] for t in range(2, 5)], axis=1)
        at = j * tokens
        tgt = (-steps[:, j : j + 1] * values.astype(F32)).astype(BF16)
        both = dot(keys, w13, ((1,), (0,))) * scale
        back = dot(tgt, w2, ((1,), (1,))) * scale
        gate, up = both[:, :wide], both[:, wide:]
        sig = 1.0 / (1.0 + jnp.exp(-gate))
        silu = gate * sig
        gates[at : at + tokens, 0:wide] = (back * up * (sig * (1.0 + gate * (1.0 - sig)))).astype(BF16)
        gates[at : at + tokens, wide:] = (back * silu).astype(BF16)
        hidden[at : at + tokens] = (silu * up).astype(BF16)
        target[at : at + tokens] = tgt
    all_keys = [
        jnp.concatenate([blocks[j][t * tokens : (t + 1) * tokens] for t in range(3)], axis=1) for j in range(heads)
    ]
    grads13 = dot(jnp.concatenate(all_keys, axis=0), gates[...], ((0,), (0,))) * scale
    grads2 = dot(hidden[...], target[...], ((0,), (0,))) * scale
    grad_ref[:, 0 : 2 * wide] = grads13[0:size]
    grad_ref[:, 2 * wide :] = grads2[0:size]


def query_side(width, heads, tokens, scale, span, steps, *refs):
    few = heads // 2
    kv_ref, copy_ref, fast_gain_ref, window_gain_ref = refs[:4]
    qs = refs[4 : 4 + few]
    outs, (qbuf, pay) = refs[-(few + 2) : -2], refs[-2:]
    chip, core = chip_core(width)
    for i, k in enumerate(steps):
        qbuf[lax.rem(chip ^ k, few)] = qs[i][...]
    wide = 3 * LANES
    mid = tokens // 2
    low = low_lanes(mid)
    high = jnp.logical_not(low_lanes(2 * tokens))
    size = heads * 40

    def query_block(j):
        tail = qbuf[j, 2 * tokens :].astype(F32)
        half = jnp.concatenate([jnp.where(low, tail, 0.0), jnp.where(low, turned(tail), 0.0)], axis=0)
        return jnp.concatenate([qbuf[j, 0:tokens], qbuf[j, tokens : 2 * tokens], half.astype(BF16)], axis=1)

    def two_blocks(j):
        place = j * width + core
        slot = j % few
        q = jnp.concatenate([query_block(slot), query_block(slot + 1)], axis=0)
        blocks = min(width * (j + 2), span + 1 + width)
        start = 0 if blocks == width * (j + 2) else jnp.maximum(place - span, 0)
        keys_seen = blocks * tokens
        seen = kv_ref[pl.ds(start, blocks)]
        tiles = [seen[:, t * tokens : (t + 1) * tokens].reshape(keys_seen, LANES) for t in range(5)]
        row = lax.broadcasted_iota(I32, (2 * tokens, 1), 0)
        row = jnp.where(row < tokens, row, row + (width - 1) * tokens) + (place - start) * tokens
        distance = row - lax.broadcasted_iota(I32, (2 * tokens, keys_seen), 1)
        allowed = distance >= 0
        if keys_seen > span * tokens:
            allowed = allowed & (distance < span * tokens)
        score = dot(q, jnp.concatenate(tiles[0:3], axis=1), ((1,), (1,)))
        score = jnp.where(allowed, score, -jnp.inf)
        top = jnp.max(score, axis=1, keepdims=True)
        weight = jnp.exp2((score - top) * (scale * math.log2(math.e)))
        total = jnp.sum(weight, axis=1, keepdims=True)
        attended = dot(weight.astype(BF16), jnp.concatenate(tiles[2:5], axis=1), ((1,), (0,))) / total
        attended = jnp.concatenate([jnp.where(high, attended[:, 0:LANES], 0.0), attended[:, LANES:]], axis=1)
        mean_sq = jnp.sum(attended * attended, axis=1, keepdims=True) * (1.0 / size)
        window_part = attended * lax.rsqrt(mean_sq + 1e-05) * window_gain_ref[...]

        both = dot(q, copy_ref[:, 0 : 2 * wide], ((1,), (0,))) * scale
        gate, up = both[:, :wide], both[:, wide:]
        hid = (gate / (1.0 + jnp.exp(-gate)) * up).astype(BF16)
        out = dot(hid, copy_ref[:, 2 * wide :], ((1,), (0,))) * scale
        mean_sq = jnp.sum(out * out, axis=1, keepdims=True) * (1.0 / size)
        layer = out * lax.rsqrt(mean_sq + 1e-05) * fast_gain_ref[...] + window_part
        for i in range(2):
            part = layer[i * tokens : (i + 1) * tokens]
            pay[slot + i, 0:tokens] = part[:, LANES : 2 * LANES].astype(BF16)
            pay[slot + i, tokens : 2 * tokens] = part[:, 2 * LANES :].astype(BF16)
            pay[slot + i, 2 * tokens :] = jnp.where(
                low, turned(part[mid:, 0:LANES]), part[0:mid, 0:LANES]
            ).astype(BF16)

    first_half = (chip ^ steps[0]) < few

    @pl.when(first_half)
    def _():
        for j in range(0, few, 2):
            two_blocks(j)

    @pl.when(jnp.logical_not(first_half))
    def _():
        for j in range(few, heads, 2):
            two_blocks(j)

    for i, k in enumerate(steps):
        outs[i][...] = pay[lax.rem(chip ^ k, few)]


def pack_momentum(width, heads, rows, slot, *refs):
    grads = refs[:width]
    copy_ref = refs[width]
    layers = refs[width + 1 : width + 1 + heads]
    outs = refs[width + 1 + heads : width + 1 + 2 * heads]
    (pay,) = refs[width + 1 + 2 * heads :]
    chip, core = chip_core(width)
    odd = lax.rem(chip, 2)
    size = rows * heads * width
    wide = 3 * LANES
    summed = grads[0][...]
    for other in grads[1:]:
        summed = summed + other[...]
    rounded = summed.astype(BF16)
    old = copy_ref[0:size].astype(F32)
    moved = old - rounded.astype(F32)
    ratio = (jnp.sum(old * old, axis=0, keepdims=True) + 1e-06) / (jnp.sum(moved * moved, axis=0, keepdims=True) + 1e-06)
    ratio = jnp.sqrt(ratio)
    ratio_high = ratio.astype(BF16).astype(F32)
    head, row_in = slot_of(lax.broadcasted_iota(I32, (heads * slot, size), 0), slot)
    wanted = (head * width + core) * rows + row_in
    chosen = (wanted == natural_row(lax.broadcasted_iota(I32, (heads * slot, size), 1), odd)) & (row_in < rows)
    picked = dot(jnp.where(chosen, 1.0, 0.0).astype(BF16), rounded, ((1,), (0,)))
    _, row_in = slot_of(lax.broadcasted_iota(I32, (heads * slot, 1), 0), slot)
    picked = jnp.where(row_in == rows, ratio_high, jnp.where(row_in == rows + 1, ratio - ratio_high, picked))
    tile = [picked[:, t * LANES : (t + 1) * LANES] for t in range(9)]
    low = low_lanes(heads * slot)
    order = [tile[0], tile[1], tile[3], tile[4], tile[7], tile[8], jnp.where(low, tile[2], tile[6]), tile[5]]
    for b in range(heads):
        pay[b] = jnp.concatenate([part[b * slot : (b + 1) * slot] for part in order], axis=0).astype(BF16)
    for i, k in enumerate(FAR + NEAR):
        cut = layers[i].shape[0]
        outs[i][0:cut] = layers[i][...]
        outs[i][cut:] = pay[chip ^ k]


def unpack(width, heads, rows, slot, tokens, steps, *refs):
    few = heads // 2
    pieces = refs[:few]
    fw_hbm = refs[few]
    layer_hbm, new_hbm, momentum_hbm, buf, fw_ref, layer_ref, new_ref, momentum_ref, in_sems, sems = refs[-10:]
    chip, _ = chip_core(width)
    side = (chip ^ steps[0]) // few
    slab = layer_ref.shape[1]
    matrix = fw_hbm.shape[1] // 3

    def lanes(m):
        return pl.ds(pl.multiple_of(side * slab + m * matrix, LANES), slab)

    reads = copy_all([(fw_hbm.at[:, lanes(m)], fw_ref.at[m]) for m in range(3)], in_sems)
    for i, k in enumerate(steps):
        buf[lax.rem(chip ^ k, few)] = pieces[i][...]
    mid = tokens // 2
    cut = 2 * tokens + mid
    low = low_lanes(mid)
    low_r = low_lanes(slot)
    for head in range(few):
        whole, half = tiles_of(head)
        layer_ref[:, whole : whole + LANES] = buf[head, 0:tokens]
        layer_ref[:, whole + LANES : whole + 2 * LANES] = buf[head, tokens : 2 * tokens]
    for head in range(0, few, 2):
        _, half = tiles_of(head)
        even = buf[head, 2 * tokens : cut].astype(F32)
        odd = buf[head + 1, 2 * tokens : cut].astype(F32)
        layer_ref[0:mid, half : half + LANES] = jnp.where(low, turned(even), odd).astype(BF16)
        layer_ref[mid:, half : half + LANES] = jnp.where(low, even, turned(odd)).astype(BF16)
    writes = copy_all([(layer_ref, layer_hbm.at[:, lanes(0)])], sems)

    for copy in reads:
        copy.wait()

    def write(m, lane, block):
        moment = block[0:rows]
        factor = block[rows : rows + 1] + block[rows + 1 : rows + 2]
        momentum_ref[m, :, lane : lane + LANES] = moment
        new_ref[m, :, lane : lane + LANES] = (fw_ref[m, :, lane : lane + LANES] - moment) * factor

    moments = [buf[head, cut:].astype(F32) for head in range(few)]
    for head in range(few):
        whole, half = tiles_of(head)
        for m in range(3):
            for t in range(2):
                write(m, whole + t * LANES, moments[head][(2 * m + t) * slot : (2 * m + t + 1) * slot])
    for head in range(0, few, 2):
        _, half = tiles_of(head)
        even = moments[head][6 * slot : 7 * slot]
        odd = moments[head + 1][6 * slot : 7 * slot]
        write(0, half, jnp.where(low_r, even, turned(odd)))
        write(2, half, jnp.where(low_r, turned(even), odd))
        even = moments[head][7 * slot :]
        odd = moments[head + 1][7 * slot :]
        write(1, half, jnp.where(low_r, even, turned(odd)))
    pairs = [(new_ref.at[m], new_hbm.at[:, lanes(m)]) for m in range(3)]
    pairs += [(momentum_ref.at[m], momentum_hbm.at[:, lanes(m)]) for m in range(3)]
    for copy in writes + copy_all(pairs, sems.at[pl.ds(1, 6)]):
        copy.wait()


def shards(queries, key_vectors, value_vectors, step_sizes, fast_weights, fast_gain, window_gain):
    tokens = queries.shape[0]
    heads = step_sizes.shape[1]
    few = heads // 2
    head_width = queries.shape[1] // heads
    scale = 1.0 / math.sqrt(head_width)
    count = lax.axis_size("seq")
    width = count // heads
    rows = fast_weights.shape[0]
    slot = -(-(rows + 3) // 8) * 8
    span = WINDOW // tokens
    wide = 3 * LANES
    slab = few * head_width
    params = pltpu.CompilerParams(vmem_limit_bytes=VMEM_LIMIT)
    sem = pltpu.SemaphoreType.DMA
    key_rows = 5 * tokens + 8 * slot
    query_rows = 2 * tokens + tokens // 2
    out_rows = query_rows + 8 * slot

    def across(value, step):
        return lax.ppermute(value, "seq", [(i, i ^ step) for i in range(count)])

    def exchange(pieces, steps):
        return [across(piece, k * width) if k else piece for piece, k in zip(pieces, steps)]

    def packed(size, many):
        return [jax.ShapeDtypeStruct((size, LANES), BF16)] * many

    def cost(micros):
        return pl.CostEstimate(flops=micros * 500_000_000, transcendentals=0, bytes_accessed=micros * 2_000_000)

    def call(body, name, micros, *operands, **kwargs):
        return pl.pallas_call(
            body, compiler_params=params, cost_estimate=cost(micros), name=name, **kwargs
        )(*operands)

    step_rows = step_sizes.T

    def keys_for(steps):
        return call(
            functools.partial(pack_keys, width, heads, rows, slot, steps),
            "pack_keys",
            2,
            key_vectors,
            value_vectors,
            step_rows,
            fast_weights,
            out_shape=packed(key_rows, few),
            in_specs=[HBM, HBM, VMEM, HBM],
            out_specs=[VMEM] * few,
            scratch_shapes=[
                pltpu.VMEM((tokens, slab), BF16),
                pltpu.VMEM((tokens, slab), BF16),
                pltpu.VMEM((3, rows, slab), F32),
                pltpu.VMEM((few, key_rows, LANES), BF16),
                pltpu.VMEM((few, 8 * slot, LANES), F32),
                sem((5,)),
            ],
        )

    key_blocks = exchange(keys_for(FAR), FAR) + exchange(keys_for(NEAR), NEAR)
    for other in range(1, width):
        key_blocks = key_blocks + [across(block, other) for block in key_blocks[:heads]]
    query_pieces = call(
        functools.partial(pack_queries, width, heads),
        "pack_queries",
        1,
        queries,
        out_shape=packed(query_rows, heads),
        in_specs=[VMEM],
        out_specs=[VMEM] * heads,
        scratch_shapes=[pltpu.VMEM((heads, query_rows, LANES), BF16)],
    )
    query_blocks = exchange(query_pieces, FAR + NEAR)

    gradient, copies, key_values = call(
        functools.partial(key_side, width, heads, rows, slot, tokens, scale),
        "key_side",
        0,
        *key_blocks,
        out_shape=[
            jax.ShapeDtypeStruct((head_width, 3 * wide), F32),
            jax.ShapeDtypeStruct((wide, 3 * wide), BF16),
            jax.ShapeDtypeStruct((count, 5 * tokens, LANES), BF16),
        ],
        in_specs=[VMEM] * count,
        out_specs=[VMEM] * 3,
        scratch_shapes=[
            pltpu.VMEM((heads * tokens, 2 * wide), BF16),
            pltpu.VMEM((heads * tokens, wide), BF16),
            pltpu.VMEM((heads * tokens, wide), BF16),
        ],
    )
    gradients = [across(gradient, other) for other in range(1, width)]

    head = lax.axis_index("seq") // width
    odd = head % 2

    def gain_row(gain):
        row = lax.dynamic_slice_in_dim(gain.reshape(heads, head_width), head, 1, 0)
        gap = jnp.zeros((1, HALF), F32)
        even_row = jnp.concatenate([gap, row[:, 2 * LANES :], row[:, : 2 * LANES]], axis=1)
        odd_row = jnp.concatenate([gap, row], axis=1)
        return jnp.where(odd == 1, odd_row, even_row)

    gains = (gain_row(fast_gain), gain_row(window_gain))

    def layers_of(steps, blocks, micros):
        return call(
            functools.partial(query_side, width, heads, tokens, scale, span, steps),
            "query_side",
            micros,
            key_values,
            copies,
            *gains,
            *blocks,
            out_shape=packed(query_rows, few),
            in_specs=[VMEM] * (4 + few),
            out_specs=[VMEM] * few,
            scratch_shapes=[
                pltpu.VMEM((few, query_rows, LANES), BF16),
                pltpu.VMEM((few, query_rows, LANES), BF16),
            ],
        )

    near_layers = layers_of(NEAR, query_blocks[few:], 0)
    far_layers = layers_of(FAR, query_blocks[:few], 40)
    pieces = call(
        functools.partial(pack_momentum, width, heads, rows, slot),
        "pack_momentum",
        2,
        gradient,
        *gradients,
        copies,
        *far_layers,
        *near_layers,
        out_shape=packed(out_rows, heads),
        in_specs=[VMEM] * (width + 1 + heads),
        out_specs=[VMEM] * heads,
        scratch_shapes=[pltpu.VMEM((heads, 8 * slot, LANES), BF16)],
    )
    pieces = exchange(pieces, FAR + NEAR)

    def outputs_of(steps, blocks, *before):
        return call(
            functools.partial(unpack, width, heads, rows, slot, tokens, steps),
            "unpack",
            2,
            *blocks,
            fast_weights,
            *before,
            out_shape=[
                jax.ShapeDtypeStruct(queries.shape, BF16),
                jax.ShapeDtypeStruct(fast_weights.shape, F32),
                jax.ShapeDtypeStruct(fast_weights.shape, F32),
            ],
            in_specs=[VMEM] * few + [HBM] * (1 + len(before)),
            out_specs=[HBM] * 3,
            scratch_shapes=[
                pltpu.VMEM((few, out_rows, LANES), BF16),
                pltpu.VMEM((3, rows, slab), F32),
                pltpu.VMEM((tokens, slab), BF16),
                pltpu.VMEM((3, rows, slab), F32),
                pltpu.VMEM((3, rows, slab), F32),
                sem((3,)),
                sem((7,)),
            ],
            input_output_aliases={few + 1 + i: i for i in range(len(before))},
        )

    return tuple(outputs_of(FAR, pieces[:few], *outputs_of(NEAR, pieces[few:])))


def solution(mesh):
    in_specs = (
        P(("groups", "seq"), None),
        P(("groups", "seq"), None),
        P(("groups", "seq"), None),
        P(("groups", "seq"), None),
        P("seq", None),
        P(),
        P(),
    )
    out_specs = (P(("groups", "seq"), None), P(("groups", "seq"), None), P(("groups", "seq"), None))
    return jax.shard_map(shards, mesh=mesh, in_specs=in_specs, out_specs=out_specs, check_vma=False)
```

time: 504 us -> 102 us (0.20)
  the two profiles are of different devices: /device:TPU:0 before, /device:TPU:12 now
where the time goes in v3:
time: 102 us
  waiting for transfers between devices  52.9 us (52%)
  starting transfers between devices  28.6 us (28%)
  Pallas kernels  15.4 us (15%)
  local copies, waits for them, and re-layouts  4.31 us (4%)
    ppermute x30, waiting for transfers between devices, across(): return lax.ppermute(value, 'seq', [(i, i ^ step) for i in range(count)])  52.9 us
    ppermute x30, starting transfers between devices, across(): return lax.ppermute(value, 'seq', [(i, i ^ step) for i in range(count)])  28.6 us
    pallas_call x9, Pallas kernels, call(): pl.pallas_call(body, compiler_params=params, cost_estimate=cost(micros),...  15.4 us
    unnamed x18, local copies, waits for them, and re-layouts  3.99 us
  transfers between devices with their start and end apart: 30, of which 13 were waited for; matrix products, arithmetic and copies ran while one was open for 0% of the time, Pallas kernels for 13%

profile of v3, /device:TPU:12, one launch (start us, length us, event | category | flops | bytes accessed | tf_op | source)
XLA Modules:
  0.0 102.2 jit_solution(7224908154821026004)
XLA Ops:
  0.6 1.1 %copy-done = f32[20,7680]{1,0:T(8,128)S(1)} copy-done((f32[20,7680]{1,0:T(8,128)S(1)}, f32[20,7680]{1,0:T(8,128)}, u32[]{:S(2)}) %copy-start) | copy-done | bytes 614424
  1.8 1.1 %copy-done.3 = bf16[128,2560]{1,0:T(8,128)(2,1)S(1)} copy-done((bf16[128,2560]{1,0:T(8,128)(2,1)S(1)}, bf16[128,2560]{1,0:T(8,128)(2,1)}, u32[]{:S(2)}) %copy-start.3) | copy-done | bytes 655384
  2.8 1.1 %copy-done.4 = bf16[128,2560]{1,0:T(8,128)(2,1)S(1)} copy-done((bf16[128,2560]{1,0:T(8,128)(2,1)S(1)}, bf16[128,2560]{1,0:T(8,128)(2,1)}, u32[]{:S(2)}) %copy-start.4) | copy-done | bytes 655384
  3.9 0.7 copy-done.6
  4.6 0.5 pack_keys.2
  5.1 2.7 %collective-permute-start = (bf16[832,128]{1,0:T(8,128)(2,1)S(1)}, bf16[832,128]{1,0:T(8,128)(2,1)S(1)}, u32[]{:S(2)}, u32[]{:S(2)}) collective-permute-start(bf16[832,128]{1,0:T(8,128)(2,1)S(1)} %get-tuple-element.41), channel_id=1, source_target_pairs={{0,8},{1,9},{2,10},{3,11},{4,12},{5,13},{6,14},{7,15},{8,0},{9,1},... | collective-permute-start | bytes 638984 | tf_op jit(solution)/shard_map/ppermute | solution.py:390
  7.8 0.3 collective-permute-start.1
  8.1 1.6 %collective-permute-start.2 = (bf16[832,128]{1,0:T(8,128)(2,1)S(1)}, bf16[832,128]{1,0:T(8,128)(2,1)S(1)}, u32[]{:S(2)}, u32[]{:S(2)}) collective-permute-start(bf16[832,128]{1,0:T(8,128)(2,1)S(1)} %get-tuple-element.43), channel_id=1, source_target_pairs={{0,12},{1,13},{2,14},{3,15},{4,8},{5,9},{6,10},{7,11},{8,4},{9,5},... | collective-permute-start | bytes 638984 | tf_op jit(solution)/shard_map/ppermute | solution.py:390
  9.7 0.2 pack_queries.1
  9.8 2.5 %collective-permute-start.20 = (bf16[320,128]{1,0:T(8,128)(2,1)S(1)}, bf16[320,128]{1,0:T(8,128)(2,1)S(1)}, u32[]{:S(2)}, u32[]{:S(2)}) collective-permute-start(bf16[320,128]{1,0:T(8,128)(2,1)S(1)} %get-tuple-element.60), channel_id=1, source_target_pairs={{0,4},{1,5},{2,6},{3,7},{4,0},{5,1},{6,2},{7,3},{8,12},{9,13},{10,... | collective-permute-start | bytes 245768 | tf_op jit(solution)/shard_map/ppermute | solution.py:390
  12.4 1.1 %collective-permute-start.21 = (bf16[320,128]{1,0:T(8,128)(2,1)S(1)}, bf16[320,128]{1,0:T(8,128)(2,1)S(1)}, u32[]{:S(2)}, u32[]{:S(2)}) collective-permute-start(bf16[320,128]{1,0:T(8,128)(2,1)S(1)} %get-tuple-element.61), channel_id=1, source_target_pairs={{0,6},{1,7},{2,4},{3,5},{4,2},{5,3},{6,0},{7,1},{8,14},{9,15},{10,... | collective-permute-start | bytes 245768 | tf_op jit(solution)/shard_map/ppermute | solution.py:390
  13.4 0.5 pack_keys.3
  13.9 11.3 %collective-permute-done.20.refs_4_ = bf16[320,128]{1,0:T(8,128)(2,1)S(1)} collective-permute-done((bf16[320,128]{1,0:T(8,128)(2,1)S(1)}, bf16[320,128]{1,0:T(8,128)(2,1)S(1)}, u32[]{:S(2)}, u32[]{:S(2)}) %collective-permute-start.20) | collective-permute-done | bytes 81952 | tf_op jit(solution)/shard_map/ppermute | solution.py:390
  25.4 0.7 collective-permute-done.21.refs_5_
  26.1 0.5 collective-permute-start.4
  26.6 3.2 %collective-permute-done.refs_0_ = bf16[832,128]{1,0:T(8,128)(2,1)S(1)} collective-permute-done((bf16[832,128]{1,0:T(8,128)(2,1)S(1)}, bf16[832,128]{1,0:T(8,128)(2,1)S(1)}, u32[]{:S(2)}, u32[]{:S(2)}) %collective-permute-start) | collective-permute-done | bytes 213024 | tf_op jit(solution)/shard_map/ppermute | solution.py:390
  30.0 5.2 %collective-permute-done.1.refs_1_ = bf16[832,128]{1,0:T(8,128)(2,1)S(1)} collective-permute-done((bf16[832,128]{1,0:T(8,128)(2,1)S(1)}, bf16[832,128]{1,0:T(8,128)(2,1)S(1)}, u32[]{:S(2)}, u32[]{:S(2)}) %collective-permute-start.1) | collective-permute-done | bytes 213024 | tf_op jit(solution)/shard_map/ppermute | solution.py:390
  35.2 0.5 collective-permute-start.6
  35.7 5.0 %collective-permute-done.2.refs_2_ = bf16[832,128]{1,0:T(8,128)(2,1)S(1)} collective-permute-done((bf16[832,128]{1,0:T(8,128)(2,1)S(1)}, bf16[832,128]{1,0:T(8,128)(2,1)S(1)}, u32[]{:S(2)}, u32[]{:S(2)}) %collective-permute-start.2) | collective-permute-done | bytes 213024 | tf_op jit(solution)/shard_map/ppermute | solution.py:390
  40.6 3.6 %collective-permute-done.3.refs_3_ = bf16[832,128]{1,0:T(8,128)(2,1)S(1)} collective-permute-done((bf16[832,128]{1,0:T(8,128)(2,1)S(1)}, bf16[832,128]{1,0:T(8,128)(2,1)S(1)}, u32[]{:S(2)}, u32[]{:S(2)}) %collective-permute-start.3) | collective-permute-done | bytes 213024 | tf_op jit(solution)/shard_map/ppermute | solution.py:390
  44.3 0.5 collective-permute-start.8
  45.2 3.6 %collective-permute-done.6.refs_6_ = bf16[832,128]{1,0:T(8,128)(2,1)S(1)} collective-permute-done((bf16[832,128]{1,0:T(8,128)(2,1)S(1)}, bf16[832,128]{1,0:T(8,128)(2,1)S(1)}, u32[]{:S(2)}, u32[]{:S(2)}) %collective-permute-start.6) | collective-permute-done | bytes 213024 | tf_op jit(solution)/shard_map/ppermute | solution.py:390
  48.7 0.5 collective-permute-start.11
  49.3 0.4 collective-permute-start.13
  49.8 1.5 %collective-permute-start.16 = (bf16[320,128]{1,0:T(8,128)(2,1)S(1)}, bf16[320,128]{1,0:T(8,128)(2,1)S(1)}, u32[]{:S(2)}, u32[]{:S(2)}) collective-permute-start(bf16[320,128]{1,0:T(8,128)(2,1)S(1)} %get-tuple-element.52), channel_id=1, source_target_pairs={{0,8},{1,9},{2,10},{3,11},{4,12},{5,13},{6,14},{7,15},{8,0},{9,1},... | collective-permute-start | bytes 245768 | tf_op jit(solution)/shard_map/ppermute | solution.py:390
  51.2 2.4 %collective-permute-start.17 = (bf16[320,128]{1,0:T(8,128)(2,1)S(1)}, bf16[320,128]{1,0:T(8,128)(2,1)S(1)}, u32[]{:S(2)}, u32[]{:S(2)}) collective-permute-start(bf16[320,128]{1,0:T(8,128)(2,1)S(1)} %get-tuple-element.53), channel_id=1, source_target_pairs={{0,10},{1,11},{2,8},{3,9},{4,14},{5,15},{6,12},{7,13},{8,2},{9,3},... | collective-permute-start | bytes 245768 | tf_op jit(solution)/shard_map/ppermute | solution.py:390
  53.7 0.4 collective-permute-start.18
  54.1 1.6 %collective-permute-start.19 = (bf16[320,128]{1,0:T(8,128)(2,1)S(1)}, bf16[320,128]{1,0:T(8,128)(2,1)S(1)}, u32[]{:S(2)}, u32[]{:S(2)}) collective-permute-start(bf16[320,128]{1,0:T(8,128)(2,1)S(1)} %get-tuple-element.55), channel_id=1, source_target_pairs={{0,14},{1,15},{2,12},{3,13},{4,10},{5,11},{6,8},{7,9},{8,6},{9,7},... | collective-permute-start | bytes 245768 | tf_op jit(solution)/shard_map/ppermute | solution.py:390
  55.7 1.5 %collective-permute-start.22 = (bf16[320,128]{1,0:T(8,128)(2,1)S(1)}, bf16[320,128]{1,0:T(8,128)(2,1)S(1)}, u32[]{:S(2)}, u32[]{:S(2)}) collective-permute-start(bf16[320,128]{1,0:T(8,128)(2,1)S(1)} %get-tuple-element.62), channel_id=1, source_target_pairs={{0,2},{1,3},{2,0},{3,1},{4,6},{5,7},{6,4},{7,5},{8,10},{9,11},{10,... | collective-permute-start | bytes 245768 | tf_op jit(solution)/shard_map/ppermute | solution.py:390
  57.2 4.0 %key_side.1 = (f32[320,1152]{1,0:T(8,128)S(1)}, bf16[384,1152]{1,0:T(8,128)(2,1)S(1)}, bf16[16,640,128]{2,1,0:T(8,128)(2,1)S(1)}) custom-call(bf16[832,128]{1,0:T(8,128)(2,1)S(1)} %collective-permute-done.refs_0_, bf16[832,128]{1,0:T(8,128)(2,1)S(1)} %collective-permute-done.1.refs_1_, bf16[832,128]{1,0:T(8,128)(2,1)S(1)} %collective-permute-done.2.refs_2_, ...), custom_call_target="tpu_custom_call" | custom-call | tf_op jit(solution)/shard_map/key_side/pallas_call | solution.py:402
  61.3 2.9 %query_side.3 = (bf16[320,128]{1,0:T(8,128)(2,1)S(1)}, bf16[320,128]{1,0:T(8,128)(2,1)S(1)}, bf16[320,128]{1,0:T(8,128)(2,1)S(1)}, bf16[320,128]{1,0:T(8,128)(2,1)S(1)}) custom-call(bf16[16,640,128]{2,1,0:T(8,128)(2,1)S(1)} %get-tuple-element.51.refs_0_, bf16[384,1152]{1,0:T(8,128)(2,1)S(1)} %get-tuple-element.50.refs_1_.refs_2_, ...), custom_call_target="tpu_custom_call" | custom-call | tf_op jit(solution)/shard_map/query_side/pallas_call | solution.py:402
  64.3 1.9 %collective-permute-done.19.refs_7_ = bf16[320,128]{1,0:T(8,128)(2,1)S(1)} collective-permute-done((bf16[320,128]{1,0:T(8,128)(2,1)S(1)}, bf16[320,128]{1,0:T(8,128)(2,1)S(1)}, u32[]{:S(2)}, u32[]{:S(2)}) %collective-permute-start.19) | collective-permute-done | bytes 81952 | tf_op jit(solution)/shard_map/ppermute | solution.py:390
  66.2 4.0 %query_side.2 = (bf16[320,128]{1,0:T(8,128)(2,1)S(1)}, bf16[320,128]{1,0:T(8,128)(2,1)S(1)}, bf16[320,128]{1,0:T(8,128)(2,1)S(1)}, bf16[320,128]{1,0:T(8,128)(2,1)S(1)}) custom-call(bf16[16,640,128]{2,1,0:T(8,128)(2,1)S(1)} %get-tuple-element.51.refs_0_, bf16[384,1152]{1,0:T(8,128)(2,1)S(1)} %get-tuple-element.50.refs_1_.refs_2_, ...), custom_call_target="tpu_custom_call" | custom-call | flops 20000000000 | bytes 80000000 | tf_op jit(solution)/shard_map/query_side/pallas_call | solution.py:402
  70.2 0.7 pack_momentum.1
  70.9 0.2 collective-permute-start.27
  71.1 2.3 %collective-permute-start.28 = (bf16[512,128]{1,0:T(8,128)(2,1)S(1)}, bf16[512,128]{1,0:T(8,128)(2,1)S(1)}, u32[]{:S(2)}, u32[]{:S(2)}) collective-permute-start(bf16[512,128]{1,0:T(8,128)(2,1)S(1)} %get-tuple-element.73), channel_id=1, source_target_pairs={{0,6},{1,7},{2,4},{3,5},{4,2},{5,3},{6,0},{7,1},{8,14},{9,15},{10,... | collective-permute-start | bytes 393224 | tf_op jit(solution)/shard_map/ppermute | solution.py:390
  73.4 1.0 %collective-permute-start.29 = (bf16[512,128]{1,0:T(8,128)(2,1)S(1)}, bf16[512,128]{1,0:T(8,128)(2,1)S(1)}, u32[]{:S(2)}, u32[]{:S(2)}) collective-permute-start(bf16[512,128]{1,0:T(8,128)(2,1)S(1)} %get-tuple-element.74), channel_id=1, source_target_pairs={{0,2},{1,3},{2,0},{3,1},{4,6},{5,7},{6,4},{7,5},{8,10},{9,11},{10,... | collective-permute-start | bytes 393224 | tf_op jit(solution)/shard_map/ppermute | solution.py:390
  74.4 1.5 %collective-permute-start.23 = (bf16[512,128]{1,0:T(8,128)(2,1)S(1)}, bf16[512,128]{1,0:T(8,128)(2,1)S(1)}, u32[]{:S(2)}, u32[]{:S(2)}) collective-permute-start(bf16[512,128]{1,0:T(8,128)(2,1)S(1)} %get-tuple-element.68), channel_id=1, source_target_pairs={{0,8},{1,9},{2,10},{3,11},{4,12},{5,13},{6,14},{7,15},{8,0},{9,1},... | collective-permute-start | bytes 393224 | tf_op jit(solution)/shard_map/ppermute | solution.py:390
  76.0 1.8 %collective-permute-start.24 = (bf16[512,128]{1,0:T(8,128)(2,1)S(1)}, bf16[512,128]{1,0:T(8,128)(2,1)S(1)}, u32[]{:S(2)}, u32[]{:S(2)}) collective-permute-start(bf16[512,128]{1,0:T(8,128)(2,1)S(1)} %get-tuple-element.69), channel_id=1, source_target_pairs={{0,10},{1,11},{2,8},{3,9},{4,14},{5,15},{6,12},{7,13},{8,2},{9,3},... | collective-permute-start | bytes 393224 | tf_op jit(solution)/shard_map/ppermute | solution.py:390
  77.8 1.2 %collective-permute-start.25 = (bf16[512,128]{1,0:T(8,128)(2,1)S(1)}, bf16[512,128]{1,0:T(8,128)(2,1)S(1)}, u32[]{:S(2)}, u32[]{:S(2)}) collective-permute-start(bf16[512,128]{1,0:T(8,128)(2,1)S(1)} %get-tuple-element.70), channel_id=1, source_target_pairs={{0,12},{1,13},{2,14},{3,15},{4,8},{5,9},{6,10},{7,11},{8,4},{9,5},... | collective-permute-start | bytes 393224 | tf_op jit(solution)/shard_map/ppermute | solution.py:390
  79.0 1.6 %collective-permute-done.28.refs_1_ = bf16[512,128]{1,0:T(8,128)(2,1)S(1)} collective-permute-done((bf16[512,128]{1,0:T(8,128)(2,1)S(1)}, bf16[512,128]{1,0:T(8,128)(2,1)S(1)}, u32[]{:S(2)}, u32[]{:S(2)}) %collective-permute-start.28) | collective-permute-done | bytes 131104 | tf_op jit(solution)/shard_map/ppermute | solution.py:390
  80.5 2.1 %collective-permute-start.26 = (bf16[512,128]{1,0:T(8,128)(2,1)S(1)}, bf16[512,128]{1,0:T(8,128)(2,1)S(1)}, u32[]{:S(2)}, u32[]{:S(2)}) collective-permute-start(bf16[512,128]{1,0:T(8,128)(2,1)S(1)} %get-tuple-element.71), channel_id=1, source_target_pairs={{0,14},{1,15},{2,12},{3,13},{4,10},{5,11},{6,8},{7,9},{8,6},{9,7},... | collective-permute-start | bytes 393224 | tf_op jit(solution)/shard_map/ppermute | solution.py:390
  82.6 1.3 %unpack.2 = (bf16[128,2560]{1,0:T(8,128)(2,1)}, f32[20,7680]{1,0:T(8,128)}, f32[20,7680]{1,0:T(8,128)}) custom-call(bf16[512,128]{1,0:T(8,128)(2,1)S(1)} %collective-permute-done.27.refs_0_, bf16[512,128]{1,0:T(8,128)(2,1)S(1)} %collective-permute-done.28.refs_1_, bf16[512,128]{1,0:T(8,128)(2,1)S(1)} %collective-permute-done.29.refs_2_, ...), custom_call_target="tpu_custom_call" | custom-call | flops 1000000000 | bytes 4000000 | tf_op jit(solution)/shard_map/unpack/pallas_call | solution.py:402
  83.9 7.1 %collective-permute-done.23.refs_0_ = bf16[512,128]{1,0:T(8,128)(2,1)S(1)} collective-permute-done((bf16[512,128]{1,0:T(8,128)(2,1)S(1)}, bf16[512,128]{1,0:T(8,128)(2,1)S(1)}, u32[]{:S(2)}, u32[]{:S(2)}) %collective-permute-start.23) | collective-permute-done | bytes 131104 | tf_op jit(solution)/shard_map/ppermute | solution.py:390
  91.1 2.8 %collective-permute-done.24.refs_1_ = bf16[512,128]{1,0:T(8,128)(2,1)S(1)} collective-permute-done((bf16[512,128]{1,0:T(8,128)(2,1)S(1)}, bf16[512,128]{1,0:T(8,128)(2,1)S(1)}, u32[]{:S(2)}, u32[]{:S(2)}) %collective-permute-start.24) | collective-permute-done | bytes 131104 | tf_op jit(solution)/shard_map/ppermute | solution.py:390
  93.9 3.5 %collective-permute-done.25.refs_2_ = bf16[512,128]{1,0:T(8,128)(2,1)S(1)} collective-permute-done((bf16[512,128]{1,0:T(8,128)(2,1)S(1)}, bf16[512,128]{1,0:T(8,128)(2,1)S(1)}, u32[]{:S(2)}, u32[]{:S(2)}) %collective-permute-start.25) | collective-permute-done | bytes 131104 | tf_op jit(solution)/shard_map/ppermute | solution.py:390
  97.4 3.3 %collective-permute-done.26.refs_3_ = bf16[512,128]{1,0:T(8,128)(2,1)S(1)} collective-permute-done((bf16[512,128]{1,0:T(8,128)(2,1)S(1)}, bf16[512,128]{1,0:T(8,128)(2,1)S(1)}, u32[]{:S(2)}, u32[]{:S(2)}) %collective-permute-start.26) | collective-permute-done | bytes 131104 | tf_op jit(solution)/shard_map/ppermute | solution.py:390
  100.7 1.3 %unpack.3 = (bf16[128,2560]{1,0:T(8,128)(2,1)}, f32[20,7680]{1,0:T(8,128)}, f32[20,7680]{1,0:T(8,128)}) custom-call(bf16[512,128]{1,0:T(8,128)(2,1)S(1)} %collective-permute-done.23.refs_0_, bf16[512,128]{1,0:T(8,128)(2,1)S(1)} %collective-permute-done.24.refs_1_, ...), custom_call_target="tpu_custom_call", output_to_operand_aliasing={{0}: (5, {}), {1}: (6, {}), {2}: (7, {})} | custom-call | flops 1000000000 | bytes 4000000 | tf_op jit(solution)/shard_map/unpack/pallas_call | solution.py:402
  (48 shorter events, 1.0 us)
Async XLA Ops:
  0.6 1.1 %copy-start = (f32[20,7680]{1,0:T(8,128)S(1)}, f32[20,7680]{1,0:T(8,128)}, u32[]{:S(2)}) copy-start(f32[20,7680]{1,0:T(8,128)} %refs_4_.3) | copy-start | bytes 1843204
  1.7 1.1 %copy-start.3 = (bf16[128,2560]{1,0:T(8,128)(2,1)S(1)}, bf16[128,2560]{1,0:T(8,128)(2,1)}, u32[]{:S(2)}) copy-start(bf16[128,2560]{1,0:T(8,128)(2,1)} %k_hbm.3) | copy-start | bytes 1966084
  2.8 1.1 %copy-start.4 = (bf16[128,2560]{1,0:T(8,128)(2,1)S(1)}, bf16[128,2560]{1,0:T(8,128)(2,1)}, u32[]{:S(2)}) copy-start(bf16[128,2560]{1,0:T(8,128)(2,1)} %v_hbm.3) | copy-start | bytes 1966084
  3.9 0.7 copy-start.6
  4.6 5.0 %copy-start.2 = (bf16[128,2560]{1,0:T(8,128)(2,1)S(1)}, bf16[128,2560]{1,0:T(8,128)(2,1)}, u32[]{:S(2)}) copy-start(bf16[128,2560]{1,0:T(8,128)(2,1)} %q_ref.1) | copy-start | bytes 1966084
  5.1 8.3 %copy-start.5 = (bf16[128,2560]{1,0:T(8,128)(2,1)S(1)}, bf16[128,2560]{1,0:T(8,128)(2,1)}, u32[]{:S(2)}) copy-start(bf16[128,2560]{1,0:T(8,128)(2,1)} %v_hbm.3) | copy-start | bytes 1966084
  5.1 24.7 %collective-permute-start = (bf16[832,128]{1,0:T(8,128)(2,1)S(1)}, bf16[832,128]{1,0:T(8,128)(2,1)S(1)}, u32[]{:S(2)}, u32[]{:S(2)}) collective-permute-start(bf16[832,128]{1,0:T(8,128)(2,1)S(1)} %get-tuple-element.41), channel_id=1, source_target_pairs={{0,8},{1,9},{2,10},{3,11},{4,12},{5,13},{6,14},{7,15},{8,0},{9,1},... | collective-permute-start | bytes 638984 | tf_op jit(solution)/shard_map/ppermute | solution.py:390
  7.8 27.4 %collective-permute-start.1 = (bf16[832,128]{1,0:T(8,128)(2,1)S(1)}, bf16[832,128]{1,0:T(8,128)(2,1)S(1)}, u32[]{:S(2)}, u32[]{:S(2)}) collective-permute-start(bf16[832,128]{1,0:T(8,128)(2,1)S(1)} %get-tuple-element.42), channel_id=1, source_target_pairs={{0,10},{1,11},{2,8},{3,9},{4,14},{5,15},{6,12},{7,13},{8,2},{9,3},... | collective-permute-start | bytes 638984 | tf_op jit(solution)/shard_map/ppermute | solution.py:390
  8.1 32.6 %collective-permute-start.2 = (bf16[832,128]{1,0:T(8,128)(2,1)S(1)}, bf16[832,128]{1,0:T(8,128)(2,1)S(1)}, u32[]{:S(2)}, u32[]{:S(2)}) collective-permute-start(bf16[832,128]{1,0:T(8,128)(2,1)S(1)} %get-tuple-element.43), channel_id=1, source_target_pairs={{0,12},{1,13},{2,14},{3,15},{4,8},{5,9},{6,10},{7,11},{8,4},{9,5},... | collective-permute-start | bytes 638984 | tf_op jit(solution)/shard_map/ppermute | solution.py:390
  9.8 15.5 %collective-permute-start.20 = (bf16[320,128]{1,0:T(8,128)(2,1)S(1)}, bf16[320,128]{1,0:T(8,128)(2,1)S(1)}, u32[]{:S(2)}, u32[]{:S(2)}) collective-permute-start(bf16[320,128]{1,0:T(8,128)(2,1)S(1)} %get-tuple-element.60), channel_id=1, source_target_pairs={{0,4},{1,5},{2,6},{3,7},{4,0},{5,1},{6,2},{7,3},{8,12},{9,13},{10,... | collective-permute-start | bytes 245768 | tf_op jit(solution)/shard_map/ppermute | solution.py:390
  12.4 32.4 %copy-start.7 = (f32[2560]{0:T(1024)S(1)}, f32[2560]{0:T(1024)}, u32[]{:S(2)}) copy-start(f32[2560]{0:T(1024)} %param.13) | copy-start | bytes 30724
  12.4 32.5 %copy-start.8 = (f32[2560]{0:T(1024)S(1)}, f32[2560]{0:T(1024)}, u32[]{:S(2)}) copy-start(f32[2560]{0:T(1024)} %param.12) | copy-start | bytes 30724
  12.4 13.7 %collective-permute-start.21 = (bf16[320,128]{1,0:T(8,128)(2,1)S(1)}, bf16[320,128]{1,0:T(8,128)(2,1)S(1)}, u32[]{:S(2)}, u32[]{:S(2)}) collective-permute-start(bf16[320,128]{1,0:T(8,128)(2,1)S(1)} %get-tuple-element.61), channel_id=1, source_target_pairs={{0,6},{1,7},{2,4},{3,5},{4,2},{5,3},{6,0},{7,1},{8,14},{9,15},{10,... | collective-permute-start | bytes 245768 | tf_op jit(solution)/shard_map/ppermute | solution.py:390
  25.3 19.0 %collective-permute-start.3 = (bf16[832,128]{1,0:T(8,128)(2,1)S(1)}, bf16[832,128]{1,0:T(8,128)(2,1)S(1)}, u32[]{:S(2)}, u32[]{:S(2)}) collective-permute-start(bf16[832,128]{1,0:T(8,128)(2,1)S(1)} %get-tuple-element.44), channel_id=1, source_target_pairs={{0,14},{1,15},{2,12},{3,13},{4,10},{5,11},{6,8},{7,9},{8,6},{9,7},... | collective-permute-start | bytes 638984 | tf_op jit(solution)/shard_map/ppermute | solution.py:390
  26.1 18.2 %collective-permute-start.4 = (bf16[832,128]{1,0:T(8,128)(2,1)S(1)}, bf16[832,128]{1,0:T(8,128)(2,1)S(1)}, u32[]{:S(2)}, u32[]{:S(2)}) collective-permute-start(bf16[832,128]{1,0:T(8,128)(2,1)S(1)} %get-tuple-element.45), channel_id=1, source_target_pairs={{0,4},{1,5},{2,6},{3,7},{4,0},{5,1},{6,2},{7,3},{8,12},{9,13},{10,... | collective-permute-start | bytes 638984 | tf_op jit(solution)/shard_map/ppermute | solution.py:390
  29.8 15.2 %collective-permute-start.5 = (bf16[832,128]{1,0:T(8,128)(2,1)S(1)}, bf16[832,128]{1,0:T(8,128)(2,1)S(1)}, u32[]{:S(2)}, u32[]{:S(2)}) collective-permute-start(bf16[832,128]{1,0:T(8,128)(2,1)S(1)} %get-tuple-element.46), channel_id=1, source_target_pairs={{0,6},{1,7},{2,4},{3,5},{4,2},{5,3},{6,0},{7,1},{8,14},{9,15},{10,... | collective-permute-start | bytes 638984 | tf_op jit(solution)/shard_map/ppermute | solution.py:390
  35.2 13.6 %collective-permute-start.6 = (bf16[832,128]{1,0:T(8,128)(2,1)S(1)}, bf16[832,128]{1,0:T(8,128)(2,1)S(1)}, u32[]{:S(2)}, u32[]{:S(2)}) collective-permute-start(bf16[832,128]{1,0:T(8,128)(2,1)S(1)} %get-tuple-element.47), channel_id=1, source_target_pairs={{0,2},{1,3},{2,0},{3,1},{4,6},{5,7},{6,4},{7,5},{8,10},{9,11},{10,... | collective-permute-start | bytes 638984 | tf_op jit(solution)/shard_map/ppermute | solution.py:390
  40.6 8.1 %collective-permute-start.14 = (bf16[832,128]{1,0:T(8,128)(2,1)S(1)}, bf16[832,128]{1,0:T(8,128)(2,1)S(1)}, u32[]{:S(2)}, u32[]{:S(2)}) collective-permute-start(bf16[832,128]{1,0:T(8,128)(2,1)S(1)} %get-tuple-element.48.refs_7_), channel_id=1, source_target_pairs={{0,1},{1,0},{2,3},{3,2},{4,5},{5,4},{6,7},{7,6},{8,9},{9,8},{10,11... | collective-permute-start | bytes 638984 | tf_op jit(solution)/shard_map/ppermute | solution.py:390
  44.2 5.0 %collective-permute-start.7 = (bf16[832,128]{1,0:T(8,128)(2,1)S(1)}, bf16[832,128]{1,0:T(8,128)(2,1)S(1)}, u32[]{:S(2)}, u32[]{:S(2)}) collective-permute-start(bf16[832,128]{1,0:T(8,128)(2,1)S(1)} %collective-permute-done.refs_0_), channel_id=1, source_target_pairs={{0,1},{1,0},{2,3},{3,2},{4,5},{5,4},{6,7},{7,6},{8,9},{9,8},{10,11... | collective-permute-start | bytes 638984 | tf_op jit(solution)/shard_map/ppermute | solution.py:390
  44.3 5.0 %collective-permute-start.8 = (bf16[832,128]{1,0:T(8,128)(2,1)S(1)}, bf16[832,128]{1,0:T(8,128)(2,1)S(1)}, u32[]{:S(2)}, u32[]{:S(2)}) collective-permute-start(bf16[832,128]{1,0:T(8,128)(2,1)S(1)} %collective-permute-done.1.refs_1_), channel_id=1, source_target_pairs={{0,1},{1,0},{2,3},{3,2},{4,5},{5,4},{6,7},{7,6},{8,9},{9,8},{10,11... | collective-permute-start | bytes 638984 | tf_op jit(solution)/shard_map/ppermute | solution.py:390
  45.1 4.7 %collective-permute-start.9 = (bf16[832,128]{1,0:T(8,128)(2,1)S(1)}, bf16[832,128]{1,0:T(8,128)(2,1)S(1)}, u32[]{:S(2)}, u32[]{:S(2)}) collective-permute-start(bf16[832,128]{1,0:T(8,128)(2,1)S(1)} %collective-permute-done.2.refs_2_), channel_id=1, source_target_pairs={{0,1},{1,0},{2,3},{3,2},{4,5},{5,4},{6,7},{7,6},{8,9},{9,8},{10,11... | collective-permute-start | bytes 638984 | tf_op jit(solution)/shard_map/ppermute | solution.py:390
  48.7 2.5 %collective-permute-start.10 = (bf16[832,128]{1,0:T(8,128)(2,1)S(1)}, bf16[832,128]{1,0:T(8,128)(2,1)S(1)}, u32[]{:S(2)}, u32[]{:S(2)}) collective-permute-start(bf16[832,128]{1,0:T(8,128)(2,1)S(1)} %collective-permute-done.3.refs_3_), channel_id=1, source_target_pairs={{0,1},{1,0},{2,3},{3,2},{4,5},{5,4},{6,7},{7,6},{8,9},{9,8},{10,11... | collective-permute-start | bytes 638984 | tf_op jit(solution)/shard_map/ppermute | solution.py:390
  48.7 4.9 %collective-permute-start.11 = (bf16[832,128]{1,0:T(8,128)(2,1)S(1)}, bf16[832,128]{1,0:T(8,128)(2,1)S(1)}, u32[]{:S(2)}, u32[]{:S(2)}) collective-permute-start(bf16[832,128]{1,0:T(8,128)(2,1)S(1)} %collective-permute-done.4.refs_4_), channel_id=1, source_target_pairs={{0,1},{1,0},{2,3},{3,2},{4,5},{5,4},{6,7},{7,6},{8,9},{9,8},{10,11... | collective-permute-start | bytes 638984 | tf_op jit(solution)/shard_map/ppermute | solution.py:390
  49.2 4.9 %collective-permute-start.12 = (bf16[832,128]{1,0:T(8,128)(2,1)S(1)}, bf16[832,128]{1,0:T(8,128)(2,1)S(1)}, u32[]{:S(2)}, u32[]{:S(2)}) collective-permute-start(bf16[832,128]{1,0:T(8,128)(2,1)S(1)} %collective-permute-done.5.refs_5_), channel_id=1, source_target_pairs={{0,1},{1,0},{2,3},{3,2},{4,5},{5,4},{6,7},{7,6},{8,9},{9,8},{10,11... | collective-permute-start | bytes 638984 | tf_op jit(solution)/shard_map/ppermute | solution.py:390
  49.3 6.4 %collective-permute-start.13 = (bf16[832,128]{1,0:T(8,128)(2,1)S(1)}, bf16[832,128]{1,0:T(8,128)(2,1)S(1)}, u32[]{:S(2)}, u32[]{:S(2)}) collective-permute-start(bf16[832,128]{1,0:T(8,128)(2,1)S(1)} %collective-permute-done.6.refs_6_), channel_id=1, source_target_pairs={{0,1},{1,0},{2,3},{3,2},{4,5},{5,4},{6,7},{7,6},{8,9},{9,8},{10,11... | collective-permute-start | bytes 638984 | tf_op jit(solution)/shard_map/ppermute | solution.py:390
  49.8 14.5 %collective-permute-start.16 = (bf16[320,128]{1,0:T(8,128)(2,1)S(1)}, bf16[320,128]{1,0:T(8,128)(2,1)S(1)}, u32[]{:S(2)}, u32[]{:S(2)}) collective-permute-start(bf16[320,128]{1,0:T(8,128)(2,1)S(1)} %get-tuple-element.52), channel_id=1, source_target_pairs={{0,8},{1,9},{2,10},{3,11},{4,12},{5,13},{6,14},{7,15},{8,0},{9,1},... | collective-permute-start | bytes 245768 | tf_op jit(solution)/shard_map/ppermute | solution.py:390
  51.2 13.0 %collective-permute-start.17 = (bf16[320,128]{1,0:T(8,128)(2,1)S(1)}, bf16[320,128]{1,0:T(8,128)(2,1)S(1)}, u32[]{:S(2)}, u32[]{:S(2)}) collective-permute-start(bf16[320,128]{1,0:T(8,128)(2,1)S(1)} %get-tuple-element.53), channel_id=1, source_target_pairs={{0,10},{1,11},{2,8},{3,9},{4,14},{5,15},{6,12},{7,13},{8,2},{9,3},... | collective-permute-start | bytes 245768 | tf_op jit(solution)/shard_map/ppermute | solution.py:390
  53.7 10.6 %collective-permute-start.18 = (bf16[320,128]{1,0:T(8,128)(2,1)S(1)}, bf16[320,128]{1,0:T(8,128)(2,1)S(1)}, u32[]{:S(2)}, u32[]{:S(2)}) collective-permute-start(bf16[320,128]{1,0:T(8,128)(2,1)S(1)} %get-tuple-element.54), channel_id=1, source_target_pairs={{0,12},{1,13},{2,14},{3,15},{4,8},{5,9},{6,10},{7,11},{8,4},{9,5},... | collective-permute-start | bytes 245768 | tf_op jit(solution)/shard_map/ppermute | solution.py:390
  54.1 12.1 %collective-permute-start.19 = (bf16[320,128]{1,0:T(8,128)(2,1)S(1)}, bf16[320,128]{1,0:T(8,128)(2,1)S(1)}, u32[]{:S(2)}, u32[]{:S(2)}) collective-permute-start(bf16[320,128]{1,0:T(8,128)(2,1)S(1)} %get-tuple-element.55), channel_id=1, source_target_pairs={{0,14},{1,15},{2,12},{3,13},{4,10},{5,11},{6,8},{7,9},{8,6},{9,7},... | collective-permute-start | bytes 245768 | tf_op jit(solution)/shard_map/ppermute | solution.py:390
  55.7 5.6 %collective-permute-start.22 = (bf16[320,128]{1,0:T(8,128)(2,1)S(1)}, bf16[320,128]{1,0:T(8,128)(2,1)S(1)}, u32[]{:S(2)}, u32[]{:S(2)}) collective-permute-start(bf16[320,128]{1,0:T(8,128)(2,1)S(1)} %get-tuple-element.62), channel_id=1, source_target_pairs={{0,2},{1,3},{2,0},{3,1},{4,6},{5,7},{6,4},{7,5},{8,10},{9,11},{10,... | collective-permute-start | bytes 245768 | tf_op jit(solution)/shard_map/ppermute | solution.py:390
  61.3 8.9 %collective-permute-start.15 = (f32[320,1152]{1,0:T(8,128)S(1)}, f32[320,1152]{1,0:T(8,128)S(1)}, u32[]{:S(2)}, u32[]{:S(2)}) collective-permute-start(f32[320,1152]{1,0:T(8,128)S(1)} %get-tuple-element.49.refs_0_), channel_id=1, source_target_pairs={{0,1},{1,0},{2,3},{3,2},{4,5},{5,4},{6,7},{7,6},{8,9},{9,8},{10,11... | collective-permute-start | bytes 4423688 | tf_op jit(solution)/shard_map/ppermute | solution.py:390
  70.2 12.4 %copy-start.1 = (f32[20,7680]{1,0:T(8,128)S(1)}, f32[20,7680]{1,0:T(8,128)}, u32[]{:S(2)}) copy-start(f32[20,7680]{1,0:T(8,128)} %refs_4_.3) | copy-start | bytes 1843204
  70.9 6.9 %collective-permute-start.27 = (bf16[512,128]{1,0:T(8,128)(2,1)S(1)}, bf16[512,128]{1,0:T(8,128)(2,1)S(1)}, u32[]{:S(2)}, u32[]{:S(2)}) collective-permute-start(bf16[512,128]{1,0:T(8,128)(2,1)S(1)} %get-tuple-element.72), channel_id=1, source_target_pairs={{0,4},{1,5},{2,6},{3,7},{4,0},{5,1},{6,2},{7,3},{8,12},{9,13},{10,... | collective-permute-start | bytes 393224 | tf_op jit(solution)/shard_map/ppermute | solution.py:390
  71.1 9.4 %collective-permute-start.28 = (bf16[512,128]{1,0:T(8,128)(2,1)S(1)}, bf16[512,128]{1,0:T(8,128)(2,1)S(1)}, u32[]{:S(2)}, u32[]{:S(2)}) collective-permute-start(bf16[512,128]{1,0:T(8,128)(2,1)S(1)} %get-tuple-element.73), channel_id=1, source_target_pairs={{0,6},{1,7},{2,4},{3,5},{4,2},{5,3},{6,0},{7,1},{8,14},{9,15},{10,... | collective-permute-start | bytes 393224 | tf_op jit(solution)/shard_map/ppermute | solution.py:390
  73.4 9.2 %collective-permute-start.29 = (bf16[512,128]{1,0:T(8,128)(2,1)S(1)}, bf16[512,128]{1,0:T(8,128)(2,1)S(1)}, u32[]{:S(2)}, u32[]{:S(2)}) collective-permute-start(bf16[512,128]{1,0:T(8,128)(2,1)S(1)} %get-tuple-element.74), channel_id=1, source_target_pairs={{0,2},{1,3},{2,0},{3,1},{4,6},{5,7},{6,4},{7,5},{8,10},{9,11},{10,... | collective-permute-start | bytes 393224 | tf_op jit(solution)/shard_map/ppermute | solution.py:390
  74.4 16.6 %collective-permute-start.23 = (bf16[512,128]{1,0:T(8,128)(2,1)S(1)}, bf16[512,128]{1,0:T(8,128)(2,1)S(1)}, u32[]{:S(2)}, u32[]{:S(2)}) collective-permute-start(bf16[512,128]{1,0:T(8,128)(2,1)S(1)} %get-tuple-element.68), channel_id=1, source_target_pairs={{0,8},{1,9},{2,10},{3,11},{4,12},{5,13},{6,14},{7,15},{8,0},{9,1},... | collective-permute-start | bytes 393224 | tf_op jit(solution)/shard_map/ppermute | solution.py:390
  76.0 17.9 %collective-permute-start.24 = (bf16[512,128]{1,0:T(8,128)(2,1)S(1)}, bf16[512,128]{1,0:T(8,128)(2,1)S(1)}, u32[]{:S(2)}, u32[]{:S(2)}) collective-permute-start(bf16[512,128]{1,0:T(8,128)(2,1)S(1)} %get-tuple-element.69), channel_id=1, source_target_pairs={{0,10},{1,11},{2,8},{3,9},{4,14},{5,15},{6,12},{7,13},{8,2},{9,3},... | collective-permute-start | bytes 393224 | tf_op jit(solution)/shard_map/ppermute | solution.py:390
  77.8 19.6 %collective-permute-start.25 = (bf16[512,128]{1,0:T(8,128)(2,1)S(1)}, bf16[512,128]{1,0:T(8,128)(2,1)S(1)}, u32[]{:S(2)}, u32[]{:S(2)}) collective-permute-start(bf16[512,128]{1,0:T(8,128)(2,1)S(1)} %get-tuple-element.70), channel_id=1, source_target_pairs={{0,12},{1,13},{2,14},{3,15},{4,8},{5,9},{6,10},{7,11},{8,4},{9,5},... | collective-permute-start | bytes 393224 | tf_op jit(solution)/shard_map/ppermute | solution.py:390
  80.5 20.2 %collective-permute-start.26 = (bf16[512,128]{1,0:T(8,128)(2,1)S(1)}, bf16[512,128]{1,0:T(8,128)(2,1)S(1)}, u32[]{:S(2)}, u32[]{:S(2)}) collective-permute-start(bf16[512,128]{1,0:T(8,128)(2,1)S(1)} %get-tuple-element.71), channel_id=1, source_target_pairs={{0,14},{1,15},{2,12},{3,13},{4,10},{5,11},{6,8},{7,9},{8,6},{9,7},... | collective-permute-start | bytes 393224 | tf_op jit(solution)/shard_map/ppermute | solution.py:390

commit v4 on v3

--- a/solution.py
+++ b/solution.py
@@ -12,11 +12,14 @@
 LANES = 128
 HALF = 64
 VMEM_LIMIT = 24 * 1024 * 1024
+FULL_VMEM = 58 * 1024 * 1024
 BF16 = jnp.bfloat16
 F32 = jnp.float32
 I32 = jnp.int32
 FAR = (4, 5, 6, 7)
 NEAR = (2, 3, 1, 0)
+BOTH = FAR + NEAR
+KEY_ORDER = (4, 5, 2, 3, 1, 6, 7, 0)
 HBM = pl.BlockSpec(memory_space=pltpu.HBM)
 ANY = pl.BlockSpec(memory_space=pl.ANY)
 VMEM = pl.BlockSpec(memory_space=pltpu.VMEM)
@@ -61,15 +64,15 @@
     return copies
 
 
-def pack_keys(width, heads, rows, slot, steps, k_hbm, v_hbm, step_ref, fw_hbm, *rest):
+def pack_keys(width, heads, rows, slot, steps, k_hbm, v_hbm, step_hbm, fw_hbm, *rest):
     few = heads // 2
-    outs, (k_ref, v_ref, fw_ref, pay, wbuf, sems) = rest[:few], rest[few:]
+    outs, (k_ref, v_ref, step_ref, fw_ref, pay, wbuf, sems) = rest[:few], rest[few:]
     chip, _ = chip_core(width)
     side = (chip ^ steps[0]) // few
     slab = k_ref.shape[1]
     matrix = fw_hbm.shape[1] // 3
     at = pl.multiple_of(side * slab, LANES)
-    pairs = [(k_hbm.at[:, pl.ds(at, slab)], k_ref), (v_hbm.at[:, pl.ds(at, slab)], v_ref)]
+    pairs = [(k_hbm.at[:, pl.ds(at, slab)], k_ref), (v_hbm.at[:, pl.ds(at, slab)], v_ref), (step_hbm, step_ref)]
     for m in range(3):
         lane = pl.multiple_of(side * slab + m * matrix, LANES)
         pairs.append((fw_hbm.at[:, pl.ds(lane, slab)], fw_ref.at[m]))
@@ -77,6 +80,7 @@
     tokens = k_ref.shape[0]
     low = low_lanes(tokens)
     low_r = low_lanes(rows)
+    share = pl.multiple_of(lax.rem(lax.axis_index("groups"), 2) * (4 * slot), 8)
     for copy in copies:
         copy.wait()
     wbuf[...] = jnp.zeros_like(wbuf)
@@ -107,10 +111,10 @@
         step = step_ref[pl.ds(side * few + head, 1)]
         high = step.astype(BF16).astype(F32)
         middle = (step - high).astype(BF16).astype(F32)
-        wbuf[head, rows : rows + 1] = high
-        wbuf[head, rows + 1 : rows + 2] = middle
-        wbuf[head, rows + 2 : rows + 3] = step - high - middle
-        pay[head, 5 * tokens :] = wbuf[head].astype(BF16)
+        wbuf[head, pl.ds(share + rows, 1)] = high
+        wbuf[head, pl.ds(share + rows + 1, 1)] = middle
+        wbuf[head, pl.ds(share + rows + 2, 1)] = step - high - middle
+        pay[head, 5 * tokens :] = wbuf[head, pl.ds(share, 4 * slot)].astype(BF16)
     for i, k in enumerate(steps):
         outs[i][...] = pay[lax.rem(chip ^ k, few)]
 
@@ -136,16 +140,24 @@
         outs[i][...] = pay[chip ^ k]
 
 
+def pack_weights(heads, tokens, *refs):
+    ins, out_ref = refs[:heads], refs[heads]
+    size = ins[0].shape[0] - 5 * tokens
+    for i, k in enumerate(KEY_ORDER):
+        out_ref[k * size : (k + 1) * size] = ins[i][5 * tokens :]
+
+
 def key_side(width, heads, rows, slot, tokens, scale, *refs):
     count = heads * width
     ins = refs[:count]
-    grad_ref, copy_ref, kv_ref = refs[count : count + 3]
-    gates, hidden, target = refs[count + 3 :]
+    shared = refs[count : count + width]
+    grad_ref, copy_ref, kv_ref = refs[count + width : count + width + 3]
+    gates, hidden, target = refs[count + width + 3 :]
     chip, core = chip_core(width)
     odd = lax.rem(chip, 2)
     wide = 3 * LANES
     size = rows * count
-    place = {k: i for i, k in enumerate(FAR + NEAR)}
+    place = {k: i for i, k in enumerate(KEY_ORDER)}
     blocks = [ins[other * heads + place[k]] for other in range(width) for k in range(heads)]
     for index, block in enumerate(blocks):
         other, k = divmod(index, heads)
@@ -156,11 +168,18 @@
     wanted = lax.broadcasted_iota(I32, (wide, count * slot), 0)
     chosen = (source * rows + row_in == natural_row(wanted, odd)) & (row_in < rows) & (wanted < size)
     chosen = jnp.where(chosen, 1.0, 0.0).astype(BF16)
+    size_4 = 4 * slot
+    others = [shared[i // heads][(i % heads) * size_4 : (i % heads + 1) * size_4].astype(F32) for i in range(count)]
     gathered = [
-        jnp.concatenate([part[t * slot : (t + 1) * slot] for part in parts], axis=0).astype(BF16) for t in range(8)
+        jnp.concatenate([part[t * slot : (t + 1) * slot] for part in source], axis=0).astype(BF16)
+        for source in (parts, others)
+        for t in range(4)
     ]
     placed = dot(chosen, jnp.concatenate(gathered, axis=1), ((1,), (0,)))
-    tile = [placed[:, t * LANES : (t + 1) * LANES] for t in range(8)]
+    mine, theirs = placed[:, : 4 * LANES], placed[:, 4 * LANES :]
+    first_share = lax.rem(lax.axis_index("groups"), 2) == 0
+    tile = [jnp.where(first_share, mine, theirs), jnp.where(first_share, theirs, mine)]
+    tile = [part[:, t * LANES : (t + 1) * LANES] for part in tile for t in range(4)]
     low = low_lanes(wide)
     columns = [tile[0], tile[1], jnp.where(low, tile[6], 0.0), tile[2], tile[3], tile[7]]
     columns += [jnp.where(low, 0.0, tile[6]), tile[4], tile[5]]
@@ -305,65 +324,51 @@
         outs[i][cut:] = pay[chip ^ k]
 
 
-def unpack(width, heads, rows, slot, tokens, steps, *refs):
-    few = heads // 2
-    pieces = refs[:few]
-    fw_hbm = refs[few]
-    layer_hbm, new_hbm, momentum_hbm, buf, fw_ref, layer_ref, new_ref, momentum_ref, in_sems, sems = refs[-10:]
+def unpack(width, heads, rows, slot, tokens, *refs):
+    pieces = refs[:heads]
+    fw_ref, layer_hbm, new_hbm, momentum_hbm, buf, layer_ref, new_ref, momentum_ref, sems = refs[heads:]
     chip, _ = chip_core(width)
-    side = (chip ^ steps[0]) // few
-    slab = layer_ref.shape[1]
-    matrix = fw_hbm.shape[1] // 3
-
-    def lanes(m):
-        return pl.ds(pl.multiple_of(side * slab + m * matrix, LANES), slab)
-
-    reads = copy_all([(fw_hbm.at[:, lanes(m)], fw_ref.at[m]) for m in range(3)], in_sems)
-    for i, k in enumerate(steps):
-        buf[lax.rem(chip ^ k, few)] = pieces[i][...]
+    matrix = fw_ref.shape[1] // 3
+    for i, k in enumerate(KEY_ORDER):
+        buf[chip ^ k] = pieces[i][...]
     mid = tokens // 2
     cut = 2 * tokens + mid
     low = low_lanes(mid)
     low_r = low_lanes(slot)
-    for head in range(few):
+
+    def write(lane, block):
+        moment = block[0:rows]
+        factor = block[rows : rows + 1] + block[rows + 1 : rows + 2]
+        momentum_ref[:, lane : lane + LANES] = moment
+        new_ref[:, lane : lane + LANES] = (fw_ref[:, lane : lane + LANES] - moment) * factor
+
+    moments = [buf[head, cut:].astype(F32) for head in range(heads)]
+    for head in range(heads):
+        whole, half = tiles_of(head)
+        for m in range(3):
+            for t in range(2):
+                write(m * matrix + whole + t * LANES, moments[head][(2 * m + t) * slot : (2 * m + t + 1) * slot])
+    for head in range(0, heads, 2):
+        _, half = tiles_of(head)
+        even = moments[head][6 * slot : 7 * slot]
+        odd = moments[head + 1][6 * slot : 7 * slot]
+        write(half, jnp.where(low_r, even, turned(odd)))
+        write(2 * matrix + half, jnp.where(low_r, turned(even), odd))
+        even = moments[head][7 * slot :]
+        odd = moments[head + 1][7 * slot :]
+        write(matrix + half, jnp.where(low_r, even, turned(odd)))
+    writes = copy_all([(new_ref, new_hbm), (momentum_ref, momentum_hbm)], sems)
+    for head in range(heads):
         whole, half = tiles_of(head)
         layer_ref[:, whole : whole + LANES] = buf[head, 0:tokens]
         layer_ref[:, whole + LANES : whole + 2 * LANES] = buf[head, tokens : 2 * tokens]
-    for head in range(0, few, 2):
+    for head in range(0, heads, 2):
         _, half = tiles_of(head)
         even = buf[head, 2 * tokens : cut].astype(F32)
         odd = buf[head + 1, 2 * tokens : cut].astype(F32)
         layer_ref[0:mid, half : half + LANES] = jnp.where(low, turned(even), odd).astype(BF16)
         layer_ref[mid:, half : half + LANES] = jnp.where(low, even, turned(odd)).astype(BF16)
-    writes = copy_all([(layer_ref, layer_hbm.at[:, lanes(0)])], sems)
-
-    for copy in reads:
-        copy.wait()
-
-    def write(m, lane, block):
-        moment = block[0:rows]
-        factor = block[rows : rows + 1] + block[rows + 1 : rows + 2]
-        momentum_ref[m, :, lane : lane + LANES] = moment
-        new_ref[m, :, lane : lane + LANES] = (fw_ref[m, :, lane : lane + LANES] - moment) * factor
-
-    moments = [buf[head, cut:].astype(F32) for head in range(few)]
-    for head in range(few):
-        whole, half = tiles_of(head)
-        for m in range(3):
-            for t in range(2):
-                write(m, whole + t * LANES, moments[head][(2 * m + t) * slot : (2 * m + t + 1) * slot])
-    for head in range(0, few, 2):
-        _, half = tiles_of(head)
-        even = moments[head][6 * slot : 7 * slot]
-        odd = moments[head + 1][6 * slot : 7 * slot]
-        write(0, half, jnp.where(low_r, even, turned(odd)))
-        write(2, half, jnp.where(low_r, turned(even), odd))
-        even = moments[head][7 * slot :]
-        odd = moments[head + 1][7 * slot :]
-        write(1, half, jnp.where(low_r, even, turned(odd)))
-    pairs = [(new_ref.at[m], new_hbm.at[:, lanes(m)]) for m in range(3)]
-    pairs += [(momentum_ref.at[m], momentum_hbm.at[:, lanes(m)]) for m in range(3)]
-    for copy in writes + copy_all(pairs, sems.at[pl.ds(1, 6)]):
+    for copy in writes + copy_all([(layer_ref, layer_hbm)], sems.at[pl.ds(2, 1)]):
         copy.wait()
 
 
@@ -380,9 +385,8 @@
     span = WINDOW // tokens
     wide = 3 * LANES
     slab = few * head_width
-    params = pltpu.CompilerParams(vmem_limit_bytes=VMEM_LIMIT)
     sem = pltpu.SemaphoreType.DMA
-    key_rows = 5 * tokens + 8 * slot
+    key_rows = 5 * tokens + 4 * slot
     query_rows = 2 * tokens + tokens // 2
     out_rows = query_rows + 8 * slot
 
@@ -398,7 +402,8 @@
     def cost(micros):
         return pl.CostEstimate(flops=micros * 500_000_000, transcendentals=0, bytes_accessed=micros * 2_000_000)
 
-    def call(body, name, micros, *operands, **kwargs):
+    def call(body, name, micros, *operands, grant=VMEM_LIMIT, **kwargs):
+        params = pltpu.CompilerParams(vmem_limit_bytes=grant)
         return pl.pallas_call(
             body, compiler_params=params, cost_estimate=cost(micros), name=name, **kwargs
         )(*operands)
@@ -414,22 +419,36 @@
             value_vectors,
             step_rows,
             fast_weights,
+            grant=FULL_VMEM if steps == FAR else VMEM_LIMIT,
             out_shape=packed(key_rows, few),
-            in_specs=[HBM, HBM, VMEM, HBM],
+            in_specs=[HBM] * 4,
             out_specs=[VMEM] * few,
             scratch_shapes=[
                 pltpu.VMEM((tokens, slab), BF16),
                 pltpu.VMEM((tokens, slab), BF16),
+                pltpu.VMEM((heads, tokens), F32),
                 pltpu.VMEM((3, rows, slab), F32),
                 pltpu.VMEM((few, key_rows, LANES), BF16),
                 pltpu.VMEM((few, 8 * slot, LANES), F32),
-                sem((5,)),
+                sem((6,)),
             ],
         )
 
-    key_blocks = exchange(keys_for(FAR), FAR) + exchange(keys_for(NEAR), NEAR)
+    key_pieces = dict(zip(BOTH, keys_for(FAR) + keys_for(NEAR)))
+    key_blocks = exchange([key_pieces[k] for k in KEY_ORDER], KEY_ORDER)
     for other in range(1, width):
         key_blocks = key_blocks + [across(block, other) for block in key_blocks[:heads]]
+    shared = call(
+        functools.partial(pack_weights, heads, tokens),
+        "pack_weights",
+        0,
+        *key_blocks[:heads],
+        out_shape=jax.ShapeDtypeStruct((heads * 4 * slot, LANES), BF16),
+        in_specs=[VMEM] * heads,
+        out_specs=VMEM,
+    )
+    shared = lax.ppermute(shared, "groups", [(i, i ^ 1) for i in range(lax.axis_size("groups"))])
+    shared = [shared] + [across(shared, other) for other in range(1, width)]
     query_pieces = call(
         functools.partial(pack_queries, width, heads),
         "pack_queries",
@@ -447,12 +466,13 @@
         "key_side",
         0,
         *key_blocks,
+        *shared,
         out_shape=[
             jax.ShapeDtypeStruct((head_width, 3 * wide), F32),
             jax.ShapeDtypeStruct((wide, 3 * wide), BF16),
             jax.ShapeDtypeStruct((count, 5 * tokens, LANES), BF16),
         ],
-        in_specs=[VMEM] * count,
+        in_specs=[VMEM] * (count + width),
         out_specs=[VMEM] * 3,
         scratch_shapes=[
             pltpu.VMEM((heads * tokens, 2 * wide), BF16),
@@ -508,36 +528,32 @@
         out_specs=[VMEM] * heads,
         scratch_shapes=[pltpu.VMEM((heads, 8 * slot, LANES), BF16)],
     )
-    pieces = exchange(pieces, FAR + NEAR)
-
-    def outputs_of(steps, blocks, *before):
-        return call(
-            functools.partial(unpack, width, heads, rows, slot, tokens, steps),
+    pieces = dict(zip(BOTH, pieces))
+    pieces = exchange([pieces[k] for k in KEY_ORDER], KEY_ORDER)
+
+    return tuple(
+        call(
+            functools.partial(unpack, width, heads, rows, slot, tokens),
             "unpack",
             2,
-            *blocks,
+            *pieces,
             fast_weights,
-            *before,
             out_shape=[
                 jax.ShapeDtypeStruct(queries.shape, BF16),
                 jax.ShapeDtypeStruct(fast_weights.shape, F32),
                 jax.ShapeDtypeStruct(fast_weights.shape, F32),
             ],
-            in_specs=[VMEM] * few + [HBM] * (1 + len(before)),
+            in_specs=[VMEM] * (heads + 1),
             out_specs=[HBM] * 3,
             scratch_shapes=[
-                pltpu.VMEM((few, out_rows, LANES), BF16),
-                pltpu.VMEM((3, rows, slab), F32),
-                pltpu.VMEM((tokens, slab), BF16),
-                pltpu.VMEM((3, rows, slab), F32),
-                pltpu.VMEM((3, rows, slab), F32),
+                pltpu.VMEM((heads, out_rows, LANES), BF16),
+                pltpu.VMEM(queries.shape, BF16),
+                pltpu.VMEM(fast_weights.shape, F32),
+                pltpu.VMEM(fast_weights.shape, F32),
                 sem((3,)),
-                sem((7,)),
             ],
-            input_output_aliases={few + 1 + i: i for i in range(len(before))},
         )
-
-    return tuple(outputs_of(FAR, pieces[:few], *outputs_of(NEAR, pieces[few:])))
+    )
 
 
 def solution(mesh):

time: 102 us -> 95.7 us (0.938)
  the two profiles are of different devices: /device:TPU:12 before, /device:TPU:0 now
where the time goes in v4:
time: 95.7 us; the launch traced here: 95.1 us
  starting transfers between devices  48.3 us (50%)
  waiting for transfers between devices  28.6 us (30%)
  Pallas kernels  16.7 us (17%)
  between operations  1.03 us (1%)
    ppermute x31, starting transfers between devices, across(): return lax.ppermute(value, 'seq', [(i, i ^ step) for i in range(count)])  46.7 us
    ppermute x31, waiting for transfers between devices, across(): return lax.ppermute(value, 'seq', [(i, i ^ step) for i in range(count)])  26.9 us
    pallas_call x9, Pallas kernels, call(): pl.pallas_call(body, compiler_params=params, cost_estimate=cost(micros),...  16.7 us
  transfers between devices with their start and end apart: 32, of which 10 were waited for; matrix products, arithmetic and copies ran while one was open for 0% of the time, Pallas kernels for 12%

profile of v4, /device:TPU:0, one launch (start us, length us, event | category | flops | bytes accessed | tf_op | source)
XLA Modules:
  0.0 95.1 jit_solution(4629445004949426282)
XLA Ops:
  0.7 2.5 %pack_keys.2 = (bf16[736,128]{1,0:T(8,128)(2,1)}, bf16[736,128]{1,0:T(8,128)(2,1)}, bf16[736,128]{1,0:T(8,128)(2,1)}, bf16[736,128]{1,0:T(8,128)(2,1)}) custom-call(bf16[128,2560]{1,0:T(8,128)(2,1)} %k_hbm.3, bf16[128,2560]{1,0:T(8,128)(2,1)} %v_hbm.3, f32[8,128]{1,0:T(8,128)} %bitcast.1, f32[20,7680]{1,0:T(8,128)} %refs_8_.1), custom_call_target="tpu_custom_call" | custom-call | flops 1000000000 | bytes 4000000 | tf_op jit(solution)/shard_map/pack_keys/pallas_call | solution.py:407
  3.2 4.1 %collective-permute-start = (bf16[736,128]{1,0:T(8,128)(2,1)}, bf16[736,128]{1,0:T(8,128)(2,1)S(1)}, u32[]{:S(2)}, u32[]{:S(2)}) collective-permute-start(bf16[736,128]{1,0:T(8,128)(2,1)} %get-tuple-element.38), channel_id=1, source_target_pairs={{0,8},{1,9},{2,10},{3,11},{4,12},{5,13},{6,14},{7,15},{8,0},{9,1},... | collective-permute-start | bytes 565256 | tf_op jit(solution)/shard_map/ppermute | solution.py:394
  7.3 1.3 %collective-permute-start.1 = (bf16[736,128]{1,0:T(8,128)(2,1)}, bf16[736,128]{1,0:T(8,128)(2,1)S(1)}, u32[]{:S(2)}, u32[]{:S(2)}) collective-permute-start(bf16[736,128]{1,0:T(8,128)(2,1)} %get-tuple-element.39), channel_id=1, source_target_pairs={{0,10},{1,11},{2,8},{3,9},{4,14},{5,15},{6,12},{7,13},{8,2},{9,3},... | collective-permute-start | bytes 565256 | tf_op jit(solution)/shard_map/ppermute | solution.py:394
  8.6 0.6 pack_keys.3
  9.1 1.6 %collective-permute-start.2 = (bf16[736,128]{1,0:T(8,128)(2,1)S(1)}, bf16[736,128]{1,0:T(8,128)(2,1)S(1)}, u32[]{:S(2)}, u32[]{:S(2)}) collective-permute-start(bf16[736,128]{1,0:T(8,128)(2,1)S(1)} %get-tuple-element.40), channel_id=1, source_target_pairs={{0,4},{1,5},{2,6},{3,7},{4,0},{5,1},{6,2},{7,3},{8,12},{9,13},{10,... | collective-permute-start | bytes 565256 | tf_op jit(solution)/shard_map/ppermute | solution.py:394
  10.8 0.2 collective-permute-start.3
  10.9 1.7 %collective-permute-start.4 = (bf16[736,128]{1,0:T(8,128)(2,1)S(1)}, bf16[736,128]{1,0:T(8,128)(2,1)S(1)}, u32[]{:S(2)}, u32[]{:S(2)}) collective-permute-start(bf16[736,128]{1,0:T(8,128)(2,1)S(1)} %get-tuple-element.42), channel_id=1, source_target_pairs={{0,2},{1,3},{2,0},{3,1},{4,6},{5,7},{6,4},{7,5},{8,10},{9,11},{10,... | collective-permute-start | bytes 565256 | tf_op jit(solution)/shard_map/ppermute | solution.py:394
  12.7 8.5 %collective-permute-done.refs_0_ = bf16[736,128]{1,0:T(8,128)(2,1)S(1)} collective-permute-done((bf16[736,128]{1,0:T(8,128)(2,1)}, bf16[736,128]{1,0:T(8,128)(2,1)S(1)}, u32[]{:S(2)}, u32[]{:S(2)}) %collective-permute-start) | collective-permute-done | bytes 188448 | tf_op jit(solution)/shard_map/ppermute | solution.py:394
  21.2 2.8 %collective-permute-start.5 = (bf16[736,128]{1,0:T(8,128)(2,1)S(1)}, bf16[736,128]{1,0:T(8,128)(2,1)S(1)}, u32[]{:S(2)}, u32[]{:S(2)}) collective-permute-start(bf16[736,128]{1,0:T(8,128)(2,1)S(1)} %copy-done.9), channel_id=1, source_target_pairs={{0,12},{1,13},{2,14},{3,15},{4,8},{5,9},{6,10},{7,11},{8,4},{9,5},... | collective-permute-start | bytes 565256 | tf_op jit(solution)/shard_map/ppermute | solution.py:394
  24.0 3.1 %collective-permute-done.1.refs_1_ = bf16[736,128]{1,0:T(8,128)(2,1)S(1)} collective-permute-done((bf16[736,128]{1,0:T(8,128)(2,1)}, bf16[736,128]{1,0:T(8,128)(2,1)S(1)}, u32[]{:S(2)}, u32[]{:S(2)}) %collective-permute-start.1) | collective-permute-done | bytes 188448 | tf_op jit(solution)/shard_map/ppermute | solution.py:394
  27.2 1.7 %collective-permute-start.6 = (bf16[736,128]{1,0:T(8,128)(2,1)S(1)}, bf16[736,128]{1,0:T(8,128)(2,1)S(1)}, u32[]{:S(2)}, u32[]{:S(2)}) collective-permute-start(bf16[736,128]{1,0:T(8,128)(2,1)S(1)} %copy-done.8), channel_id=1, source_target_pairs={{0,14},{1,15},{2,12},{3,13},{4,10},{5,11},{6,8},{7,9},{8,6},{9,7},... | collective-permute-start | bytes 565256 | tf_op jit(solution)/shard_map/ppermute | solution.py:394
  28.9 0.2 pack_queries.1
  29.2 3.0 %collective-permute-start.23 = (bf16[320,128]{1,0:T(8,128)(2,1)S(1)}, bf16[320,128]{1,0:T(8,128)(2,1)S(1)}, u32[]{:S(2)}, u32[]{:S(2)}) collective-permute-start(bf16[320,128]{1,0:T(8,128)(2,1)S(1)} %get-tuple-element.58), channel_id=1, source_target_pairs={{0,6},{1,7},{2,4},{3,5},{4,2},{5,3},{6,0},{7,1},{8,14},{9,15},{10,... | collective-permute-start | bytes 245768 | tf_op jit(solution)/shard_map/ppermute | solution.py:394
  32.1 3.9 %collective-permute-done.6.refs_6_ = bf16[736,128]{1,0:T(8,128)(2,1)S(1)} collective-permute-done((bf16[736,128]{1,0:T(8,128)(2,1)S(1)}, bf16[736,128]{1,0:T(8,128)(2,1)S(1)}, u32[]{:S(2)}, u32[]{:S(2)}) %collective-permute-start.6) | collective-permute-done | bytes 188448 | tf_op jit(solution)/shard_map/ppermute | solution.py:394
  36.0 1.6 %collective-permute-start.15 = (bf16[768,128]{1,0:T(8,128)(2,1)S(1)}, bf16[768,128]{1,0:T(8,128)(2,1)S(1)}, u32[]{:S(2)}, u32[]{:S(2)}) collective-permute-start(bf16[768,128]{1,0:T(8,128)(2,1)S(1)} %pack_weights.1), channel_id=1, source_target_pairs={{0,16},{16,0},{1,17},{17,1},{2,18},{18,2},{3,19},{19,3},{4,20},{20... | collective-permute-start | bytes 589832 | tf_op jit(solution)/shard_map/ppermute | solution.py:450
  37.6 0.5 collective-permute-start.10
  38.1 0.5 collective-permute-start.12
  38.6 0.1 reshape.12
  38.7 0.1 reshape.13
  38.8 0.1 dynamic-slice
  38.9 0.1 dynamic-slice.2
  39.0 0.1 collective-permute-done.14.refs_15_
  39.0 0.1 collective-permute-start.13
  39.2 0.1 collective-permute-done.10.refs_11_
  39.3 0.2 collective-permute-start.7
  39.6 0.2 collective-permute-start.8
  39.9 0.2 collective-permute-start.9
  40.1 1.7 %collective-permute-done.15.refs_16_ = bf16[768,128]{1,0:T(8,128)(2,1)S(1)} collective-permute-done((bf16[768,128]{1,0:T(8,128)(2,1)S(1)}, bf16[768,128]{1,0:T(8,128)(2,1)S(1)}, u32[]{:S(2)}, u32[]{:S(2)}) %collective-permute-start.15) | collective-permute-done | bytes 196640 | tf_op jit(solution)/shard_map/ppermute | solution.py:450
  41.8 1.1 %collective-permute-start.24 = (bf16[320,128]{1,0:T(8,128)(2,1)S(1)}, bf16[320,128]{1,0:T(8,128)(2,1)S(1)}, u32[]{:S(2)}, u32[]{:S(2)}) collective-permute-start(bf16[320,128]{1,0:T(8,128)(2,1)S(1)} %get-tuple-element.59), channel_id=1, source_target_pairs={{0,2},{1,3},{2,0},{3,1},{4,6},{5,7},{6,4},{7,5},{8,10},{9,11},{10,... | collective-permute-start | bytes 245768 | tf_op jit(solution)/shard_map/ppermute | solution.py:394
  42.9 9.3 %collective-permute-start.18 = (bf16[320,128]{1,0:T(8,128)(2,1)S(1)}, bf16[320,128]{1,0:T(8,128)(2,1)S(1)}, u32[]{:S(2)}, u32[]{:S(2)}) collective-permute-start(bf16[320,128]{1,0:T(8,128)(2,1)S(1)} %get-tuple-element.49), channel_id=1, source_target_pairs={{0,8},{1,9},{2,10},{3,11},{4,12},{5,13},{6,14},{7,15},{8,0},{9,1},... | collective-permute-start | bytes 245768 | tf_op jit(solution)/shard_map/ppermute | solution.py:394
  52.2 0.6 collective-permute-start.19
  52.8 4.2 %collective-permute-start.21 = (bf16[320,128]{1,0:T(8,128)(2,1)S(1)}, bf16[320,128]{1,0:T(8,128)(2,1)S(1)}, u32[]{:S(2)}, u32[]{:S(2)}) collective-permute-start(bf16[320,128]{1,0:T(8,128)(2,1)S(1)} %get-tuple-element.52), channel_id=1, source_target_pairs={{0,14},{1,15},{2,12},{3,13},{4,10},{5,11},{6,8},{7,9},{8,6},{9,7},... | collective-permute-start | bytes 245768 | tf_op jit(solution)/shard_map/ppermute | solution.py:394
  57.1 4.2 %key_side.1 = (f32[320,1152]{1,0:T(8,128)S(1)}, bf16[384,1152]{1,0:T(8,128)(2,1)S(1)}, bf16[16,640,128]{2,1,0:T(8,128)(2,1)S(1)}) custom-call(bf16[736,128]{1,0:T(8,128)(2,1)S(1)} %collective-permute-done.refs_0_, bf16[736,128]{1,0:T(8,128)(2,1)S(1)} %collective-permute-done.1.refs_1_, bf16[736,128]{1,0:T(8,128)(2,1)S(1)} %collective-permute-done.2.refs_2_, ...), custom_call_target="tpu_custom_call" | custom-call | tf_op jit(solution)/shard_map/key_side/pallas_call | solution.py:407
  61.4 2.9 %query_side.3 = (bf16[320,128]{1,0:T(8,128)(2,1)S(1)}, bf16[320,128]{1,0:T(8,128)(2,1)S(1)}, bf16[320,128]{1,0:T(8,128)(2,1)S(1)}, bf16[320,128]{1,0:T(8,128)(2,1)S(1)}) custom-call(bf16[16,640,128]{2,1,0:T(8,128)(2,1)S(1)} %get-tuple-element.48.refs_0_, bf16[384,1152]{1,0:T(8,128)(2,1)S(1)} %get-tuple-element.47.refs_1_.refs_2_, ...), custom_call_target="tpu_custom_call" | custom-call | tf_op jit(solution)/shard_map/query_side/pallas_call | solution.py:407
  64.3 4.0 %query_side.2 = (bf16[320,128]{1,0:T(8,128)(2,1)S(1)}, bf16[320,128]{1,0:T(8,128)(2,1)S(1)}, bf16[320,128]{1,0:T(8,128)(2,1)S(1)}, bf16[320,128]{1,0:T(8,128)(2,1)S(1)}) custom-call(bf16[16,640,128]{2,1,0:T(8,128)(2,1)S(1)} %get-tuple-element.48.refs_0_, bf16[384,1152]{1,0:T(8,128)(2,1)S(1)} %get-tuple-element.47.refs_1_.refs_2_, ...), custom_call_target="tpu_custom_call" | custom-call | flops 20000000000 | bytes 80000000 | tf_op jit(solution)/shard_map/query_side/pallas_call | solution.py:407
  68.4 0.7 pack_momentum.1
  69.1 2.3 %collective-permute-start.25 = (bf16[512,128]{1,0:T(8,128)(2,1)S(1)}, bf16[512,128]{1,0:T(8,128)(2,1)S(1)}, u32[]{:S(2)}, u32[]{:S(2)}) collective-permute-start(bf16[512,128]{1,0:T(8,128)(2,1)S(1)} %get-tuple-element.65), channel_id=1, source_target_pairs={{0,8},{1,9},{2,10},{3,11},{4,12},{5,13},{6,14},{7,15},{8,0},{9,1},... | collective-permute-start | bytes 393224 | tf_op jit(solution)/shard_map/ppermute | solution.py:394
  71.4 1.2 %collective-permute-start.26 = (bf16[512,128]{1,0:T(8,128)(2,1)S(1)}, bf16[512,128]{1,0:T(8,128)(2,1)S(1)}, u32[]{:S(2)}, u32[]{:S(2)}) collective-permute-start(bf16[512,128]{1,0:T(8,128)(2,1)S(1)} %get-tuple-element.66), channel_id=1, source_target_pairs={{0,10},{1,11},{2,8},{3,9},{4,14},{5,15},{6,12},{7,13},{8,2},{9,3},... | collective-permute-start | bytes 393224 | tf_op jit(solution)/shard_map/ppermute | solution.py:394
  72.6 3.5 %collective-permute-start.27 = (bf16[512,128]{1,0:T(8,128)(2,1)S(1)}, bf16[512,128]{1,0:T(8,128)(2,1)S(1)}, u32[]{:S(2)}, u32[]{:S(2)}) collective-permute-start(bf16[512,128]{1,0:T(8,128)(2,1)S(1)} %get-tuple-element.67), channel_id=1, source_target_pairs={{0,4},{1,5},{2,6},{3,7},{4,0},{5,1},{6,2},{7,3},{8,12},{9,13},{10,... | collective-permute-start | bytes 393224 | tf_op jit(solution)/shard_map/ppermute | solution.py:394
  76.1 0.5 collective-permute-start.28
  76.7 0.9 collective-permute-start.29
  77.6 3.9 %collective-permute-done.25.refs_0_ = bf16[512,128]{1,0:T(8,128)(2,1)S(1)} collective-permute-done((bf16[512,128]{1,0:T(8,128)(2,1)S(1)}, bf16[512,128]{1,0:T(8,128)(2,1)S(1)}, u32[]{:S(2)}, u32[]{:S(2)}) %collective-permute-start.25) | collective-permute-done | bytes 131104 | tf_op jit(solution)/shard_map/ppermute | solution.py:394
  81.5 2.4 %collective-permute-start.30 = (bf16[512,128]{1,0:T(8,128)(2,1)S(1)}, bf16[512,128]{1,0:T(8,128)(2,1)S(1)}, u32[]{:S(2)}, u32[]{:S(2)}) collective-permute-start(bf16[512,128]{1,0:T(8,128)(2,1)S(1)} %get-tuple-element.70), channel_id=1, source_target_pairs={{0,12},{1,13},{2,14},{3,15},{4,8},{5,9},{6,10},{7,11},{8,4},{9,5},... | collective-permute-start | bytes 393224 | tf_op jit(solution)/shard_map/ppermute | solution.py:394
  83.8 1.5 %collective-permute-done.26.refs_1_ = bf16[512,128]{1,0:T(8,128)(2,1)S(1)} collective-permute-done((bf16[512,128]{1,0:T(8,128)(2,1)S(1)}, bf16[512,128]{1,0:T(8,128)(2,1)S(1)}, u32[]{:S(2)}, u32[]{:S(2)}) %collective-permute-start.26) | collective-permute-done | bytes 131104 | tf_op jit(solution)/shard_map/ppermute | solution.py:394
  85.4 2.1 %collective-permute-start.31 = (bf16[512,128]{1,0:T(8,128)(2,1)S(1)}, bf16[512,128]{1,0:T(8,128)(2,1)S(1)}, u32[]{:S(2)}, u32[]{:S(2)}) collective-permute-start(bf16[512,128]{1,0:T(8,128)(2,1)S(1)} %get-tuple-element.71), channel_id=1, source_target_pairs={{0,14},{1,15},{2,12},{3,13},{4,10},{5,11},{6,8},{7,9},{8,6},{9,7},... | collective-permute-start | bytes 393224 | tf_op jit(solution)/shard_map/ppermute | solution.py:394
  87.5 3.1 %collective-permute-done.30.refs_5_ = bf16[512,128]{1,0:T(8,128)(2,1)S(1)} collective-permute-done((bf16[512,128]{1,0:T(8,128)(2,1)S(1)}, bf16[512,128]{1,0:T(8,128)(2,1)S(1)}, u32[]{:S(2)}, u32[]{:S(2)}) %collective-permute-start.30) | collective-permute-done | bytes 131104 | tf_op jit(solution)/shard_map/ppermute | solution.py:394
  90.6 2.6 %collective-permute-done.31.refs_6_ = bf16[512,128]{1,0:T(8,128)(2,1)S(1)} collective-permute-done((bf16[512,128]{1,0:T(8,128)(2,1)S(1)}, bf16[512,128]{1,0:T(8,128)(2,1)S(1)}, u32[]{:S(2)}, u32[]{:S(2)}) %collective-permute-start.31) | collective-permute-done | bytes 131104 | tf_op jit(solution)/shard_map/ppermute | solution.py:394
  93.2 1.7 %unpack.1 = (bf16[128,2560]{1,0:T(8,128)(2,1)}, f32[20,7680]{1,0:T(8,128)}, f32[20,7680]{1,0:T(8,128)}) custom-call(bf16[512,128]{1,0:T(8,128)(2,1)S(1)} %collective-permute-done.25.refs_0_, bf16[512,128]{1,0:T(8,128)(2,1)S(1)} %collective-permute-done.26.refs_1_, bf16[512,128]{1,0:T(8,128)(2,1)S(1)} %collective-permute-done.27.refs_2_, ...), custom_call_target="tpu_custom_call" | custom-call | flops 1000000000 | bytes 4000000 | tf_op jit(solution)/shard_map/unpack/pallas_call | solution.py:407
  (54 shorter events, 0.4 us)
Async XLA Ops:
  0.6 7.9 %copy-start = (f32[20,7680]{1,0:T(8,128)S(1)}, f32[20,7680]{1,0:T(8,128)}, u32[]{:S(2)}) copy-start(f32[20,7680]{1,0:T(8,128)} %refs_8_.1) | copy-start | bytes 1843204
  0.6 7.9 %copy-start.2 = (bf16[128,2560]{1,0:T(8,128)(2,1)S(1)}, bf16[128,2560]{1,0:T(8,128)(2,1)}, u32[]{:S(2)}) copy-start(bf16[128,2560]{1,0:T(8,128)(2,1)} %k_hbm.3) | copy-start | bytes 1966084
  0.7 7.9 %copy-start.3 = (bf16[128,2560]{1,0:T(8,128)(2,1)S(1)}, bf16[128,2560]{1,0:T(8,128)(2,1)}, u32[]{:S(2)}) copy-start(bf16[128,2560]{1,0:T(8,128)(2,1)} %v_hbm.3) | copy-start | bytes 1966084
  0.7 7.9 %copy-start.5 = (f32[128,8]{0,1:T(8,128)S(1)}, f32[128,8]{0,1:T(8,128)}, u32[]{:S(2)}) copy-start(f32[128,8]{0,1:T(8,128)} %param.10) | copy-start | bytes 12292
  3.2 18.0 %collective-permute-start = (bf16[736,128]{1,0:T(8,128)(2,1)}, bf16[736,128]{1,0:T(8,128)(2,1)S(1)}, u32[]{:S(2)}, u32[]{:S(2)}) collective-permute-start(bf16[736,128]{1,0:T(8,128)(2,1)} %get-tuple-element.38), channel_id=1, source_target_pairs={{0,8},{1,9},{2,10},{3,11},{4,12},{5,13},{6,14},{7,15},{8,0},{9,1},... | collective-permute-start | bytes 565256 | tf_op jit(solution)/shard_map/ppermute | solution.py:394
  7.3 13.9 %copy-start.9 = (bf16[736,128]{1,0:T(8,128)(2,1)S(1)}, bf16[736,128]{1,0:T(8,128)(2,1)}, u32[]{:S(2)}) copy-start(bf16[736,128]{1,0:T(8,128)(2,1)} %get-tuple-element.43) | copy-start | bytes 565252
  7.3 19.9 %copy-start.8 = (bf16[736,128]{1,0:T(8,128)(2,1)S(1)}, bf16[736,128]{1,0:T(8,128)(2,1)}, u32[]{:S(2)}) copy-start(bf16[736,128]{1,0:T(8,128)(2,1)} %get-tuple-element.44) | copy-start | bytes 565252
  7.3 21.6 %copy-start.4 = (bf16[128,2560]{1,0:T(8,128)(2,1)S(1)}, bf16[128,2560]{1,0:T(8,128)(2,1)}, u32[]{:S(2)}) copy-start(bf16[128,2560]{1,0:T(8,128)(2,1)} %q_ref.1) | copy-start | bytes 1966084
  7.3 19.9 %collective-permute-start.1 = (bf16[736,128]{1,0:T(8,128)(2,1)}, bf16[736,128]{1,0:T(8,128)(2,1)S(1)}, u32[]{:S(2)}, u32[]{:S(2)}) collective-permute-start(bf16[736,128]{1,0:T(8,128)(2,1)} %get-tuple-element.39), channel_id=1, source_target_pairs={{0,10},{1,11},{2,8},{3,9},{4,14},{5,15},{6,12},{7,13},{8,2},{9,3},... | collective-permute-start | bytes 565256 | tf_op jit(solution)/shard_map/ppermute | solution.py:394
  9.1 19.9 %collective-permute-start.2 = (bf16[736,128]{1,0:T(8,128)(2,1)S(1)}, bf16[736,128]{1,0:T(8,128)(2,1)S(1)}, u32[]{:S(2)}, u32[]{:S(2)}) collective-permute-start(bf16[736,128]{1,0:T(8,128)(2,1)S(1)} %get-tuple-element.40), channel_id=1, source_target_pairs={{0,4},{1,5},{2,6},{3,7},{4,0},{5,1},{6,2},{7,3},{8,12},{9,13},{10,... | collective-permute-start | bytes 565256 | tf_op jit(solution)/shard_map/ppermute | solution.py:394
  10.8 18.4 %collective-permute-start.3 = (bf16[736,128]{1,0:T(8,128)(2,1)S(1)}, bf16[736,128]{1,0:T(8,128)(2,1)S(1)}, u32[]{:S(2)}, u32[]{:S(2)}) collective-permute-start(bf16[736,128]{1,0:T(8,128)(2,1)S(1)} %get-tuple-element.41), channel_id=1, source_target_pairs={{0,6},{1,7},{2,4},{3,5},{4,2},{5,3},{6,0},{7,1},{8,14},{9,15},{10,... | collective-permute-start | bytes 565256 | tf_op jit(solution)/shard_map/ppermute | solution.py:394
  10.9 21.2 %collective-permute-start.4 = (bf16[736,128]{1,0:T(8,128)(2,1)S(1)}, bf16[736,128]{1,0:T(8,128)(2,1)S(1)}, u32[]{:S(2)}, u32[]{:S(2)}) collective-permute-start(bf16[736,128]{1,0:T(8,128)(2,1)S(1)} %get-tuple-element.42), channel_id=1, source_target_pairs={{0,2},{1,3},{2,0},{3,1},{4,6},{5,7},{6,4},{7,5},{8,10},{9,11},{10,... | collective-permute-start | bytes 565256 | tf_op jit(solution)/shard_map/ppermute | solution.py:394
  21.2 10.9 %collective-permute-start.5 = (bf16[736,128]{1,0:T(8,128)(2,1)S(1)}, bf16[736,128]{1,0:T(8,128)(2,1)S(1)}, u32[]{:S(2)}, u32[]{:S(2)}) collective-permute-start(bf16[736,128]{1,0:T(8,128)(2,1)S(1)} %copy-done.9), channel_id=1, source_target_pairs={{0,12},{1,13},{2,14},{3,15},{4,8},{5,9},{6,10},{7,11},{8,4},{9,5},... | collective-permute-start | bytes 565256 | tf_op jit(solution)/shard_map/ppermute | solution.py:394
  27.1 11.5 %copy-start.6 = (f32[2560]{0:T(1024)S(1)}, f32[2560]{0:T(1024)}, u32[]{:S(2)}) copy-start(f32[2560]{0:T(1024)} %param.12) | copy-start | bytes 30724
  27.1 11.6 %copy-start.7 = (f32[2560]{0:T(1024)S(1)}, f32[2560]{0:T(1024)}, u32[]{:S(2)}) copy-start(f32[2560]{0:T(1024)} %param.13) | copy-start | bytes 30724
  27.2 8.9 %collective-permute-start.6 = (bf16[736,128]{1,0:T(8,128)(2,1)S(1)}, bf16[736,128]{1,0:T(8,128)(2,1)S(1)}, u32[]{:S(2)}, u32[]{:S(2)}) collective-permute-start(bf16[736,128]{1,0:T(8,128)(2,1)S(1)} %copy-done.8), channel_id=1, source_target_pairs={{0,14},{1,15},{2,12},{3,13},{4,10},{5,11},{6,8},{7,9},{8,6},{9,7},... | collective-permute-start | bytes 565256 | tf_op jit(solution)/shard_map/ppermute | solution.py:394
  29.1 9.0 %collective-permute-start.22 = (bf16[320,128]{1,0:T(8,128)(2,1)S(1)}, bf16[320,128]{1,0:T(8,128)(2,1)S(1)}, u32[]{:S(2)}, u32[]{:S(2)}) collective-permute-start(bf16[320,128]{1,0:T(8,128)(2,1)S(1)} %get-tuple-element.57), channel_id=1, source_target_pairs={{0,4},{1,5},{2,6},{3,7},{4,0},{5,1},{6,2},{7,3},{8,12},{9,13},{10,... | collective-permute-start | bytes 245768 | tf_op jit(solution)/shard_map/ppermute | solution.py:394
  29.2 9.0 %collective-permute-start.23 = (bf16[320,128]{1,0:T(8,128)(2,1)S(1)}, bf16[320,128]{1,0:T(8,128)(2,1)S(1)}, u32[]{:S(2)}, u32[]{:S(2)}) collective-permute-start(bf16[320,128]{1,0:T(8,128)(2,1)S(1)} %get-tuple-element.58), channel_id=1, source_target_pairs={{0,6},{1,7},{2,4},{3,5},{4,2},{5,3},{6,0},{7,1},{8,14},{9,15},{10,... | collective-permute-start | bytes 245768 | tf_op jit(solution)/shard_map/ppermute | solution.py:394
  36.0 5.7 %collective-permute-start.15 = (bf16[768,128]{1,0:T(8,128)(2,1)S(1)}, bf16[768,128]{1,0:T(8,128)(2,1)S(1)}, u32[]{:S(2)}, u32[]{:S(2)}) collective-permute-start(bf16[768,128]{1,0:T(8,128)(2,1)S(1)} %pack_weights.1), channel_id=1, source_target_pairs={{0,16},{16,0},{1,17},{17,1},{2,18},{18,2},{3,19},{19,3},{4,20},{20... | collective-permute-start | bytes 589832 | tf_op jit(solution)/shard_map/ppermute | solution.py:450
  37.6 1.4 %collective-permute-start.14 = (bf16[736,128]{1,0:T(8,128)(2,1)S(1)}, bf16[736,128]{1,0:T(8,128)(2,1)S(1)}, u32[]{:S(2)}, u32[]{:S(2)}) collective-permute-start(bf16[736,128]{1,0:T(8,128)(2,1)S(1)} %get-tuple-element.45.refs_7_), channel_id=1, source_target_pairs={{0,1},{1,0},{2,3},{3,2},{4,5},{5,4},{6,7},{7,6},{8,9},{9,8},{10,11... | collective-permute-start | bytes 565256 | tf_op jit(solution)/shard_map/ppermute | solution.py:394
  37.6 1.7 %collective-permute-start.10 = (bf16[736,128]{1,0:T(8,128)(2,1)S(1)}, bf16[736,128]{1,0:T(8,128)(2,1)S(1)}, u32[]{:S(2)}, u32[]{:S(2)}) collective-permute-start(bf16[736,128]{1,0:T(8,128)(2,1)S(1)} %collective-permute-done.3.refs_3_), channel_id=1, source_target_pairs={{0,1},{1,0},{2,3},{3,2},{4,5},{5,4},{6,7},{7,6},{8,9},{9,8},{10,11... | collective-permute-start | bytes 565256 | tf_op jit(solution)/shard_map/ppermute | solution.py:394
  38.1 1.5 %collective-permute-start.11 = (bf16[736,128]{1,0:T(8,128)(2,1)S(1)}, bf16[736,128]{1,0:T(8,128)(2,1)S(1)}, u32[]{:S(2)}, u32[]{:S(2)}) collective-permute-start(bf16[736,128]{1,0:T(8,128)(2,1)S(1)} %collective-permute-done.4.refs_4_), channel_id=1, source_target_pairs={{0,1},{1,0},{2,3},{3,2},{4,5},{5,4},{6,7},{7,6},{8,9},{9,8},{10,11... | collective-permute-start | bytes 565256 | tf_op jit(solution)/shard_map/ppermute | solution.py:394
  38.1 1.7 %collective-permute-start.12 = (bf16[736,128]{1,0:T(8,128)(2,1)S(1)}, bf16[736,128]{1,0:T(8,128)(2,1)S(1)}, u32[]{:S(2)}, u32[]{:S(2)}) collective-permute-start(bf16[736,128]{1,0:T(8,128)(2,1)S(1)} %collective-permute-done.5.refs_5_), channel_id=1, source_target_pairs={{0,1},{1,0},{2,3},{3,2},{4,5},{5,4},{6,7},{7,6},{8,9},{9,8},{10,11... | collective-permute-start | bytes 565256 | tf_op jit(solution)/shard_map/ppermute | solution.py:394
  39.0 2.8 %collective-permute-start.13 = (bf16[736,128]{1,0:T(8,128)(2,1)S(1)}, bf16[736,128]{1,0:T(8,128)(2,1)S(1)}, u32[]{:S(2)}, u32[]{:S(2)}) collective-permute-start(bf16[736,128]{1,0:T(8,128)(2,1)S(1)} %collective-permute-done.6.refs_6_), channel_id=1, source_target_pairs={{0,1},{1,0},{2,3},{3,2},{4,5},{5,4},{6,7},{7,6},{8,9},{9,8},{10,11... | collective-permute-start | bytes 565256 | tf_op jit(solution)/shard_map/ppermute | solution.py:394
  39.3 3.6 %collective-permute-start.7 = (bf16[736,128]{1,0:T(8,128)(2,1)S(1)}, bf16[736,128]{1,0:T(8,128)(2,1)S(1)}, u32[]{:S(2)}, u32[]{:S(2)}) collective-permute-start(bf16[736,128]{1,0:T(8,128)(2,1)S(1)} %collective-permute-done.refs_0_), channel_id=1, source_target_pairs={{0,1},{1,0},{2,3},{3,2},{4,5},{5,4},{6,7},{7,6},{8,9},{9,8},{10,11... | collective-permute-start | bytes 565256 | tf_op jit(solution)/shard_map/ppermute | solution.py:394
  39.6 12.6 %collective-permute-start.8 = (bf16[736,128]{1,0:T(8,128)(2,1)S(1)}, bf16[736,128]{1,0:T(8,128)(2,1)S(1)}, u32[]{:S(2)}, u32[]{:S(2)}) collective-permute-start(bf16[736,128]{1,0:T(8,128)(2,1)S(1)} %collective-permute-done.1.refs_1_), channel_id=1, source_target_pairs={{0,1},{1,0},{2,3},{3,2},{4,5},{5,4},{6,7},{7,6},{8,9},{9,8},{10,11... | collective-permute-start | bytes 565256 | tf_op jit(solution)/shard_map/ppermute | solution.py:394
  39.9 13.0 %collective-permute-start.9 = (bf16[736,128]{1,0:T(8,128)(2,1)S(1)}, bf16[736,128]{1,0:T(8,128)(2,1)S(1)}, u32[]{:S(2)}, u32[]{:S(2)}) collective-permute-start(bf16[736,128]{1,0:T(8,128)(2,1)S(1)} %collective-permute-done.2.refs_2_), channel_id=1, source_target_pairs={{0,1},{1,0},{2,3},{3,2},{4,5},{5,4},{6,7},{7,6},{8,9},{9,8},{10,11... | collective-permute-start | bytes 565256 | tf_op jit(solution)/shard_map/ppermute | solution.py:394
  41.8 11.0 %collective-permute-start.16 = (bf16[768,128]{1,0:T(8,128)(2,1)S(1)}, bf16[768,128]{1,0:T(8,128)(2,1)S(1)}, u32[]{:S(2)}, u32[]{:S(2)}) collective-permute-start(bf16[768,128]{1,0:T(8,128)(2,1)S(1)} %collective-permute-done.15.refs_16_), channel_id=1, source_target_pairs={{0,1},{1,0},{2,3},{3,2},{4,5},{5,4},{6,7},{7,6},{8,9},{9,8},{10,11... | collective-permute-start | bytes 589832 | tf_op jit(solution)/shard_map/ppermute | solution.py:394
  41.8 19.5 %collective-permute-start.24 = (bf16[320,128]{1,0:T(8,128)(2,1)S(1)}, bf16[320,128]{1,0:T(8,128)(2,1)S(1)}, u32[]{:S(2)}, u32[]{:S(2)}) collective-permute-start(bf16[320,128]{1,0:T(8,128)(2,1)S(1)} %get-tuple-element.59), channel_id=1, source_target_pairs={{0,2},{1,3},{2,0},{3,1},{4,6},{5,7},{6,4},{7,5},{8,10},{9,11},{10,... | collective-permute-start | bytes 245768 | tf_op jit(solution)/shard_map/ppermute | solution.py:394
  42.9 21.4 %collective-permute-start.18 = (bf16[320,128]{1,0:T(8,128)(2,1)S(1)}, bf16[320,128]{1,0:T(8,128)(2,1)S(1)}, u32[]{:S(2)}, u32[]{:S(2)}) collective-permute-start(bf16[320,128]{1,0:T(8,128)(2,1)S(1)} %get-tuple-element.49), channel_id=1, source_target_pairs={{0,8},{1,9},{2,10},{3,11},{4,12},{5,13},{6,14},{7,15},{8,0},{9,1},... | collective-permute-start | bytes 245768 | tf_op jit(solution)/shard_map/ppermute | solution.py:394
  52.2 12.1 %collective-permute-start.19 = (bf16[320,128]{1,0:T(8,128)(2,1)S(1)}, bf16[320,128]{1,0:T(8,128)(2,1)S(1)}, u32[]{:S(2)}, u32[]{:S(2)}) collective-permute-start(bf16[320,128]{1,0:T(8,128)(2,1)S(1)} %get-tuple-element.50), channel_id=1, source_target_pairs={{0,10},{1,11},{2,8},{3,9},{4,14},{5,15},{6,12},{7,13},{8,2},{9,3},... | collective-permute-start | bytes 245768 | tf_op jit(solution)/shard_map/ppermute | solution.py:394
  52.8 11.5 %collective-permute-start.20 = (bf16[320,128]{1,0:T(8,128)(2,1)S(1)}, bf16[320,128]{1,0:T(8,128)(2,1)S(1)}, u32[]{:S(2)}, u32[]{:S(2)}) collective-permute-start(bf16[320,128]{1,0:T(8,128)(2,1)S(1)} %get-tuple-element.51), channel_id=1, source_target_pairs={{0,12},{1,13},{2,14},{3,15},{4,8},{5,9},{6,10},{7,11},{8,4},{9,5},... | collective-permute-start | bytes 245768 | tf_op jit(solution)/shard_map/ppermute | solution.py:394
  52.8 11.5 %collective-permute-start.21 = (bf16[320,128]{1,0:T(8,128)(2,1)S(1)}, bf16[320,128]{1,0:T(8,128)(2,1)S(1)}, u32[]{:S(2)}, u32[]{:S(2)}) collective-permute-start(bf16[320,128]{1,0:T(8,128)(2,1)S(1)} %get-tuple-element.52), channel_id=1, source_target_pairs={{0,14},{1,15},{2,12},{3,13},{4,10},{5,11},{6,8},{7,9},{8,6},{9,7},... | collective-permute-start | bytes 245768 | tf_op jit(solution)/shard_map/ppermute | solution.py:394
  61.3 7.1 %collective-permute-start.17 = (f32[320,1152]{1,0:T(8,128)S(1)}, f32[320,1152]{1,0:T(8,128)S(1)}, u32[]{:S(2)}, u32[]{:S(2)}) collective-permute-start(f32[320,1152]{1,0:T(8,128)S(1)} %get-tuple-element.46.refs_0_), channel_id=1, source_target_pairs={{0,1},{1,0},{2,3},{3,2},{4,5},{5,4},{6,7},{7,6},{8,9},{9,8},{10,11... | collective-permute-start | bytes 4423688 | tf_op jit(solution)/shard_map/ppermute | solution.py:394
  68.4 24.8 %copy-start.1 = (f32[20,7680]{1,0:T(8,128)S(1)}, f32[20,7680]{1,0:T(8,128)}, u32[]{:S(2)}) copy-start(f32[20,7680]{1,0:T(8,128)} %refs_8_.1) | copy-start | bytes 1843204
  69.1 12.4 %collective-permute-start.25 = (bf16[512,128]{1,0:T(8,128)(2,1)S(1)}, bf16[512,128]{1,0:T(8,128)(2,1)S(1)}, u32[]{:S(2)}, u32[]{:S(2)}) collective-permute-start(bf16[512,128]{1,0:T(8,128)(2,1)S(1)} %get-tuple-element.65), channel_id=1, source_target_pairs={{0,8},{1,9},{2,10},{3,11},{4,12},{5,13},{6,14},{7,15},{8,0},{9,1},... | collective-permute-start | bytes 393224 | tf_op jit(solution)/shard_map/ppermute | solution.py:394
  71.4 14.0 %collective-permute-start.26 = (bf16[512,128]{1,0:T(8,128)(2,1)S(1)}, bf16[512,128]{1,0:T(8,128)(2,1)S(1)}, u32[]{:S(2)}, u32[]{:S(2)}) collective-permute-start(bf16[512,128]{1,0:T(8,128)(2,1)S(1)} %get-tuple-element.66), channel_id=1, source_target_pairs={{0,10},{1,11},{2,8},{3,9},{4,14},{5,15},{6,12},{7,13},{8,2},{9,3},... | collective-permute-start | bytes 393224 | tf_op jit(solution)/shard_map/ppermute | solution.py:394
  72.6 14.9 %collective-permute-start.27 = (bf16[512,128]{1,0:T(8,128)(2,1)S(1)}, bf16[512,128]{1,0:T(8,128)(2,1)S(1)}, u32[]{:S(2)}, u32[]{:S(2)}) collective-permute-start(bf16[512,128]{1,0:T(8,128)(2,1)S(1)} %get-tuple-element.67), channel_id=1, source_target_pairs={{0,4},{1,5},{2,6},{3,7},{4,0},{5,1},{6,2},{7,3},{8,12},{9,13},{10,... | collective-permute-start | bytes 393224 | tf_op jit(solution)/shard_map/ppermute | solution.py:394
  76.1 11.4 %collective-permute-start.28 = (bf16[512,128]{1,0:T(8,128)(2,1)S(1)}, bf16[512,128]{1,0:T(8,128)(2,1)S(1)}, u32[]{:S(2)}, u32[]{:S(2)}) collective-permute-start(bf16[512,128]{1,0:T(8,128)(2,1)S(1)} %get-tuple-element.68), channel_id=1, source_target_pairs={{0,6},{1,7},{2,4},{3,5},{4,2},{5,3},{6,0},{7,1},{8,14},{9,15},{10,... | collective-permute-start | bytes 393224 | tf_op jit(solution)/shard_map/ppermute | solution.py:394
  76.7 10.8 %collective-permute-start.29 = (bf16[512,128]{1,0:T(8,128)(2,1)S(1)}, bf16[512,128]{1,0:T(8,128)(2,1)S(1)}, u32[]{:S(2)}, u32[]{:S(2)}) collective-permute-start(bf16[512,128]{1,0:T(8,128)(2,1)S(1)} %get-tuple-element.69), channel_id=1, source_target_pairs={{0,2},{1,3},{2,0},{3,1},{4,6},{5,7},{6,4},{7,5},{8,10},{9,11},{10,... | collective-permute-start | bytes 393224 | tf_op jit(solution)/shard_map/ppermute | solution.py:394
  81.5 9.1 %collective-permute-start.30 = (bf16[512,128]{1,0:T(8,128)(2,1)S(1)}, bf16[512,128]{1,0:T(8,128)(2,1)S(1)}, u32[]{:S(2)}, u32[]{:S(2)}) collective-permute-start(bf16[512,128]{1,0:T(8,128)(2,1)S(1)} %get-tuple-element.70), channel_id=1, source_target_pairs={{0,12},{1,13},{2,14},{3,15},{4,8},{5,9},{6,10},{7,11},{8,4},{9,5},... | collective-permute-start | bytes 393224 | tf_op jit(solution)/shard_map/ppermute | solution.py:394
  85.4 7.8 %collective-permute-start.31 = (bf16[512,128]{1,0:T(8,128)(2,1)S(1)}, bf16[512,128]{1,0:T(8,128)(2,1)S(1)}, u32[]{:S(2)}, u32[]{:S(2)}) collective-permute-start(bf16[512,128]{1,0:T(8,128)(2,1)S(1)} %get-tuple-element.71), channel_id=1, source_target_pairs={{0,14},{1,15},{2,12},{3,13},{4,10},{5,11},{6,8},{7,9},{8,6},{9,7},... | collective-permute-start | bytes 393224 | tf_op jit(solution)/shard_map/ppermute | solution.py:394

commit v5 on v4

--- a/solution.py
+++ b/solution.py
@@ -19,7 +19,8 @@
 FAR = (4, 5, 6, 7)
 NEAR = (2, 3, 1, 0)
 BOTH = FAR + NEAR
-KEY_ORDER = (4, 5, 2, 3, 1, 6, 7, 0)
+KEY_ORDER = (7, 5, 2, 3, 1, 4, 6, 0)
+OUT_ORDER = (4, 5, 2, 3, 1, 6, 7, 0)
 HBM = pl.BlockSpec(memory_space=pltpu.HBM)
 ANY = pl.BlockSpec(memory_space=pl.ANY)
 VMEM = pl.BlockSpec(memory_space=pltpu.VMEM)
@@ -199,7 +200,7 @@
         both = dot(keys, w13, ((1,), (0,))) * scale
         back = dot(tgt, w2, ((1,), (1,))) * scale
         gate, up = both[:, :wide], both[:, wide:]
-        sig = 1.0 / (1.0 + jnp.exp(-gate))
+        sig = 0.5 + 0.5 * jnp.tanh(0.5 * gate)
         silu = gate * sig
         gates[at : at + tokens, 0:wide] = (back * up * (sig * (1.0 + gate * (1.0 - sig)))).astype(BF16)
         gates[at : at + tokens, wide:] = (back * silu).astype(BF16)
@@ -244,26 +245,37 @@
         tiles = [seen[:, t * tokens : (t + 1) * tokens].reshape(keys_seen, LANES) for t in range(5)]
         row = lax.broadcasted_iota(I32, (2 * tokens, 1), 0)
         row = jnp.where(row < tokens, row, row + (width - 1) * tokens) + (place - start) * tokens
-        distance = row - lax.broadcasted_iota(I32, (2 * tokens, keys_seen), 1)
-        allowed = distance >= 0
-        if keys_seen > span * tokens:
-            allowed = allowed & (distance < span * tokens)
         score = dot(q, jnp.concatenate(tiles[0:3], axis=1), ((1,), (1,)))
-        score = jnp.where(allowed, score, -jnp.inf)
+
+        def masked(first, last):
+            distance = row - lax.broadcasted_iota(I32, (2 * tokens, (last - first) * tokens), 1) - first * tokens
+            allowed = distance >= 0
+            if keys_seen > span * tokens:
+                allowed = allowed & (distance < span * tokens)
+            return jnp.where(allowed, score[:, first * tokens : last * tokens], -jnp.inf)
+
+        whole = (width + 1, span) if keys_seen > span * tokens else (0, width * j)
+        if whole[0] < whole[1]:
+            parts = [masked(0, whole[0])] if whole[0] else []
+            parts += [score[:, whole[0] * tokens : whole[1] * tokens], masked(whole[1], blocks)]
+            score = jnp.concatenate(parts, axis=1)
+        else:
+            score = masked(0, blocks)
         top = jnp.max(score, axis=1, keepdims=True)
         weight = jnp.exp2((score - top) * (scale * math.log2(math.e)))
         total = jnp.sum(weight, axis=1, keepdims=True)
-        attended = dot(weight.astype(BF16), jnp.concatenate(tiles[2:5], axis=1), ((1,), (0,))) / total
+        attended = dot(weight.astype(BF16), jnp.concatenate(tiles[2:5], axis=1), ((1,), (0,)))
         attended = jnp.concatenate([jnp.where(high, attended[:, 0:LANES], 0.0), attended[:, LANES:]], axis=1)
-        mean_sq = jnp.sum(attended * attended, axis=1, keepdims=True) * (1.0 / size)
-        window_part = attended * lax.rsqrt(mean_sq + 1e-05) * window_gain_ref[...]
-
-        both = dot(q, copy_ref[:, 0 : 2 * wide], ((1,), (0,))) * scale
+        share = 1.0 / total
+        mean_sq = jnp.sum(attended * attended, axis=1, keepdims=True) * (share * share * (1.0 / size))
+        window_part = attended * (share * lax.rsqrt(mean_sq + 1e-05)) * window_gain_ref[...]
+
+        both = dot(q, copy_ref[:, 0 : 2 * wide], ((1,), (0,)))
         gate, up = both[:, :wide], both[:, wide:]
-        hid = (gate / (1.0 + jnp.exp(-gate)) * up).astype(BF16)
-        out = dot(hid, copy_ref[:, 2 * wide :], ((1,), (0,))) * scale
-        mean_sq = jnp.sum(out * out, axis=1, keepdims=True) * (1.0 / size)
-        layer = out * lax.rsqrt(mean_sq + 1e-05) * fast_gain_ref[...] + window_part
+        hid = (gate * up * (0.5 * scale * scale) * (1.0 + jnp.tanh(gate * (0.5 * scale)))).astype(BF16)
+        out = dot(hid, copy_ref[:, 2 * wide :], ((1,), (0,)))
+        mean_sq = jnp.sum(out * out, axis=1, keepdims=True) * (scale * scale / size)
+        layer = out * (scale * lax.rsqrt(mean_sq + 1e-05)) * fast_gain_ref[...] + window_part
         for i in range(2):
             part = layer[i * tokens : (i + 1) * tokens]
             pay[slot + i, 0:tokens] = part[:, LANES : 2 * LANES].astype(BF16)
@@ -329,7 +341,7 @@
     fw_ref, layer_hbm, new_hbm, momentum_hbm, buf, layer_ref, new_ref, momentum_ref, sems = refs[heads:]
     chip, _ = chip_core(width)
     matrix = fw_ref.shape[1] // 3
-    for i, k in enumerate(KEY_ORDER):
+    for i, k in enumerate(OUT_ORDER):
         buf[chip ^ k] = pieces[i][...]
     mid = tokens // 2
     cut = 2 * tokens + mid
@@ -529,7 +541,7 @@
         scratch_shapes=[pltpu.VMEM((heads, 8 * slot, LANES), BF16)],
     )
     pieces = dict(zip(BOTH, pieces))
-    pieces = exchange([pieces[k] for k in KEY_ORDER], KEY_ORDER)
+    pieces = exchange([pieces[k] for k in OUT_ORDER], OUT_ORDER)
 
     return tuple(
         call(

time: 95.7 us -> 93.6 us (0.978)
  waiting for transfers between devices: 28.6 us -> 21.3 us
  starting transfers between devices: 48.3 us -> 53.4 us
    ppermute x31, waiting for transfers between devices: 26.9 us -> 19.6 us  [across(): return lax.ppermute(value, 'seq', [(i, i ^ step) for i in range(count)])]
    ppermute x31, starting transfers between devices: 46.7 us -> 51.9 us  [across(): return lax.ppermute(value, 'seq', [(i, i ^ step) for i in range(count)])]
  transfers between devices with their start and end apart: 32 -> 32, of which waited for: 10 -> 11; matrix products, arithmetic and copies ran while one was open for 0% -> 0% of each run, Pallas kernels for 12% -> 13%
where the time goes in v5:
time: 93.6 us; the launch traced here: 92.7 us
  starting transfers between devices  53.4 us (57%)
  waiting for transfers between devices  21.3 us (23%)
  Pallas kernels  16.6 us (18%)
  between operations  1.04 us (1%)
    ppermute x31, starting transfers between devices, across(): return lax.ppermute(value, 'seq', [(i, i ^ step) for i in range(count)])  51.9 us
    ppermute x31, waiting for transfers between devices, across(): return lax.ppermute(value, 'seq', [(i, i ^ step) for i in range(count)])  19.6 us
    pallas_call x9, Pallas kernels, call(): pl.pallas_call(body, compiler_params=params, cost_estimate=cost(micros),...  16.6 us
  transfers between devices with their start and end apart: 32, of which 11 were waited for; matrix products, arithmetic and copies ran while one was open for 0% of the time, Pallas kernels for 13%

profile of v5, /device:TPU:0, one launch (start us, length us, event | category | flops | bytes accessed | tf_op | source)
XLA Modules:
  0.0 92.7 jit_solution(10058429541301407656)
XLA Ops:
  0.7 2.5 %pack_keys.2 = (bf16[736,128]{1,0:T(8,128)(2,1)}, bf16[736,128]{1,0:T(8,128)(2,1)}, bf16[736,128]{1,0:T(8,128)(2,1)}, bf16[736,128]{1,0:T(8,128)(2,1)}) custom-call(bf16[128,2560]{1,0:T(8,128)(2,1)} %k_hbm.3, bf16[128,2560]{1,0:T(8,128)(2,1)} %v_hbm.3, f32[8,128]{1,0:T(8,128)} %bitcast.1, f32[20,7680]{1,0:T(8,128)} %refs_8_.1), custom_call_target="tpu_custom_call" | custom-call | flops 1000000000 | bytes 4000000 | tf_op jit(solution)/shard_map/pack_keys/pallas_call | solution.py:419
  3.2 6.1 %collective-permute-start = (bf16[736,128]{1,0:T(8,128)(2,1)}, bf16[736,128]{1,0:T(8,128)(2,1)S(1)}, u32[]{:S(2)}, u32[]{:S(2)}) collective-permute-start(bf16[736,128]{1,0:T(8,128)(2,1)} %get-tuple-element.38), channel_id=1, source_target_pairs={{0,14},{1,15},{2,12},{3,13},{4,10},{5,11},{6,8},{7,9},{8,6},{9,7},... | collective-permute-start | bytes 565256 | tf_op jit(solution)/shard_map/ppermute | solution.py:406
  9.3 0.6 pack_keys.3
  9.8 0.7 collective-permute-start.2
  10.5 1.7 %collective-permute-start.3 = (bf16[736,128]{1,0:T(8,128)(2,1)S(1)}, bf16[736,128]{1,0:T(8,128)(2,1)S(1)}, u32[]{:S(2)}, u32[]{:S(2)}) collective-permute-start(bf16[736,128]{1,0:T(8,128)(2,1)S(1)} %get-tuple-element.41), channel_id=1, source_target_pairs={{0,6},{1,7},{2,4},{3,5},{4,2},{5,3},{6,0},{7,1},{8,14},{9,15},{10,... | collective-permute-start | bytes 565256 | tf_op jit(solution)/shard_map/ppermute | solution.py:406
  12.2 1.2 %collective-permute-start.4 = (bf16[736,128]{1,0:T(8,128)(2,1)S(1)}, bf16[736,128]{1,0:T(8,128)(2,1)S(1)}, u32[]{:S(2)}, u32[]{:S(2)}) collective-permute-start(bf16[736,128]{1,0:T(8,128)(2,1)S(1)} %get-tuple-element.42), channel_id=1, source_target_pairs={{0,2},{1,3},{2,0},{3,1},{4,6},{5,7},{6,4},{7,5},{8,10},{9,11},{10,... | collective-permute-start | bytes 565256 | tf_op jit(solution)/shard_map/ppermute | solution.py:406
  13.4 1.7 %collective-permute-done.refs_0_ = bf16[736,128]{1,0:T(8,128)(2,1)S(1)} collective-permute-done((bf16[736,128]{1,0:T(8,128)(2,1)}, bf16[736,128]{1,0:T(8,128)(2,1)S(1)}, u32[]{:S(2)}, u32[]{:S(2)}) %collective-permute-start) | collective-permute-done | bytes 188448 | tf_op jit(solution)/shard_map/ppermute | solution.py:406
  15.1 9.2 %collective-permute-start.5 = (bf16[736,128]{1,0:T(8,128)(2,1)S(1)}, bf16[736,128]{1,0:T(8,128)(2,1)S(1)}, u32[]{:S(2)}, u32[]{:S(2)}) collective-permute-start(bf16[736,128]{1,0:T(8,128)(2,1)S(1)} %copy-done.9), channel_id=1, source_target_pairs={{0,8},{1,9},{2,10},{3,11},{4,12},{5,13},{6,14},{7,15},{8,0},{9,1},... | collective-permute-start | bytes 565256 | tf_op jit(solution)/shard_map/ppermute | solution.py:406
  24.3 2.9 %collective-permute-done.1.refs_1_ = bf16[736,128]{1,0:T(8,128)(2,1)S(1)} collective-permute-done((bf16[736,128]{1,0:T(8,128)(2,1)}, bf16[736,128]{1,0:T(8,128)(2,1)S(1)}, u32[]{:S(2)}, u32[]{:S(2)}) %collective-permute-start.1) | collective-permute-done | bytes 188448 | tf_op jit(solution)/shard_map/ppermute | solution.py:406
  27.2 2.1 %collective-permute-start.6 = (bf16[736,128]{1,0:T(8,128)(2,1)S(1)}, bf16[736,128]{1,0:T(8,128)(2,1)S(1)}, u32[]{:S(2)}, u32[]{:S(2)}) collective-permute-start(bf16[736,128]{1,0:T(8,128)(2,1)S(1)} %copy-done.8), channel_id=1, source_target_pairs={{0,12},{1,13},{2,14},{3,15},{4,8},{5,9},{6,10},{7,11},{8,4},{9,5},... | collective-permute-start | bytes 565256 | tf_op jit(solution)/shard_map/ppermute | solution.py:406
  29.4 0.2 pack_queries.1
  29.7 2.9 %collective-permute-start.23 = (bf16[320,128]{1,0:T(8,128)(2,1)S(1)}, bf16[320,128]{1,0:T(8,128)(2,1)S(1)}, u32[]{:S(2)}, u32[]{:S(2)}) collective-permute-start(bf16[320,128]{1,0:T(8,128)(2,1)S(1)} %get-tuple-element.58), channel_id=1, source_target_pairs={{0,6},{1,7},{2,4},{3,5},{4,2},{5,3},{6,0},{7,1},{8,14},{9,15},{10,... | collective-permute-start | bytes 245768 | tf_op jit(solution)/shard_map/ppermute | solution.py:406
  32.6 6.0 %collective-permute-done.5.refs_5_ = bf16[736,128]{1,0:T(8,128)(2,1)S(1)} collective-permute-done((bf16[736,128]{1,0:T(8,128)(2,1)S(1)}, bf16[736,128]{1,0:T(8,128)(2,1)S(1)}, u32[]{:S(2)}, u32[]{:S(2)}) %collective-permute-start.5) | collective-permute-done | bytes 188448 | tf_op jit(solution)/shard_map/ppermute | solution.py:406
  38.6 1.6 %collective-permute-start.15 = (bf16[768,128]{1,0:T(8,128)(2,1)S(1)}, bf16[768,128]{1,0:T(8,128)(2,1)S(1)}, u32[]{:S(2)}, u32[]{:S(2)}) collective-permute-start(bf16[768,128]{1,0:T(8,128)(2,1)S(1)} %pack_weights.1), channel_id=1, source_target_pairs={{0,16},{16,0},{1,17},{17,1},{2,18},{18,2},{3,19},{19,3},{4,20},{20... | collective-permute-start | bytes 589832 | tf_op jit(solution)/shard_map/ppermute | solution.py:462
  40.2 0.5 collective-permute-start.10
  40.7 0.5 collective-permute-start.12
  41.2 0.1 reshape.12
  41.3 0.1 reshape.13
  41.3 0.1 dynamic-slice
  41.4 0.1 dynamic-slice.2
  41.5 0.1 collective-permute-done.14.refs_15_
  41.6 0.1 collective-permute-start.13
  41.7 0.1 collective-permute-done.10.refs_11_
  41.9 0.2 collective-permute-start.7
  42.1 0.2 collective-permute-start.8
  42.4 0.2 collective-permute-start.9
  42.6 1.7 %collective-permute-done.15.refs_16_ = bf16[768,128]{1,0:T(8,128)(2,1)S(1)} collective-permute-done((bf16[768,128]{1,0:T(8,128)(2,1)S(1)}, bf16[768,128]{1,0:T(8,128)(2,1)S(1)}, u32[]{:S(2)}, u32[]{:S(2)}) %collective-permute-start.15) | collective-permute-done | bytes 196640 | tf_op jit(solution)/shard_map/ppermute | solution.py:462
  44.4 0.7 collective-permute-start.24
  45.1 4.6 %collective-permute-start.18 = (bf16[320,128]{1,0:T(8,128)(2,1)S(1)}, bf16[320,128]{1,0:T(8,128)(2,1)S(1)}, u32[]{:S(2)}, u32[]{:S(2)}) collective-permute-start(bf16[320,128]{1,0:T(8,128)(2,1)S(1)} %get-tuple-element.49), channel_id=1, source_target_pairs={{0,8},{1,9},{2,10},{3,11},{4,12},{5,13},{6,14},{7,15},{8,0},{9,1},... | collective-permute-start | bytes 245768 | tf_op jit(solution)/shard_map/ppermute | solution.py:406
  49.7 1.0 %collective-permute-start.19 = (bf16[320,128]{1,0:T(8,128)(2,1)S(1)}, bf16[320,128]{1,0:T(8,128)(2,1)S(1)}, u32[]{:S(2)}, u32[]{:S(2)}) collective-permute-start(bf16[320,128]{1,0:T(8,128)(2,1)S(1)} %get-tuple-element.50), channel_id=1, source_target_pairs={{0,10},{1,11},{2,8},{3,9},{4,14},{5,15},{6,12},{7,13},{8,2},{9,3},... | collective-permute-start | bytes 245768 | tf_op jit(solution)/shard_map/ppermute | solution.py:406
  50.7 1.6 %collective-permute-start.20 = (bf16[320,128]{1,0:T(8,128)(2,1)S(1)}, bf16[320,128]{1,0:T(8,128)(2,1)S(1)}, u32[]{:S(2)}, u32[]{:S(2)}) collective-permute-start(bf16[320,128]{1,0:T(8,128)(2,1)S(1)} %get-tuple-element.51), channel_id=1, source_target_pairs={{0,12},{1,13},{2,14},{3,15},{4,8},{5,9},{6,10},{7,11},{8,4},{9,5},... | collective-permute-start | bytes 245768 | tf_op jit(solution)/shard_map/ppermute | solution.py:406
  52.4 2.2 %collective-permute-start.21 = (bf16[320,128]{1,0:T(8,128)(2,1)S(1)}, bf16[320,128]{1,0:T(8,128)(2,1)S(1)}, u32[]{:S(2)}, u32[]{:S(2)}) collective-permute-start(bf16[320,128]{1,0:T(8,128)(2,1)S(1)} %get-tuple-element.52), channel_id=1, source_target_pairs={{0,14},{1,15},{2,12},{3,13},{4,10},{5,11},{6,8},{7,9},{8,6},{9,7},... | collective-permute-start | bytes 245768 | tf_op jit(solution)/shard_map/ppermute | solution.py:406
  54.7 4.2 %key_side.1 = (f32[320,1152]{1,0:T(8,128)S(1)}, bf16[384,1152]{1,0:T(8,128)(2,1)S(1)}, bf16[16,640,128]{2,1,0:T(8,128)(2,1)S(1)}) custom-call(bf16[736,128]{1,0:T(8,128)(2,1)S(1)} %collective-permute-done.refs_0_, bf16[736,128]{1,0:T(8,128)(2,1)S(1)} %collective-permute-done.1.refs_1_, bf16[736,128]{1,0:T(8,128)(2,1)S(1)} %collective-permute-done.2.refs_2_, ...), custom_call_target="tpu_custom_call" | custom-call | tf_op jit(solution)/shard_map/key_side/pallas_call | solution.py:419
  58.9 2.9 %query_side.3 = (bf16[320,128]{1,0:T(8,128)(2,1)S(1)}, bf16[320,128]{1,0:T(8,128)(2,1)S(1)}, bf16[320,128]{1,0:T(8,128)(2,1)S(1)}, bf16[320,128]{1,0:T(8,128)(2,1)S(1)}) custom-call(bf16[16,640,128]{2,1,0:T(8,128)(2,1)S(1)} %get-tuple-element.48.refs_0_, bf16[384,1152]{1,0:T(8,128)(2,1)S(1)} %get-tuple-element.47.refs_1_.refs_2_, ...), custom_call_target="tpu_custom_call" | custom-call | tf_op jit(solution)/shard_map/query_side/pallas_call | solution.py:419
  61.9 0.6 collective-permute-done.19.refs_5_
  62.5 3.9 %query_side.2 = (bf16[320,128]{1,0:T(8,128)(2,1)S(1)}, bf16[320,128]{1,0:T(8,128)(2,1)S(1)}, bf16[320,128]{1,0:T(8,128)(2,1)S(1)}, bf16[320,128]{1,0:T(8,128)(2,1)S(1)}) custom-call(bf16[16,640,128]{2,1,0:T(8,128)(2,1)S(1)} %get-tuple-element.48.refs_0_, bf16[384,1152]{1,0:T(8,128)(2,1)S(1)} %get-tuple-element.47.refs_1_.refs_2_, ...), custom_call_target="tpu_custom_call" | custom-call | flops 20000000000 | bytes 80000000 | tf_op jit(solution)/shard_map/query_side/pallas_call | solution.py:419
  66.4 0.7 pack_momentum.1
  67.1 3.1 %collective-permute-start.25 = (bf16[512,128]{1,0:T(8,128)(2,1)S(1)}, bf16[512,128]{1,0:T(8,128)(2,1)S(1)}, u32[]{:S(2)}, u32[]{:S(2)}) collective-permute-start(bf16[512,128]{1,0:T(8,128)(2,1)S(1)} %get-tuple-element.65), channel_id=1, source_target_pairs={{0,8},{1,9},{2,10},{3,11},{4,12},{5,13},{6,14},{7,15},{8,0},{9,1},... | collective-permute-start | bytes 393224 | tf_op jit(solution)/shard_map/ppermute | solution.py:406
  70.2 0.2 collective-permute-start.26
  70.4 3.5 %collective-permute-start.27 = (bf16[512,128]{1,0:T(8,128)(2,1)S(1)}, bf16[512,128]{1,0:T(8,128)(2,1)S(1)}, u32[]{:S(2)}, u32[]{:S(2)}) collective-permute-start(bf16[512,128]{1,0:T(8,128)(2,1)S(1)} %get-tuple-element.67), channel_id=1, source_target_pairs={{0,4},{1,5},{2,6},{3,7},{4,0},{5,1},{6,2},{7,3},{8,12},{9,13},{10,... | collective-permute-start | bytes 393224 | tf_op jit(solution)/shard_map/ppermute | solution.py:406
  73.9 0.9 %collective-permute-start.28 = (bf16[512,128]{1,0:T(8,128)(2,1)S(1)}, bf16[512,128]{1,0:T(8,128)(2,1)S(1)}, u32[]{:S(2)}, u32[]{:S(2)}) collective-permute-start(bf16[512,128]{1,0:T(8,128)(2,1)S(1)} %get-tuple-element.68), channel_id=1, source_target_pairs={{0,6},{1,7},{2,4},{3,5},{4,2},{5,3},{6,0},{7,1},{8,14},{9,15},{10,... | collective-permute-start | bytes 393224 | tf_op jit(solution)/shard_map/ppermute | solution.py:406
  74.8 0.6 collective-permute-start.29
  75.4 4.0 %collective-permute-done.25.refs_0_ = bf16[512,128]{1,0:T(8,128)(2,1)S(1)} collective-permute-done((bf16[512,128]{1,0:T(8,128)(2,1)S(1)}, bf16[512,128]{1,0:T(8,128)(2,1)S(1)}, u32[]{:S(2)}, u32[]{:S(2)}) %collective-permute-start.25) | collective-permute-done | bytes 131104 | tf_op jit(solution)/shard_map/ppermute | solution.py:406
  79.4 3.7 %collective-permute-start.30 = (bf16[512,128]{1,0:T(8,128)(2,1)S(1)}, bf16[512,128]{1,0:T(8,128)(2,1)S(1)}, u32[]{:S(2)}, u32[]{:S(2)}) collective-permute-start(bf16[512,128]{1,0:T(8,128)(2,1)S(1)} %get-tuple-element.70), channel_id=1, source_target_pairs={{0,12},{1,13},{2,14},{3,15},{4,8},{5,9},{6,10},{7,11},{8,4},{9,5},... | collective-permute-start | bytes 393224 | tf_op jit(solution)/shard_map/ppermute | solution.py:406
  83.2 3.7 %collective-permute-start.31 = (bf16[512,128]{1,0:T(8,128)(2,1)S(1)}, bf16[512,128]{1,0:T(8,128)(2,1)S(1)}, u32[]{:S(2)}, u32[]{:S(2)}) collective-permute-start(bf16[512,128]{1,0:T(8,128)(2,1)S(1)} %get-tuple-element.71), channel_id=1, source_target_pairs={{0,14},{1,15},{2,12},{3,13},{4,10},{5,11},{6,8},{7,9},{8,6},{9,7},... | collective-permute-start | bytes 393224 | tf_op jit(solution)/shard_map/ppermute | solution.py:406
  86.8 1.7 %collective-permute-done.30.refs_5_ = bf16[512,128]{1,0:T(8,128)(2,1)S(1)} collective-permute-done((bf16[512,128]{1,0:T(8,128)(2,1)S(1)}, bf16[512,128]{1,0:T(8,128)(2,1)S(1)}, u32[]{:S(2)}, u32[]{:S(2)}) %collective-permute-start.30) | collective-permute-done | bytes 131104 | tf_op jit(solution)/shard_map/ppermute | solution.py:406
  88.5 2.3 %collective-permute-done.31.refs_6_ = bf16[512,128]{1,0:T(8,128)(2,1)S(1)} collective-permute-done((bf16[512,128]{1,0:T(8,128)(2,1)S(1)}, bf16[512,128]{1,0:T(8,128)(2,1)S(1)}, u32[]{:S(2)}, u32[]{:S(2)}) %collective-permute-start.31) | collective-permute-done | bytes 131104 | tf_op jit(solution)/shard_map/ppermute | solution.py:406
  90.8 1.7 %unpack.1 = (bf16[128,2560]{1,0:T(8,128)(2,1)}, f32[20,7680]{1,0:T(8,128)}, f32[20,7680]{1,0:T(8,128)}) custom-call(bf16[512,128]{1,0:T(8,128)(2,1)S(1)} %collective-permute-done.25.refs_0_, bf16[512,128]{1,0:T(8,128)(2,1)S(1)} %collective-permute-done.26.refs_1_, bf16[512,128]{1,0:T(8,128)(2,1)S(1)} %collective-permute-done.27.refs_2_, ...), custom_call_target="tpu_custom_call" | custom-call | flops 1000000000 | bytes 4000000 | tf_op jit(solution)/shard_map/unpack/pallas_call | solution.py:419
  (54 shorter events, 0.5 us)
Async XLA Ops:
  0.6 8.6 %copy-start = (f32[20,7680]{1,0:T(8,128)S(1)}, f32[20,7680]{1,0:T(8,128)}, u32[]{:S(2)}) copy-start(f32[20,7680]{1,0:T(8,128)} %refs_8_.1) | copy-start | bytes 1843204
  0.6 8.6 %copy-start.2 = (bf16[128,2560]{1,0:T(8,128)(2,1)S(1)}, bf16[128,2560]{1,0:T(8,128)(2,1)}, u32[]{:S(2)}) copy-start(bf16[128,2560]{1,0:T(8,128)(2,1)} %k_hbm.3) | copy-start | bytes 1966084
  0.7 8.6 %copy-start.3 = (bf16[128,2560]{1,0:T(8,128)(2,1)S(1)}, bf16[128,2560]{1,0:T(8,128)(2,1)}, u32[]{:S(2)}) copy-start(bf16[128,2560]{1,0:T(8,128)(2,1)} %v_hbm.3) | copy-start | bytes 1966084
  0.7 8.6 %copy-start.5 = (f32[128,8]{0,1:T(8,128)S(1)}, f32[128,8]{0,1:T(8,128)}, u32[]{:S(2)}) copy-start(f32[128,8]{0,1:T(8,128)} %param.10) | copy-start | bytes 12292
  3.2 11.9 %collective-permute-start = (bf16[736,128]{1,0:T(8,128)(2,1)}, bf16[736,128]{1,0:T(8,128)(2,1)S(1)}, u32[]{:S(2)}, u32[]{:S(2)}) collective-permute-start(bf16[736,128]{1,0:T(8,128)(2,1)} %get-tuple-element.38), channel_id=1, source_target_pairs={{0,14},{1,15},{2,12},{3,13},{4,10},{5,11},{6,8},{7,9},{8,6},{9,7},... | collective-permute-start | bytes 565256 | tf_op jit(solution)/shard_map/ppermute | solution.py:406
  9.2 5.9 %copy-start.9 = (bf16[736,128]{1,0:T(8,128)(2,1)S(1)}, bf16[736,128]{1,0:T(8,128)(2,1)}, u32[]{:S(2)}) copy-start(bf16[736,128]{1,0:T(8,128)(2,1)} %get-tuple-element.43) | copy-start | bytes 565252
  9.2 18.0 %copy-start.8 = (bf16[736,128]{1,0:T(8,128)(2,1)S(1)}, bf16[736,128]{1,0:T(8,128)(2,1)}, u32[]{:S(2)}) copy-start(bf16[736,128]{1,0:T(8,128)(2,1)} %get-tuple-element.44) | copy-start | bytes 565252
  9.2 20.2 %copy-start.4 = (bf16[128,2560]{1,0:T(8,128)(2,1)S(1)}, bf16[128,2560]{1,0:T(8,128)(2,1)}, u32[]{:S(2)}) copy-start(bf16[128,2560]{1,0:T(8,128)(2,1)} %q_ref.1) | copy-start | bytes 1966084
  9.2 18.0 %collective-permute-start.1 = (bf16[736,128]{1,0:T(8,128)(2,1)}, bf16[736,128]{1,0:T(8,128)(2,1)S(1)}, u32[]{:S(2)}, u32[]{:S(2)}) collective-permute-start(bf16[736,128]{1,0:T(8,128)(2,1)} %get-tuple-element.39), channel_id=1, source_target_pairs={{0,10},{1,11},{2,8},{3,9},{4,14},{5,15},{6,12},{7,13},{8,2},{9,3},... | collective-permute-start | bytes 565256 | tf_op jit(solution)/shard_map/ppermute | solution.py:406
  9.8 19.7 %collective-permute-start.2 = (bf16[736,128]{1,0:T(8,128)(2,1)S(1)}, bf16[736,128]{1,0:T(8,128)(2,1)S(1)}, u32[]{:S(2)}, u32[]{:S(2)}) collective-permute-start(bf16[736,128]{1,0:T(8,128)(2,1)S(1)} %get-tuple-element.40), channel_id=1, source_target_pairs={{0,4},{1,5},{2,6},{3,7},{4,0},{5,1},{6,2},{7,3},{8,12},{9,13},{10,... | collective-permute-start | bytes 565256 | tf_op jit(solution)/shard_map/ppermute | solution.py:406
  10.5 19.1 %collective-permute-start.3 = (bf16[736,128]{1,0:T(8,128)(2,1)S(1)}, bf16[736,128]{1,0:T(8,128)(2,1)S(1)}, u32[]{:S(2)}, u32[]{:S(2)}) collective-permute-start(bf16[736,128]{1,0:T(8,128)(2,1)S(1)} %get-tuple-element.41), channel_id=1, source_target_pairs={{0,6},{1,7},{2,4},{3,5},{4,2},{5,3},{6,0},{7,1},{8,14},{9,15},{10,... | collective-permute-start | bytes 565256 | tf_op jit(solution)/shard_map/ppermute | solution.py:406
  12.2 20.3 %collective-permute-start.4 = (bf16[736,128]{1,0:T(8,128)(2,1)S(1)}, bf16[736,128]{1,0:T(8,128)(2,1)S(1)}, u32[]{:S(2)}, u32[]{:S(2)}) collective-permute-start(bf16[736,128]{1,0:T(8,128)(2,1)S(1)} %get-tuple-element.42), channel_id=1, source_target_pairs={{0,2},{1,3},{2,0},{3,1},{4,6},{5,7},{6,4},{7,5},{8,10},{9,11},{10,... | collective-permute-start | bytes 565256 | tf_op jit(solution)/shard_map/ppermute | solution.py:406
  15.1 23.5 %collective-permute-start.5 = (bf16[736,128]{1,0:T(8,128)(2,1)S(1)}, bf16[736,128]{1,0:T(8,128)(2,1)S(1)}, u32[]{:S(2)}, u32[]{:S(2)}) collective-permute-start(bf16[736,128]{1,0:T(8,128)(2,1)S(1)} %copy-done.9), channel_id=1, source_target_pairs={{0,8},{1,9},{2,10},{3,11},{4,12},{5,13},{6,14},{7,15},{8,0},{9,1},... | collective-permute-start | bytes 565256 | tf_op jit(solution)/shard_map/ppermute | solution.py:406
  27.2 14.0 %copy-start.6 = (f32[2560]{0:T(1024)S(1)}, f32[2560]{0:T(1024)}, u32[]{:S(2)}) copy-start(f32[2560]{0:T(1024)} %param.12) | copy-start | bytes 30724
  27.2 14.0 %copy-start.7 = (f32[2560]{0:T(1024)S(1)}, f32[2560]{0:T(1024)}, u32[]{:S(2)}) copy-start(f32[2560]{0:T(1024)} %param.13) | copy-start | bytes 30724
  27.2 11.3 %collective-permute-start.6 = (bf16[736,128]{1,0:T(8,128)(2,1)S(1)}, bf16[736,128]{1,0:T(8,128)(2,1)S(1)}, u32[]{:S(2)}, u32[]{:S(2)}) collective-permute-start(bf16[736,128]{1,0:T(8,128)(2,1)S(1)} %copy-done.8), channel_id=1, source_target_pairs={{0,12},{1,13},{2,14},{3,15},{4,8},{5,9},{6,10},{7,11},{8,4},{9,5},... | collective-permute-start | bytes 565256 | tf_op jit(solution)/shard_map/ppermute | solution.py:406
  29.6 11.1 %collective-permute-start.22 = (bf16[320,128]{1,0:T(8,128)(2,1)S(1)}, bf16[320,128]{1,0:T(8,128)(2,1)S(1)}, u32[]{:S(2)}, u32[]{:S(2)}) collective-permute-start(bf16[320,128]{1,0:T(8,128)(2,1)S(1)} %get-tuple-element.57), channel_id=1, source_target_pairs={{0,4},{1,5},{2,6},{3,7},{4,0},{5,1},{6,2},{7,3},{8,12},{9,13},{10,... | collective-permute-start | bytes 245768 | tf_op jit(solution)/shard_map/ppermute | solution.py:406
  29.7 11.0 %collective-permute-start.23 = (bf16[320,128]{1,0:T(8,128)(2,1)S(1)}, bf16[320,128]{1,0:T(8,128)(2,1)S(1)}, u32[]{:S(2)}, u32[]{:S(2)}) collective-permute-start(bf16[320,128]{1,0:T(8,128)(2,1)S(1)} %get-tuple-element.58), channel_id=1, source_target_pairs={{0,6},{1,7},{2,4},{3,5},{4,2},{5,3},{6,0},{7,1},{8,14},{9,15},{10,... | collective-permute-start | bytes 245768 | tf_op jit(solution)/shard_map/ppermute | solution.py:406
  38.6 5.7 %collective-permute-start.15 = (bf16[768,128]{1,0:T(8,128)(2,1)S(1)}, bf16[768,128]{1,0:T(8,128)(2,1)S(1)}, u32[]{:S(2)}, u32[]{:S(2)}) collective-permute-start(bf16[768,128]{1,0:T(8,128)(2,1)S(1)} %pack_weights.1), channel_id=1, source_target_pairs={{0,16},{16,0},{1,17},{17,1},{2,18},{18,2},{3,19},{19,3},{4,20},{20... | collective-permute-start | bytes 589832 | tf_op jit(solution)/shard_map/ppermute | solution.py:462
  40.2 1.4 %collective-permute-start.14 = (bf16[736,128]{1,0:T(8,128)(2,1)S(1)}, bf16[736,128]{1,0:T(8,128)(2,1)S(1)}, u32[]{:S(2)}, u32[]{:S(2)}) collective-permute-start(bf16[736,128]{1,0:T(8,128)(2,1)S(1)} %get-tuple-element.45.refs_7_), channel_id=1, source_target_pairs={{0,1},{1,0},{2,3},{3,2},{4,5},{5,4},{6,7},{7,6},{8,9},{9,8},{10,11... | collective-permute-start | bytes 565256 | tf_op jit(solution)/shard_map/ppermute | solution.py:406
  40.2 1.7 %collective-permute-start.10 = (bf16[736,128]{1,0:T(8,128)(2,1)S(1)}, bf16[736,128]{1,0:T(8,128)(2,1)S(1)}, u32[]{:S(2)}, u32[]{:S(2)}) collective-permute-start(bf16[736,128]{1,0:T(8,128)(2,1)S(1)} %collective-permute-done.3.refs_3_), channel_id=1, source_target_pairs={{0,1},{1,0},{2,3},{3,2},{4,5},{5,4},{6,7},{7,6},{8,9},{9,8},{10,11... | collective-permute-start | bytes 565256 | tf_op jit(solution)/shard_map/ppermute | solution.py:406
  40.7 1.5 %collective-permute-start.11 = (bf16[736,128]{1,0:T(8,128)(2,1)S(1)}, bf16[736,128]{1,0:T(8,128)(2,1)S(1)}, u32[]{:S(2)}, u32[]{:S(2)}) collective-permute-start(bf16[736,128]{1,0:T(8,128)(2,1)S(1)} %collective-permute-done.4.refs_4_), channel_id=1, source_target_pairs={{0,1},{1,0},{2,3},{3,2},{4,5},{5,4},{6,7},{7,6},{8,9},{9,8},{10,11... | collective-permute-start | bytes 565256 | tf_op jit(solution)/shard_map/ppermute | solution.py:406
  40.7 1.7 %collective-permute-start.12 = (bf16[736,128]{1,0:T(8,128)(2,1)S(1)}, bf16[736,128]{1,0:T(8,128)(2,1)S(1)}, u32[]{:S(2)}, u32[]{:S(2)}) collective-permute-start(bf16[736,128]{1,0:T(8,128)(2,1)S(1)} %collective-permute-done.5.refs_5_), channel_id=1, source_target_pairs={{0,1},{1,0},{2,3},{3,2},{4,5},{5,4},{6,7},{7,6},{8,9},{9,8},{10,11... | collective-permute-start | bytes 565256 | tf_op jit(solution)/shard_map/ppermute | solution.py:406
  41.6 2.8 %collective-permute-start.13 = (bf16[736,128]{1,0:T(8,128)(2,1)S(1)}, bf16[736,128]{1,0:T(8,128)(2,1)S(1)}, u32[]{:S(2)}, u32[]{:S(2)}) collective-permute-start(bf16[736,128]{1,0:T(8,128)(2,1)S(1)} %collective-permute-done.6.refs_6_), channel_id=1, source_target_pairs={{0,1},{1,0},{2,3},{3,2},{4,5},{5,4},{6,7},{7,6},{8,9},{9,8},{10,11... | collective-permute-start | bytes 565256 | tf_op jit(solution)/shard_map/ppermute | solution.py:406
  41.9 3.2 %collective-permute-start.7 = (bf16[736,128]{1,0:T(8,128)(2,1)S(1)}, bf16[736,128]{1,0:T(8,128)(2,1)S(1)}, u32[]{:S(2)}, u32[]{:S(2)}) collective-permute-start(bf16[736,128]{1,0:T(8,128)(2,1)S(1)} %collective-permute-done.refs_0_), channel_id=1, source_target_pairs={{0,1},{1,0},{2,3},{3,2},{4,5},{5,4},{6,7},{7,6},{8,9},{9,8},{10,11... | collective-permute-start | bytes 565256 | tf_op jit(solution)/shard_map/ppermute | solution.py:406
  42.1 7.6 %collective-permute-start.8 = (bf16[736,128]{1,0:T(8,128)(2,1)S(1)}, bf16[736,128]{1,0:T(8,128)(2,1)S(1)}, u32[]{:S(2)}, u32[]{:S(2)}) collective-permute-start(bf16[736,128]{1,0:T(8,128)(2,1)S(1)} %collective-permute-done.1.refs_1_), channel_id=1, source_target_pairs={{0,1},{1,0},{2,3},{3,2},{4,5},{5,4},{6,7},{7,6},{8,9},{9,8},{10,11... | collective-permute-start | bytes 565256 | tf_op jit(solution)/shard_map/ppermute | solution.py:406
  42.4 8.4 %collective-permute-start.9 = (bf16[736,128]{1,0:T(8,128)(2,1)S(1)}, bf16[736,128]{1,0:T(8,128)(2,1)S(1)}, u32[]{:S(2)}, u32[]{:S(2)}) collective-permute-start(bf16[736,128]{1,0:T(8,128)(2,1)S(1)} %collective-permute-done.2.refs_2_), channel_id=1, source_target_pairs={{0,1},{1,0},{2,3},{3,2},{4,5},{5,4},{6,7},{7,6},{8,9},{9,8},{10,11... | collective-permute-start | bytes 565256 | tf_op jit(solution)/shard_map/ppermute | solution.py:406
  44.3 8.1 %collective-permute-start.16 = (bf16[768,128]{1,0:T(8,128)(2,1)S(1)}, bf16[768,128]{1,0:T(8,128)(2,1)S(1)}, u32[]{:S(2)}, u32[]{:S(2)}) collective-permute-start(bf16[768,128]{1,0:T(8,128)(2,1)S(1)} %collective-permute-done.15.refs_16_), channel_id=1, source_target_pairs={{0,1},{1,0},{2,3},{3,2},{4,5},{5,4},{6,7},{7,6},{8,9},{9,8},{10,11... | collective-permute-start | bytes 589832 | tf_op jit(solution)/shard_map/ppermute | solution.py:406
  44.4 14.4 %collective-permute-start.24 = (bf16[320,128]{1,0:T(8,128)(2,1)S(1)}, bf16[320,128]{1,0:T(8,128)(2,1)S(1)}, u32[]{:S(2)}, u32[]{:S(2)}) collective-permute-start(bf16[320,128]{1,0:T(8,128)(2,1)S(1)} %get-tuple-element.59), channel_id=1, source_target_pairs={{0,2},{1,3},{2,0},{3,1},{4,6},{5,7},{6,4},{7,5},{8,10},{9,11},{10,... | collective-permute-start | bytes 245768 | tf_op jit(solution)/shard_map/ppermute | solution.py:406
  45.1 16.8 %collective-permute-start.18 = (bf16[320,128]{1,0:T(8,128)(2,1)S(1)}, bf16[320,128]{1,0:T(8,128)(2,1)S(1)}, u32[]{:S(2)}, u32[]{:S(2)}) collective-permute-start(bf16[320,128]{1,0:T(8,128)(2,1)S(1)} %get-tuple-element.49), channel_id=1, source_target_pairs={{0,8},{1,9},{2,10},{3,11},{4,12},{5,13},{6,14},{7,15},{8,0},{9,1},... | collective-permute-start | bytes 245768 | tf_op jit(solution)/shard_map/ppermute | solution.py:406
  49.7 12.8 %collective-permute-start.19 = (bf16[320,128]{1,0:T(8,128)(2,1)S(1)}, bf16[320,128]{1,0:T(8,128)(2,1)S(1)}, u32[]{:S(2)}, u32[]{:S(2)}) collective-permute-start(bf16[320,128]{1,0:T(8,128)(2,1)S(1)} %get-tuple-element.50), channel_id=1, source_target_pairs={{0,10},{1,11},{2,8},{3,9},{4,14},{5,15},{6,12},{7,13},{8,2},{9,3},... | collective-permute-start | bytes 245768 | tf_op jit(solution)/shard_map/ppermute | solution.py:406
  50.7 11.8 %collective-permute-start.20 = (bf16[320,128]{1,0:T(8,128)(2,1)S(1)}, bf16[320,128]{1,0:T(8,128)(2,1)S(1)}, u32[]{:S(2)}, u32[]{:S(2)}) collective-permute-start(bf16[320,128]{1,0:T(8,128)(2,1)S(1)} %get-tuple-element.51), channel_id=1, source_target_pairs={{0,12},{1,13},{2,14},{3,15},{4,8},{5,9},{6,10},{7,11},{8,4},{9,5},... | collective-permute-start | bytes 245768 | tf_op jit(solution)/shard_map/ppermute | solution.py:406
  52.4 10.1 %collective-permute-start.21 = (bf16[320,128]{1,0:T(8,128)(2,1)S(1)}, bf16[320,128]{1,0:T(8,128)(2,1)S(1)}, u32[]{:S(2)}, u32[]{:S(2)}) collective-permute-start(bf16[320,128]{1,0:T(8,128)(2,1)S(1)} %get-tuple-element.52), channel_id=1, source_target_pairs={{0,14},{1,15},{2,12},{3,13},{4,10},{5,11},{6,8},{7,9},{8,6},{9,7},... | collective-permute-start | bytes 245768 | tf_op jit(solution)/shard_map/ppermute | solution.py:406
  58.8 7.5 %collective-permute-start.17 = (f32[320,1152]{1,0:T(8,128)S(1)}, f32[320,1152]{1,0:T(8,128)S(1)}, u32[]{:S(2)}, u32[]{:S(2)}) collective-permute-start(f32[320,1152]{1,0:T(8,128)S(1)} %get-tuple-element.46.refs_0_), channel_id=1, source_target_pairs={{0,1},{1,0},{2,3},{3,2},{4,5},{5,4},{6,7},{7,6},{8,9},{9,8},{10,11... | collective-permute-start | bytes 4423688 | tf_op jit(solution)/shard_map/ppermute | solution.py:406
  66.4 24.4 %copy-start.1 = (f32[20,7680]{1,0:T(8,128)S(1)}, f32[20,7680]{1,0:T(8,128)}, u32[]{:S(2)}) copy-start(f32[20,7680]{1,0:T(8,128)} %refs_8_.1) | copy-start | bytes 1843204
  67.1 12.3 %collective-permute-start.25 = (bf16[512,128]{1,0:T(8,128)(2,1)S(1)}, bf16[512,128]{1,0:T(8,128)(2,1)S(1)}, u32[]{:S(2)}, u32[]{:S(2)}) collective-permute-start(bf16[512,128]{1,0:T(8,128)(2,1)S(1)} %get-tuple-element.65), channel_id=1, source_target_pairs={{0,8},{1,9},{2,10},{3,11},{4,12},{5,13},{6,14},{7,15},{8,0},{9,1},... | collective-permute-start | bytes 393224 | tf_op jit(solution)/shard_map/ppermute | solution.py:406
  70.2 12.9 %collective-permute-start.26 = (bf16[512,128]{1,0:T(8,128)(2,1)S(1)}, bf16[512,128]{1,0:T(8,128)(2,1)S(1)}, u32[]{:S(2)}, u32[]{:S(2)}) collective-permute-start(bf16[512,128]{1,0:T(8,128)(2,1)S(1)} %get-tuple-element.66), channel_id=1, source_target_pairs={{0,10},{1,11},{2,8},{3,9},{4,14},{5,15},{6,12},{7,13},{8,2},{9,3},... | collective-permute-start | bytes 393224 | tf_op jit(solution)/shard_map/ppermute | solution.py:406
  70.4 16.5 %collective-permute-start.27 = (bf16[512,128]{1,0:T(8,128)(2,1)S(1)}, bf16[512,128]{1,0:T(8,128)(2,1)S(1)}, u32[]{:S(2)}, u32[]{:S(2)}) collective-permute-start(bf16[512,128]{1,0:T(8,128)(2,1)S(1)} %get-tuple-element.67), channel_id=1, source_target_pairs={{0,4},{1,5},{2,6},{3,7},{4,0},{5,1},{6,2},{7,3},{8,12},{9,13},{10,... | collective-permute-start | bytes 393224 | tf_op jit(solution)/shard_map/ppermute | solution.py:406
  73.9 13.0 %collective-permute-start.28 = (bf16[512,128]{1,0:T(8,128)(2,1)S(1)}, bf16[512,128]{1,0:T(8,128)(2,1)S(1)}, u32[]{:S(2)}, u32[]{:S(2)}) collective-permute-start(bf16[512,128]{1,0:T(8,128)(2,1)S(1)} %get-tuple-element.68), channel_id=1, source_target_pairs={{0,6},{1,7},{2,4},{3,5},{4,2},{5,3},{6,0},{7,1},{8,14},{9,15},{10,... | collective-permute-start | bytes 393224 | tf_op jit(solution)/shard_map/ppermute | solution.py:406
  74.8 12.0 %collective-permute-start.29 = (bf16[512,128]{1,0:T(8,128)(2,1)S(1)}, bf16[512,128]{1,0:T(8,128)(2,1)S(1)}, u32[]{:S(2)}, u32[]{:S(2)}) collective-permute-start(bf16[512,128]{1,0:T(8,128)(2,1)S(1)} %get-tuple-element.69), channel_id=1, source_target_pairs={{0,2},{1,3},{2,0},{3,1},{4,6},{5,7},{6,4},{7,5},{8,10},{9,11},{10,... | collective-permute-start | bytes 393224 | tf_op jit(solution)/shard_map/ppermute | solution.py:406
  79.4 9.1 %collective-permute-start.30 = (bf16[512,128]{1,0:T(8,128)(2,1)S(1)}, bf16[512,128]{1,0:T(8,128)(2,1)S(1)}, u32[]{:S(2)}, u32[]{:S(2)}) collective-permute-start(bf16[512,128]{1,0:T(8,128)(2,1)S(1)} %get-tuple-element.70), channel_id=1, source_target_pairs={{0,12},{1,13},{2,14},{3,15},{4,8},{5,9},{6,10},{7,11},{8,4},{9,5},... | collective-permute-start | bytes 393224 | tf_op jit(solution)/shard_map/ppermute | solution.py:406
  83.2 7.7 %collective-permute-start.31 = (bf16[512,128]{1,0:T(8,128)(2,1)S(1)}, bf16[512,128]{1,0:T(8,128)(2,1)S(1)}, u32[]{:S(2)}, u32[]{:S(2)}) collective-permute-start(bf16[512,128]{1,0:T(8,128)(2,1)S(1)} %get-tuple-element.71), channel_id=1, source_target_pairs={{0,14},{1,15},{2,12},{3,13},{4,10},{5,11},{6,8},{7,9},{8,6},{9,7},... | collective-permute-start | bytes 393224 | tf_op jit(solution)/shard_map/ppermute | solution.py:406

commit v6 on v5

--- a/solution.py
+++ b/solution.py
@@ -305,7 +305,7 @@
     copy_ref = refs[width]
     layers = refs[width + 1 : width + 1 + heads]
     outs = refs[width + 1 + heads : width + 1 + 2 * heads]
-    (pay,) = refs[width + 1 + 2 * heads :]
+    pay, wbuf = refs[width + 1 + 2 * heads :]
     chip, core = chip_core(width)
     odd = lax.rem(chip, 2)
     size = rows * heads * width
@@ -328,17 +328,21 @@
     tile = [picked[:, t * LANES : (t + 1) * LANES] for t in range(9)]
     low = low_lanes(heads * slot)
     order = [tile[0], tile[1], tile[3], tile[4], tile[7], tile[8], jnp.where(low, tile[2], tile[6]), tile[5]]
+    filled = rows + 2
+    wbuf[...] = jnp.zeros_like(wbuf)
     for b in range(heads):
-        pay[b] = jnp.concatenate([part[b * slot : (b + 1) * slot] for part in order], axis=0).astype(BF16)
+        for t, part in enumerate(order):
+            wbuf[b, t * filled : (t + 1) * filled] = part[b * slot : b * slot + filled]
+        pay[b] = wbuf[b].astype(BF16)
     for i, k in enumerate(FAR + NEAR):
         cut = layers[i].shape[0]
         outs[i][0:cut] = layers[i][...]
         outs[i][cut:] = pay[chip ^ k]
 
 
-def unpack(width, heads, rows, slot, tokens, *refs):
+def unpack(width, heads, rows, tokens, *refs):
     pieces = refs[:heads]
-    fw_ref, layer_hbm, new_hbm, momentum_hbm, buf, layer_ref, new_ref, momentum_ref, sems = refs[heads:]
+    fw_ref, layer_hbm, new_hbm, momentum_hbm, buf, wbuf, layer_ref, new_ref, momentum_ref, sems = refs[heads:]
     chip, _ = chip_core(width)
     matrix = fw_ref.shape[1] // 3
     for i, k in enumerate(OUT_ORDER):
@@ -346,6 +350,7 @@
     mid = tokens // 2
     cut = 2 * tokens + mid
     low = low_lanes(mid)
+    slot = rows + 2
     low_r = low_lanes(slot)
 
     def write(lane, block):
@@ -354,20 +359,20 @@
         momentum_ref[:, lane : lane + LANES] = moment
         new_ref[:, lane : lane + LANES] = (fw_ref[:, lane : lane + LANES] - moment) * factor
 
-    moments = [buf[head, cut:].astype(F32) for head in range(heads)]
+    wbuf[...] = buf[:, cut:].astype(F32)
     for head in range(heads):
         whole, half = tiles_of(head)
         for m in range(3):
             for t in range(2):
-                write(m * matrix + whole + t * LANES, moments[head][(2 * m + t) * slot : (2 * m + t + 1) * slot])
+                write(m * matrix + whole + t * LANES, wbuf[head, (2 * m + t) * slot : (2 * m + t + 1) * slot])
     for head in range(0, heads, 2):
         _, half = tiles_of(head)
-        even = moments[head][6 * slot : 7 * slot]
-        odd = moments[head + 1][6 * slot : 7 * slot]
+        even = wbuf[head, 6 * slot : 7 * slot]
+        odd = wbuf[head + 1, 6 * slot : 7 * slot]
         write(half, jnp.where(low_r, even, turned(odd)))
         write(2 * matrix + half, jnp.where(low_r, turned(even), odd))
-        even = moments[head][7 * slot :]
-        odd = moments[head + 1][7 * slot :]
+        even = wbuf[head, 7 * slot : 8 * slot]
+        odd = wbuf[head + 1, 7 * slot : 8 * slot]
         write(matrix + half, jnp.where(low_r, even, turned(odd)))
     writes = copy_all([(new_ref, new_hbm), (momentum_ref, momentum_hbm)], sems)
     for head in range(heads):
@@ -400,7 +405,8 @@
     sem = pltpu.SemaphoreType.DMA
     key_rows = 5 * tokens + 4 * slot
     query_rows = 2 * tokens + tokens // 2
-    out_rows = query_rows + 8 * slot
+    moment_rows = -(-8 * (rows + 2) // 16) * 16
+    out_rows = query_rows + moment_rows
 
     def across(value, step):
         return lax.ppermute(value, "seq", [(i, i ^ step) for i in range(count)])
@@ -538,14 +544,17 @@
         out_shape=packed(out_rows, heads),
         in_specs=[VMEM] * (width + 1 + heads),
         out_specs=[VMEM] * heads,
-        scratch_shapes=[pltpu.VMEM((heads, 8 * slot, LANES), BF16)],
+        scratch_shapes=[
+            pltpu.VMEM((heads, moment_rows, LANES), BF16),
+            pltpu.VMEM((heads, moment_rows, LANES), F32),
+        ],
     )
     pieces = dict(zip(BOTH, pieces))
     pieces = exchange([pieces[k] for k in OUT_ORDER], OUT_ORDER)
 
     return tuple(
         call(
-            functools.partial(unpack, width, heads, rows, slot, tokens),
+            functools.partial(unpack, width, heads, rows, tokens),
             "unpack",
             2,
             *pieces,
@@ -559,6 +568,7 @@
             out_specs=[HBM] * 3,
             scratch_shapes=[
                 pltpu.VMEM((heads, out_rows, LANES), BF16),
+                pltpu.VMEM((heads, moment_rows, LANES), F32),
                 pltpu.VMEM(queries.shape, BF16),
                 pltpu.VMEM(fast_weights.shape, F32),
                 pltpu.VMEM(fast_weights.shape, F32),

time: 93.6 us -> 93 us (level)
  transfers between devices with their start and end apart: 32 -> 32, of which waited for: 11 -> 10; matrix products, arithmetic and copies ran while one was open for 0% -> 0% of each run, Pallas kernels for 13% -> 13%
where the time goes in v6:
time: 93 us; the launch traced here: 92.6 us
  starting transfers between devices  53.7 us (58%)
  waiting for transfers between devices  20.8 us (22%)
  Pallas kernels  16.6 us (18%)
  between operations  1.04 us (1%)
    ppermute x31, starting transfers between devices, across(): return lax.ppermute(value, 'seq', [(i, i ^ step) for i in range(count)])  52.1 us
    ppermute x31, waiting for transfers between devices, across(): return lax.ppermute(value, 'seq', [(i, i ^ step) for i in range(count)])  19.1 us
    pallas_call x9, Pallas kernels, call(): pl.pallas_call(body, compiler_params=params, cost_estimate=cost(micros),...  16.6 us
  transfers between devices with their start and end apart: 32, of which 10 were waited for; matrix products, arithmetic and copies ran while one was open for 0% of the time, Pallas kernels for 13%

profile of v6, /device:TPU:0, one launch (start us, length us, event | category | flops | bytes accessed | tf_op | source)
XLA Modules:
  0.0 92.6 jit_solution(5638924154954843768)
XLA Ops:
  0.7 2.5 %pack_keys.2 = (bf16[736,128]{1,0:T(8,128)(2,1)}, bf16[736,128]{1,0:T(8,128)(2,1)}, bf16[736,128]{1,0:T(8,128)(2,1)}, bf16[736,128]{1,0:T(8,128)(2,1)}) custom-call(bf16[128,2560]{1,0:T(8,128)(2,1)} %k_hbm.3, bf16[128,2560]{1,0:T(8,128)(2,1)} %v_hbm.3, f32[8,128]{1,0:T(8,128)} %bitcast.1, f32[20,7680]{1,0:T(8,128)} %refs_8_.1), custom_call_target="tpu_custom_call" | custom-call | flops 1000000000 | bytes 4000000 | tf_op jit(solution)/shard_map/pack_keys/pallas_call | solution.py:425
  3.2 6.1 %collective-permute-start = (bf16[736,128]{1,0:T(8,128)(2,1)}, bf16[736,128]{1,0:T(8,128)(2,1)S(1)}, u32[]{:S(2)}, u32[]{:S(2)}) collective-permute-start(bf16[736,128]{1,0:T(8,128)(2,1)} %get-tuple-element.38), channel_id=1, source_target_pairs={{0,14},{1,15},{2,12},{3,13},{4,10},{5,11},{6,8},{7,9},{8,6},{9,7},... | collective-permute-start | bytes 565256 | tf_op jit(solution)/shard_map/ppermute | solution.py:412
  9.3 0.6 pack_keys.3
  9.8 0.7 collective-permute-start.2
  10.5 1.7 %collective-permute-start.3 = (bf16[736,128]{1,0:T(8,128)(2,1)S(1)}, bf16[736,128]{1,0:T(8,128)(2,1)S(1)}, u32[]{:S(2)}, u32[]{:S(2)}) collective-permute-start(bf16[736,128]{1,0:T(8,128)(2,1)S(1)} %get-tuple-element.41), channel_id=1, source_target_pairs={{0,6},{1,7},{2,4},{3,5},{4,2},{5,3},{6,0},{7,1},{8,14},{9,15},{10,... | collective-permute-start | bytes 565256 | tf_op jit(solution)/shard_map/ppermute | solution.py:412
  12.2 1.2 %collective-permute-start.4 = (bf16[736,128]{1,0:T(8,128)(2,1)S(1)}, bf16[736,128]{1,0:T(8,128)(2,1)S(1)}, u32[]{:S(2)}, u32[]{:S(2)}) collective-permute-start(bf16[736,128]{1,0:T(8,128)(2,1)S(1)} %get-tuple-element.42), channel_id=1, source_target_pairs={{0,2},{1,3},{2,0},{3,1},{4,6},{5,7},{6,4},{7,5},{8,10},{9,11},{10,... | collective-permute-start | bytes 565256 | tf_op jit(solution)/shard_map/ppermute | solution.py:412
  13.4 1.7 %collective-permute-done.refs_0_ = bf16[736,128]{1,0:T(8,128)(2,1)S(1)} collective-permute-done((bf16[736,128]{1,0:T(8,128)(2,1)}, bf16[736,128]{1,0:T(8,128)(2,1)S(1)}, u32[]{:S(2)}, u32[]{:S(2)}) %collective-permute-start) | collective-permute-done | bytes 188448 | tf_op jit(solution)/shard_map/ppermute | solution.py:412
  15.1 9.2 %collective-permute-start.5 = (bf16[736,128]{1,0:T(8,128)(2,1)S(1)}, bf16[736,128]{1,0:T(8,128)(2,1)S(1)}, u32[]{:S(2)}, u32[]{:S(2)}) collective-permute-start(bf16[736,128]{1,0:T(8,128)(2,1)S(1)} %copy-done.9), channel_id=1, source_target_pairs={{0,8},{1,9},{2,10},{3,11},{4,12},{5,13},{6,14},{7,15},{8,0},{9,1},... | collective-permute-start | bytes 565256 | tf_op jit(solution)/shard_map/ppermute | solution.py:412
  24.3 2.9 %collective-permute-done.1.refs_1_ = bf16[736,128]{1,0:T(8,128)(2,1)S(1)} collective-permute-done((bf16[736,128]{1,0:T(8,128)(2,1)}, bf16[736,128]{1,0:T(8,128)(2,1)S(1)}, u32[]{:S(2)}, u32[]{:S(2)}) %collective-permute-start.1) | collective-permute-done | bytes 188448 | tf_op jit(solution)/shard_map/ppermute | solution.py:412
  27.2 2.1 %collective-permute-start.6 = (bf16[736,128]{1,0:T(8,128)(2,1)S(1)}, bf16[736,128]{1,0:T(8,128)(2,1)S(1)}, u32[]{:S(2)}, u32[]{:S(2)}) collective-permute-start(bf16[736,128]{1,0:T(8,128)(2,1)S(1)} %copy-done.8), channel_id=1, source_target_pairs={{0,12},{1,13},{2,14},{3,15},{4,8},{5,9},{6,10},{7,11},{8,4},{9,5},... | collective-permute-start | bytes 565256 | tf_op jit(solution)/shard_map/ppermute | solution.py:412
  29.4 0.2 pack_queries.1
  29.7 2.9 %collective-permute-start.23 = (bf16[320,128]{1,0:T(8,128)(2,1)S(1)}, bf16[320,128]{1,0:T(8,128)(2,1)S(1)}, u32[]{:S(2)}, u32[]{:S(2)}) collective-permute-start(bf16[320,128]{1,0:T(8,128)(2,1)S(1)} %get-tuple-element.58), channel_id=1, source_target_pairs={{0,6},{1,7},{2,4},{3,5},{4,2},{5,3},{6,0},{7,1},{8,14},{9,15},{10,... | collective-permute-start | bytes 245768 | tf_op jit(solution)/shard_map/ppermute | solution.py:412
  32.6 6.0 %collective-permute-done.5.refs_5_ = bf16[736,128]{1,0:T(8,128)(2,1)S(1)} collective-permute-done((bf16[736,128]{1,0:T(8,128)(2,1)S(1)}, bf16[736,128]{1,0:T(8,128)(2,1)S(1)}, u32[]{:S(2)}, u32[]{:S(2)}) %collective-permute-start.5) | collective-permute-done | bytes 188448 | tf_op jit(solution)/shard_map/ppermute | solution.py:412
  38.6 1.6 %collective-permute-start.15 = (bf16[768,128]{1,0:T(8,128)(2,1)S(1)}, bf16[768,128]{1,0:T(8,128)(2,1)S(1)}, u32[]{:S(2)}, u32[]{:S(2)}) collective-permute-start(bf16[768,128]{1,0:T(8,128)(2,1)S(1)} %pack_weights.1), channel_id=1, source_target_pairs={{0,16},{16,0},{1,17},{17,1},{2,18},{18,2},{3,19},{19,3},{4,20},{20... | collective-permute-start | bytes 589832 | tf_op jit(solution)/shard_map/ppermute | solution.py:468
  40.2 0.5 collective-permute-start.10
  40.7 0.5 collective-permute-start.12
  41.3 0.1 reshape.13
  41.3 0.1 dynamic-slice
  41.4 0.1 dynamic-slice.2
  41.5 0.1 collective-permute-done.14.refs_15_
  41.6 0.1 collective-permute-start.13
  41.7 0.1 collective-permute-done.10.refs_11_
  41.9 0.2 collective-permute-start.7
  42.1 0.2 collective-permute-start.8
  42.4 0.2 collective-permute-start.9
  42.6 1.7 %collective-permute-done.15.refs_16_ = bf16[768,128]{1,0:T(8,128)(2,1)S(1)} collective-permute-done((bf16[768,128]{1,0:T(8,128)(2,1)S(1)}, bf16[768,128]{1,0:T(8,128)(2,1)S(1)}, u32[]{:S(2)}, u32[]{:S(2)}) %collective-permute-start.15) | collective-permute-done | bytes 196640 | tf_op jit(solution)/shard_map/ppermute | solution.py:468
  44.4 0.7 collective-permute-start.24
  45.1 4.6 %collective-permute-start.18 = (bf16[320,128]{1,0:T(8,128)(2,1)S(1)}, bf16[320,128]{1,0:T(8,128)(2,1)S(1)}, u32[]{:S(2)}, u32[]{:S(2)}) collective-permute-start(bf16[320,128]{1,0:T(8,128)(2,1)S(1)} %get-tuple-element.49), channel_id=1, source_target_pairs={{0,8},{1,9},{2,10},{3,11},{4,12},{5,13},{6,14},{7,15},{8,0},{9,1},... | collective-permute-start | bytes 245768 | tf_op jit(solution)/shard_map/ppermute | solution.py:412
  49.7 1.0 %collective-permute-start.19 = (bf16[320,128]{1,0:T(8,128)(2,1)S(1)}, bf16[320,128]{1,0:T(8,128)(2,1)S(1)}, u32[]{:S(2)}, u32[]{:S(2)}) collective-permute-start(bf16[320,128]{1,0:T(8,128)(2,1)S(1)} %get-tuple-element.50), channel_id=1, source_target_pairs={{0,10},{1,11},{2,8},{3,9},{4,14},{5,15},{6,12},{7,13},{8,2},{9,3},... | collective-permute-start | bytes 245768 | tf_op jit(solution)/shard_map/ppermute | solution.py:412
  50.7 1.6 %collective-permute-start.20 = (bf16[320,128]{1,0:T(8,128)(2,1)S(1)}, bf16[320,128]{1,0:T(8,128)(2,1)S(1)}, u32[]{:S(2)}, u32[]{:S(2)}) collective-permute-start(bf16[320,128]{1,0:T(8,128)(2,1)S(1)} %get-tuple-element.51), channel_id=1, source_target_pairs={{0,12},{1,13},{2,14},{3,15},{4,8},{5,9},{6,10},{7,11},{8,4},{9,5},... | collective-permute-start | bytes 245768 | tf_op jit(solution)/shard_map/ppermute | solution.py:412
  52.4 2.2 %collective-permute-start.21 = (bf16[320,128]{1,0:T(8,128)(2,1)S(1)}, bf16[320,128]{1,0:T(8,128)(2,1)S(1)}, u32[]{:S(2)}, u32[]{:S(2)}) collective-permute-start(bf16[320,128]{1,0:T(8,128)(2,1)S(1)} %get-tuple-element.52), channel_id=1, source_target_pairs={{0,14},{1,15},{2,12},{3,13},{4,10},{5,11},{6,8},{7,9},{8,6},{9,7},... | collective-permute-start | bytes 245768 | tf_op jit(solution)/shard_map/ppermute | solution.py:412
  54.6 0.1 broadcast_select_fusion
  54.7 4.2 %key_side.1 = (f32[320,1152]{1,0:T(8,128)S(1)}, bf16[384,1152]{1,0:T(8,128)(2,1)S(1)}, bf16[16,640,128]{2,1,0:T(8,128)(2,1)S(1)}) custom-call(bf16[736,128]{1,0:T(8,128)(2,1)S(1)} %collective-permute-done.refs_0_, bf16[736,128]{1,0:T(8,128)(2,1)S(1)} %collective-permute-done.1.refs_1_, bf16[736,128]{1,0:T(8,128)(2,1)S(1)} %collective-permute-done.2.refs_2_, ...), custom_call_target="tpu_custom_call" | custom-call | tf_op jit(solution)/shard_map/key_side/pallas_call | solution.py:425
  58.9 2.9 %query_side.3 = (bf16[320,128]{1,0:T(8,128)(2,1)S(1)}, bf16[320,128]{1,0:T(8,128)(2,1)S(1)}, bf16[320,128]{1,0:T(8,128)(2,1)S(1)}, bf16[320,128]{1,0:T(8,128)(2,1)S(1)}) custom-call(bf16[16,640,128]{2,1,0:T(8,128)(2,1)S(1)} %get-tuple-element.48.refs_0_, bf16[384,1152]{1,0:T(8,128)(2,1)S(1)} %get-tuple-element.47.refs_1_.refs_2_, ...), custom_call_target="tpu_custom_call" | custom-call | tf_op jit(solution)/shard_map/query_side/pallas_call | solution.py:425
  61.9 0.6 collective-permute-done.19.refs_5_
  62.5 3.9 %query_side.2 = (bf16[320,128]{1,0:T(8,128)(2,1)S(1)}, bf16[320,128]{1,0:T(8,128)(2,1)S(1)}, bf16[320,128]{1,0:T(8,128)(2,1)S(1)}, bf16[320,128]{1,0:T(8,128)(2,1)S(1)}) custom-call(bf16[16,640,128]{2,1,0:T(8,128)(2,1)S(1)} %get-tuple-element.48.refs_0_, bf16[384,1152]{1,0:T(8,128)(2,1)S(1)} %get-tuple-element.47.refs_1_.refs_2_, ...), custom_call_target="tpu_custom_call" | custom-call | flops 20000000000 | bytes 80000000 | tf_op jit(solution)/shard_map/query_side/pallas_call | solution.py:425
  66.4 0.7 pack_momentum.1
  67.1 3.1 %collective-permute-start.25 = (bf16[496,128]{1,0:T(8,128)(2,1)S(1)}, bf16[496,128]{1,0:T(8,128)(2,1)S(1)}, u32[]{:S(2)}, u32[]{:S(2)}) collective-permute-start(bf16[496,128]{1,0:T(8,128)(2,1)S(1)} %get-tuple-element.65), channel_id=1, source_target_pairs={{0,8},{1,9},{2,10},{3,11},{4,12},{5,13},{6,14},{7,15},{8,0},{9,1},... | collective-permute-start | bytes 380936 | tf_op jit(solution)/shard_map/ppermute | solution.py:412
  70.3 0.2 collective-permute-start.26
  70.4 3.5 %collective-permute-start.27 = (bf16[496,128]{1,0:T(8,128)(2,1)S(1)}, bf16[496,128]{1,0:T(8,128)(2,1)S(1)}, u32[]{:S(2)}, u32[]{:S(2)}) collective-permute-start(bf16[496,128]{1,0:T(8,128)(2,1)S(1)} %get-tuple-element.67), channel_id=1, source_target_pairs={{0,4},{1,5},{2,6},{3,7},{4,0},{5,1},{6,2},{7,3},{8,12},{9,13},{10,... | collective-permute-start | bytes 380936 | tf_op jit(solution)/shard_map/ppermute | solution.py:412
  73.9 0.9 %collective-permute-start.28 = (bf16[496,128]{1,0:T(8,128)(2,1)S(1)}, bf16[496,128]{1,0:T(8,128)(2,1)S(1)}, u32[]{:S(2)}, u32[]{:S(2)}) collective-permute-start(bf16[496,128]{1,0:T(8,128)(2,1)S(1)} %get-tuple-element.68), channel_id=1, source_target_pairs={{0,6},{1,7},{2,4},{3,5},{4,2},{5,3},{6,0},{7,1},{8,14},{9,15},{10,... | collective-permute-start | bytes 380936 | tf_op jit(solution)/shard_map/ppermute | solution.py:412
  74.9 0.6 collective-permute-start.29
  75.4 3.5 %collective-permute-done.25.refs_0_ = bf16[496,128]{1,0:T(8,128)(2,1)S(1)} collective-permute-done((bf16[496,128]{1,0:T(8,128)(2,1)S(1)}, bf16[496,128]{1,0:T(8,128)(2,1)S(1)}, u32[]{:S(2)}, u32[]{:S(2)}) %collective-permute-start.25) | collective-permute-done | bytes 127008 | tf_op jit(solution)/shard_map/ppermute | solution.py:412
  78.9 4.1 %collective-permute-start.30 = (bf16[496,128]{1,0:T(8,128)(2,1)S(1)}, bf16[496,128]{1,0:T(8,128)(2,1)S(1)}, u32[]{:S(2)}, u32[]{:S(2)}) collective-permute-start(bf16[496,128]{1,0:T(8,128)(2,1)S(1)} %get-tuple-element.70), channel_id=1, source_target_pairs={{0,12},{1,13},{2,14},{3,15},{4,8},{5,9},{6,10},{7,11},{8,4},{9,5},... | collective-permute-start | bytes 380936 | tf_op jit(solution)/shard_map/ppermute | solution.py:412
  83.0 3.6 %collective-permute-start.31 = (bf16[496,128]{1,0:T(8,128)(2,1)S(1)}, bf16[496,128]{1,0:T(8,128)(2,1)S(1)}, u32[]{:S(2)}, u32[]{:S(2)}) collective-permute-start(bf16[496,128]{1,0:T(8,128)(2,1)S(1)} %get-tuple-element.71), channel_id=1, source_target_pairs={{0,14},{1,15},{2,12},{3,13},{4,10},{5,11},{6,8},{7,9},{8,6},{9,7},... | collective-permute-start | bytes 380936 | tf_op jit(solution)/shard_map/ppermute | solution.py:412
  86.6 1.4 %collective-permute-done.30.refs_5_ = bf16[496,128]{1,0:T(8,128)(2,1)S(1)} collective-permute-done((bf16[496,128]{1,0:T(8,128)(2,1)S(1)}, bf16[496,128]{1,0:T(8,128)(2,1)S(1)}, u32[]{:S(2)}, u32[]{:S(2)}) %collective-permute-start.30) | collective-permute-done | bytes 127008 | tf_op jit(solution)/shard_map/ppermute | solution.py:412
  87.9 2.8 %collective-permute-done.31.refs_6_ = bf16[496,128]{1,0:T(8,128)(2,1)S(1)} collective-permute-done((bf16[496,128]{1,0:T(8,128)(2,1)S(1)}, bf16[496,128]{1,0:T(8,128)(2,1)S(1)}, u32[]{:S(2)}, u32[]{:S(2)}) %collective-permute-start.31) | collective-permute-done | bytes 127008 | tf_op jit(solution)/shard_map/ppermute | solution.py:412
  90.7 1.7 %unpack.1 = (bf16[128,2560]{1,0:T(8,128)(2,1)}, f32[20,7680]{1,0:T(8,128)}, f32[20,7680]{1,0:T(8,128)}) custom-call(bf16[496,128]{1,0:T(8,128)(2,1)S(1)} %collective-permute-done.25.refs_0_, bf16[496,128]{1,0:T(8,128)(2,1)S(1)} %collective-permute-done.26.refs_1_, bf16[496,128]{1,0:T(8,128)(2,1)S(1)} %collective-permute-done.27.refs_2_, ...), custom_call_target="tpu_custom_call" | custom-call | flops 1000000000 | bytes 4000000 | tf_op jit(solution)/shard_map/unpack/pallas_call | solution.py:425
  (54 shorter events, 0.4 us)
Async XLA Ops:
  0.6 8.6 %copy-start = (f32[20,7680]{1,0:T(8,128)S(1)}, f32[20,7680]{1,0:T(8,128)}, u32[]{:S(2)}) copy-start(f32[20,7680]{1,0:T(8,128)} %refs_8_.1) | copy-start | bytes 1843204
  0.6 8.6 %copy-start.2 = (bf16[128,2560]{1,0:T(8,128)(2,1)S(1)}, bf16[128,2560]{1,0:T(8,128)(2,1)}, u32[]{:S(2)}) copy-start(bf16[128,2560]{1,0:T(8,128)(2,1)} %k_hbm.3) | copy-start | bytes 1966084
  0.7 8.6 %copy-start.3 = (bf16[128,2560]{1,0:T(8,128)(2,1)S(1)}, bf16[128,2560]{1,0:T(8,128)(2,1)}, u32[]{:S(2)}) copy-start(bf16[128,2560]{1,0:T(8,128)(2,1)} %v_hbm.3) | copy-start | bytes 1966084
  0.7 8.6 %copy-start.5 = (f32[128,8]{0,1:T(8,128)S(1)}, f32[128,8]{0,1:T(8,128)}, u32[]{:S(2)}) copy-start(f32[128,8]{0,1:T(8,128)} %param.10) | copy-start | bytes 12292
  3.2 11.9 %collective-permute-start = (bf16[736,128]{1,0:T(8,128)(2,1)}, bf16[736,128]{1,0:T(8,128)(2,1)S(1)}, u32[]{:S(2)}, u32[]{:S(2)}) collective-permute-start(bf16[736,128]{1,0:T(8,128)(2,1)} %get-tuple-element.38), channel_id=1, source_target_pairs={{0,14},{1,15},{2,12},{3,13},{4,10},{5,11},{6,8},{7,9},{8,6},{9,7},... | collective-permute-start | bytes 565256 | tf_op jit(solution)/shard_map/ppermute | solution.py:412
  9.2 5.9 %copy-start.9 = (bf16[736,128]{1,0:T(8,128)(2,1)S(1)}, bf16[736,128]{1,0:T(8,128)(2,1)}, u32[]{:S(2)}) copy-start(bf16[736,128]{1,0:T(8,128)(2,1)} %get-tuple-element.43) | copy-start | bytes 565252
  9.2 18.0 %copy-start.8 = (bf16[736,128]{1,0:T(8,128)(2,1)S(1)}, bf16[736,128]{1,0:T(8,128)(2,1)}, u32[]{:S(2)}) copy-start(bf16[736,128]{1,0:T(8,128)(2,1)} %get-tuple-element.44) | copy-start | bytes 565252
  9.2 20.2 %copy-start.4 = (bf16[128,2560]{1,0:T(8,128)(2,1)S(1)}, bf16[128,2560]{1,0:T(8,128)(2,1)}, u32[]{:S(2)}) copy-start(bf16[128,2560]{1,0:T(8,128)(2,1)} %q_ref.1) | copy-start | bytes 1966084
  9.2 18.0 %collective-permute-start.1 = (bf16[736,128]{1,0:T(8,128)(2,1)}, bf16[736,128]{1,0:T(8,128)(2,1)S(1)}, u32[]{:S(2)}, u32[]{:S(2)}) collective-permute-start(bf16[736,128]{1,0:T(8,128)(2,1)} %get-tuple-element.39), channel_id=1, source_target_pairs={{0,10},{1,11},{2,8},{3,9},{4,14},{5,15},{6,12},{7,13},{8,2},{9,3},... | collective-permute-start | bytes 565256 | tf_op jit(solution)/shard_map/ppermute | solution.py:412
  9.8 19.7 %collective-permute-start.2 = (bf16[736,128]{1,0:T(8,128)(2,1)S(1)}, bf16[736,128]{1,0:T(8,128)(2,1)S(1)}, u32[]{:S(2)}, u32[]{:S(2)}) collective-permute-start(bf16[736,128]{1,0:T(8,128)(2,1)S(1)} %get-tuple-element.40), channel_id=1, source_target_pairs={{0,4},{1,5},{2,6},{3,7},{4,0},{5,1},{6,2},{7,3},{8,12},{9,13},{10,... | collective-permute-start | bytes 565256 | tf_op jit(solution)/shard_map/ppermute | solution.py:412
  10.5 19.1 %collective-permute-start.3 = (bf16[736,128]{1,0:T(8,128)(2,1)S(1)}, bf16[736,128]{1,0:T(8,128)(2,1)S(1)}, u32[]{:S(2)}, u32[]{:S(2)}) collective-permute-start(bf16[736,128]{1,0:T(8,128)(2,1)S(1)} %get-tuple-element.41), channel_id=1, source_target_pairs={{0,6},{1,7},{2,4},{3,5},{4,2},{5,3},{6,0},{7,1},{8,14},{9,15},{10,... | collective-permute-start | bytes 565256 | tf_op jit(solution)/shard_map/ppermute | solution.py:412
  12.2 20.3 %collective-permute-start.4 = (bf16[736,128]{1,0:T(8,128)(2,1)S(1)}, bf16[736,128]{1,0:T(8,128)(2,1)S(1)}, u32[]{:S(2)}, u32[]{:S(2)}) collective-permute-start(bf16[736,128]{1,0:T(8,128)(2,1)S(1)} %get-tuple-element.42), channel_id=1, source_target_pairs={{0,2},{1,3},{2,0},{3,1},{4,6},{5,7},{6,4},{7,5},{8,10},{9,11},{10,... | collective-permute-start | bytes 565256 | tf_op jit(solution)/shard_map/ppermute | solution.py:412
  15.1 23.5 %collective-permute-start.5 = (bf16[736,128]{1,0:T(8,128)(2,1)S(1)}, bf16[736,128]{1,0:T(8,128)(2,1)S(1)}, u32[]{:S(2)}, u32[]{:S(2)}) collective-permute-start(bf16[736,128]{1,0:T(8,128)(2,1)S(1)} %copy-done.9), channel_id=1, source_target_pairs={{0,8},{1,9},{2,10},{3,11},{4,12},{5,13},{6,14},{7,15},{8,0},{9,1},... | collective-permute-start | bytes 565256 | tf_op jit(solution)/shard_map/ppermute | solution.py:412
  27.2 14.0 %copy-start.6 = (f32[2560]{0:T(1024)S(1)}, f32[2560]{0:T(1024)}, u32[]{:S(2)}) copy-start(f32[2560]{0:T(1024)} %param.12) | copy-start | bytes 30724
  27.2 14.0 %copy-start.7 = (f32[2560]{0:T(1024)S(1)}, f32[2560]{0:T(1024)}, u32[]{:S(2)}) copy-start(f32[2560]{0:T(1024)} %param.13) | copy-start | bytes 30724
  27.2 11.3 %collective-permute-start.6 = (bf16[736,128]{1,0:T(8,128)(2,1)S(1)}, bf16[736,128]{1,0:T(8,128)(2,1)S(1)}, u32[]{:S(2)}, u32[]{:S(2)}) collective-permute-start(bf16[736,128]{1,0:T(8,128)(2,1)S(1)} %copy-done.8), channel_id=1, source_target_pairs={{0,12},{1,13},{2,14},{3,15},{4,8},{5,9},{6,10},{7,11},{8,4},{9,5},... | collective-permute-start | bytes 565256 | tf_op jit(solution)/shard_map/ppermute | solution.py:412
  29.6 11.1 %collective-permute-start.22 = (bf16[320,128]{1,0:T(8,128)(2,1)S(1)}, bf16[320,128]{1,0:T(8,128)(2,1)S(1)}, u32[]{:S(2)}, u32[]{:S(2)}) collective-permute-start(bf16[320,128]{1,0:T(8,128)(2,1)S(1)} %get-tuple-element.57), channel_id=1, source_target_pairs={{0,4},{1,5},{2,6},{3,7},{4,0},{5,1},{6,2},{7,3},{8,12},{9,13},{10,... | collective-permute-start | bytes 245768 | tf_op jit(solution)/shard_map/ppermute | solution.py:412
  29.7 11.0 %collective-permute-start.23 = (bf16[320,128]{1,0:T(8,128)(2,1)S(1)}, bf16[320,128]{1,0:T(8,128)(2,1)S(1)}, u32[]{:S(2)}, u32[]{:S(2)}) collective-permute-start(bf16[320,128]{1,0:T(8,128)(2,1)S(1)} %get-tuple-element.58), channel_id=1, source_target_pairs={{0,6},{1,7},{2,4},{3,5},{4,2},{5,3},{6,0},{7,1},{8,14},{9,15},{10,... | collective-permute-start | bytes 245768 | tf_op jit(solution)/shard_map/ppermute | solution.py:412
  38.6 5.7 %collective-permute-start.15 = (bf16[768,128]{1,0:T(8,128)(2,1)S(1)}, bf16[768,128]{1,0:T(8,128)(2,1)S(1)}, u32[]{:S(2)}, u32[]{:S(2)}) collective-permute-start(bf16[768,128]{1,0:T(8,128)(2,1)S(1)} %pack_weights.1), channel_id=1, source_target_pairs={{0,16},{16,0},{1,17},{17,1},{2,18},{18,2},{3,19},{19,3},{4,20},{20... | collective-permute-start | bytes 589832 | tf_op jit(solution)/shard_map/ppermute | solution.py:468
  40.2 1.4 %collective-permute-start.14 = (bf16[736,128]{1,0:T(8,128)(2,1)S(1)}, bf16[736,128]{1,0:T(8,128)(2,1)S(1)}, u32[]{:S(2)}, u32[]{:S(2)}) collective-permute-start(bf16[736,128]{1,0:T(8,128)(2,1)S(1)} %get-tuple-element.45.refs_7_), channel_id=1, source_target_pairs={{0,1},{1,0},{2,3},{3,2},{4,5},{5,4},{6,7},{7,6},{8,9},{9,8},{10,11... | collective-permute-start | bytes 565256 | tf_op jit(solution)/shard_map/ppermute | solution.py:412
  40.2 1.7 %collective-permute-start.10 = (bf16[736,128]{1,0:T(8,128)(2,1)S(1)}, bf16[736,128]{1,0:T(8,128)(2,1)S(1)}, u32[]{:S(2)}, u32[]{:S(2)}) collective-permute-start(bf16[736,128]{1,0:T(8,128)(2,1)S(1)} %collective-permute-done.3.refs_3_), channel_id=1, source_target_pairs={{0,1},{1,0},{2,3},{3,2},{4,5},{5,4},{6,7},{7,6},{8,9},{9,8},{10,11... | collective-permute-start | bytes 565256 | tf_op jit(solution)/shard_map/ppermute | solution.py:412
  40.7 1.5 %collective-permute-start.11 = (bf16[736,128]{1,0:T(8,128)(2,1)S(1)}, bf16[736,128]{1,0:T(8,128)(2,1)S(1)}, u32[]{:S(2)}, u32[]{:S(2)}) collective-permute-start(bf16[736,128]{1,0:T(8,128)(2,1)S(1)} %collective-permute-done.4.refs_4_), channel_id=1, source_target_pairs={{0,1},{1,0},{2,3},{3,2},{4,5},{5,4},{6,7},{7,6},{8,9},{9,8},{10,11... | collective-permute-start | bytes 565256 | tf_op jit(solution)/shard_map/ppermute | solution.py:412
  40.7 1.7 %collective-permute-start.12 = (bf16[736,128]{1,0:T(8,128)(2,1)S(1)}, bf16[736,128]{1,0:T(8,128)(2,1)S(1)}, u32[]{:S(2)}, u32[]{:S(2)}) collective-permute-start(bf16[736,128]{1,0:T(8,128)(2,1)S(1)} %collective-permute-done.5.refs_5_), channel_id=1, source_target_pairs={{0,1},{1,0},{2,3},{3,2},{4,5},{5,4},{6,7},{7,6},{8,9},{9,8},{10,11... | collective-permute-start | bytes 565256 | tf_op jit(solution)/shard_map/ppermute | solution.py:412
  41.6 2.8 %collective-permute-start.13 = (bf16[736,128]{1,0:T(8,128)(2,1)S(1)}, bf16[736,128]{1,0:T(8,128)(2,1)S(1)}, u32[]{:S(2)}, u32[]{:S(2)}) collective-permute-start(bf16[736,128]{1,0:T(8,128)(2,1)S(1)} %collective-permute-done.6.refs_6_), channel_id=1, source_target_pairs={{0,1},{1,0},{2,3},{3,2},{4,5},{5,4},{6,7},{7,6},{8,9},{9,8},{10,11... | collective-permute-start | bytes 565256 | tf_op jit(solution)/shard_map/ppermute | solution.py:412
  41.9 3.2 %collective-permute-start.7 = (bf16[736,128]{1,0:T(8,128)(2,1)S(1)}, bf16[736,128]{1,0:T(8,128)(2,1)S(1)}, u32[]{:S(2)}, u32[]{:S(2)}) collective-permute-start(bf16[736,128]{1,0:T(8,128)(2,1)S(1)} %collective-permute-done.refs_0_), channel_id=1, source_target_pairs={{0,1},{1,0},{2,3},{3,2},{4,5},{5,4},{6,7},{7,6},{8,9},{9,8},{10,11... | collective-permute-start | bytes 565256 | tf_op jit(solution)/shard_map/ppermute | solution.py:412
  42.1 7.6 %collective-permute-start.8 = (bf16[736,128]{1,0:T(8,128)(2,1)S(1)}, bf16[736,128]{1,0:T(8,128)(2,1)S(1)}, u32[]{:S(2)}, u32[]{:S(2)}) collective-permute-start(bf16[736,128]{1,0:T(8,128)(2,1)S(1)} %collective-permute-done.1.refs_1_), channel_id=1, source_target_pairs={{0,1},{1,0},{2,3},{3,2},{4,5},{5,4},{6,7},{7,6},{8,9},{9,8},{10,11... | collective-permute-start | bytes 565256 | tf_op jit(solution)/shard_map/ppermute | solution.py:412
  42.4 8.4 %collective-permute-start.9 = (bf16[736,128]{1,0:T(8,128)(2,1)S(1)}, bf16[736,128]{1,0:T(8,128)(2,1)S(1)}, u32[]{:S(2)}, u32[]{:S(2)}) collective-permute-start(bf16[736,128]{1,0:T(8,128)(2,1)S(1)} %collective-permute-done.2.refs_2_), channel_id=1, source_target_pairs={{0,1},{1,0},{2,3},{3,2},{4,5},{5,4},{6,7},{7,6},{8,9},{9,8},{10,11... | collective-permute-start | bytes 565256 | tf_op jit(solution)/shard_map/ppermute | solution.py:412
  44.3 8.1 %collective-permute-start.16 = (bf16[768,128]{1,0:T(8,128)(2,1)S(1)}, bf16[768,128]{1,0:T(8,128)(2,1)S(1)}, u32[]{:S(2)}, u32[]{:S(2)}) collective-permute-start(bf16[768,128]{1,0:T(8,128)(2,1)S(1)} %collective-permute-done.15.refs_16_), channel_id=1, source_target_pairs={{0,1},{1,0},{2,3},{3,2},{4,5},{5,4},{6,7},{7,6},{8,9},{9,8},{10,11... | collective-permute-start | bytes 589832 | tf_op jit(solution)/shard_map/ppermute | solution.py:412
  44.4 14.4 %collective-permute-start.24 = (bf16[320,128]{1,0:T(8,128)(2,1)S(1)}, bf16[320,128]{1,0:T(8,128)(2,1)S(1)}, u32[]{:S(2)}, u32[]{:S(2)}) collective-permute-start(bf16[320,128]{1,0:T(8,128)(2,1)S(1)} %get-tuple-element.59), channel_id=1, source_target_pairs={{0,2},{1,3},{2,0},{3,1},{4,6},{5,7},{6,4},{7,5},{8,10},{9,11},{10,... | collective-permute-start | bytes 245768 | tf_op jit(solution)/shard_map/ppermute | solution.py:412
  45.1 16.8 %collective-permute-start.18 = (bf16[320,128]{1,0:T(8,128)(2,1)S(1)}, bf16[320,128]{1,0:T(8,128)(2,1)S(1)}, u32[]{:S(2)}, u32[]{:S(2)}) collective-permute-start(bf16[320,128]{1,0:T(8,128)(2,1)S(1)} %get-tuple-element.49), channel_id=1, source_target_pairs={{0,8},{1,9},{2,10},{3,11},{4,12},{5,13},{6,14},{7,15},{8,0},{9,1},... | collective-permute-start | bytes 245768 | tf_op jit(solution)/shard_map/ppermute | solution.py:412
  49.7 12.8 %collective-permute-start.19 = (bf16[320,128]{1,0:T(8,128)(2,1)S(1)}, bf16[320,128]{1,0:T(8,128)(2,1)S(1)}, u32[]{:S(2)}, u32[]{:S(2)}) collective-permute-start(bf16[320,128]{1,0:T(8,128)(2,1)S(1)} %get-tuple-element.50), channel_id=1, source_target_pairs={{0,10},{1,11},{2,8},{3,9},{4,14},{5,15},{6,12},{7,13},{8,2},{9,3},... | collective-permute-start | bytes 245768 | tf_op jit(solution)/shard_map/ppermute | solution.py:412
  50.7 11.8 %collective-permute-start.20 = (bf16[320,128]{1,0:T(8,128)(2,1)S(1)}, bf16[320,128]{1,0:T(8,128)(2,1)S(1)}, u32[]{:S(2)}, u32[]{:S(2)}) collective-permute-start(bf16[320,128]{1,0:T(8,128)(2,1)S(1)} %get-tuple-element.51), channel_id=1, source_target_pairs={{0,12},{1,13},{2,14},{3,15},{4,8},{5,9},{6,10},{7,11},{8,4},{9,5},... | collective-permute-start | bytes 245768 | tf_op jit(solution)/shard_map/ppermute | solution.py:412
  52.4 10.1 %collective-permute-start.21 = (bf16[320,128]{1,0:T(8,128)(2,1)S(1)}, bf16[320,128]{1,0:T(8,128)(2,1)S(1)}, u32[]{:S(2)}, u32[]{:S(2)}) collective-permute-start(bf16[320,128]{1,0:T(8,128)(2,1)S(1)} %get-tuple-element.52), channel_id=1, source_target_pairs={{0,14},{1,15},{2,12},{3,13},{4,10},{5,11},{6,8},{7,9},{8,6},{9,7},... | collective-permute-start | bytes 245768 | tf_op jit(solution)/shard_map/ppermute | solution.py:412
  58.8 7.5 %collective-permute-start.17 = (f32[320,1152]{1,0:T(8,128)S(1)}, f32[320,1152]{1,0:T(8,128)S(1)}, u32[]{:S(2)}, u32[]{:S(2)}) collective-permute-start(f32[320,1152]{1,0:T(8,128)S(1)} %get-tuple-element.46.refs_0_), channel_id=1, source_target_pairs={{0,1},{1,0},{2,3},{3,2},{4,5},{5,4},{6,7},{7,6},{8,9},{9,8},{10,11... | collective-permute-start | bytes 4423688 | tf_op jit(solution)/shard_map/ppermute | solution.py:412
  66.4 24.3 %copy-start.1 = (f32[20,7680]{1,0:T(8,128)S(1)}, f32[20,7680]{1,0:T(8,128)}, u32[]{:S(2)}) copy-start(f32[20,7680]{1,0:T(8,128)} %refs_8_.1) | copy-start | bytes 1843204
  67.1 11.8 %collective-permute-start.25 = (bf16[496,128]{1,0:T(8,128)(2,1)S(1)}, bf16[496,128]{1,0:T(8,128)(2,1)S(1)}, u32[]{:S(2)}, u32[]{:S(2)}) collective-permute-start(bf16[496,128]{1,0:T(8,128)(2,1)S(1)} %get-tuple-element.65), channel_id=1, source_target_pairs={{0,8},{1,9},{2,10},{3,11},{4,12},{5,13},{6,14},{7,15},{8,0},{9,1},... | collective-permute-start | bytes 380936 | tf_op jit(solution)/shard_map/ppermute | solution.py:412
  70.3 12.7 %collective-permute-start.26 = (bf16[496,128]{1,0:T(8,128)(2,1)S(1)}, bf16[496,128]{1,0:T(8,128)(2,1)S(1)}, u32[]{:S(2)}, u32[]{:S(2)}) collective-permute-start(bf16[496,128]{1,0:T(8,128)(2,1)S(1)} %get-tuple-element.66), channel_id=1, source_target_pairs={{0,10},{1,11},{2,8},{3,9},{4,14},{5,15},{6,12},{7,13},{8,2},{9,3},... | collective-permute-start | bytes 380936 | tf_op jit(solution)/shard_map/ppermute | solution.py:412
  70.4 16.1 %collective-permute-start.27 = (bf16[496,128]{1,0:T(8,128)(2,1)S(1)}, bf16[496,128]{1,0:T(8,128)(2,1)S(1)}, u32[]{:S(2)}, u32[]{:S(2)}) collective-permute-start(bf16[496,128]{1,0:T(8,128)(2,1)S(1)} %get-tuple-element.67), channel_id=1, source_target_pairs={{0,4},{1,5},{2,6},{3,7},{4,0},{5,1},{6,2},{7,3},{8,12},{9,13},{10,... | collective-permute-start | bytes 380936 | tf_op jit(solution)/shard_map/ppermute | solution.py:412
  73.9 12.7 %collective-permute-start.28 = (bf16[496,128]{1,0:T(8,128)(2,1)S(1)}, bf16[496,128]{1,0:T(8,128)(2,1)S(1)}, u32[]{:S(2)}, u32[]{:S(2)}) collective-permute-start(bf16[496,128]{1,0:T(8,128)(2,1)S(1)} %get-tuple-element.68), channel_id=1, source_target_pairs={{0,6},{1,7},{2,4},{3,5},{4,2},{5,3},{6,0},{7,1},{8,14},{9,15},{10,... | collective-permute-start | bytes 380936 | tf_op jit(solution)/shard_map/ppermute | solution.py:412
  74.9 11.7 %collective-permute-start.29 = (bf16[496,128]{1,0:T(8,128)(2,1)S(1)}, bf16[496,128]{1,0:T(8,128)(2,1)S(1)}, u32[]{:S(2)}, u32[]{:S(2)}) collective-permute-start(bf16[496,128]{1,0:T(8,128)(2,1)S(1)} %get-tuple-element.69), channel_id=1, source_target_pairs={{0,2},{1,3},{2,0},{3,1},{4,6},{5,7},{6,4},{7,5},{8,10},{9,11},{10,... | collective-permute-start | bytes 380936 | tf_op jit(solution)/shard_map/ppermute | solution.py:412
  78.9 9.1 %collective-permute-start.30 = (bf16[496,128]{1,0:T(8,128)(2,1)S(1)}, bf16[496,128]{1,0:T(8,128)(2,1)S(1)}, u32[]{:S(2)}, u32[]{:S(2)}) collective-permute-start(bf16[496,128]{1,0:T(8,128)(2,1)S(1)} %get-tuple-element.70), channel_id=1, source_target_pairs={{0,12},{1,13},{2,14},{3,15},{4,8},{5,9},{6,10},{7,11},{8,4},{9,5},... | collective-permute-start | bytes 380936 | tf_op jit(solution)/shard_map/ppermute | solution.py:412
  83.0 7.7 %collective-permute-start.31 = (bf16[496,128]{1,0:T(8,128)(2,1)S(1)}, bf16[496,128]{1,0:T(8,128)(2,1)S(1)}, u32[]{:S(2)}, u32[]{:S(2)}) collective-permute-start(bf16[496,128]{1,0:T(8,128)(2,1)S(1)} %get-tuple-element.71), channel_id=1, source_target_pairs={{0,14},{1,15},{2,12},{3,13},{4,10},{5,11},{6,8},{7,9},{8,6},{9,7},... | collective-permute-start | bytes 380936 | tf_op jit(solution)/shard_map/ppermute | solution.py:412
